TPU v7x, 32 devices: a whole 2x2x4 slice. The times are simulated.
32 devices in a mesh: dom: 8 (over z, x), head: 4 (over y, core).
Axes of the slice: x: 2, y: 2, z: 4, core: 2. Of those that a mesh axis runs over, the one named last changes fastest.
Arguments:
- vertex_embeddings: bfloat16 [4096, 512], P(('dom', 'head')), may hold values from -6 to 6
- adjacent_group_bank_ids: int32 [8, 4, 12], P('dom', 'head'), may hold values from -1 to 15, as said below
- coupling_strength_panels: bfloat16 [16, 128, 128], replicated, may hold values from -0.3125 to 0.3125
- asking_projector: bfloat16 [512, 512], replicated, may hold values from -0.25 to 0.25
- lookup_projector: bfloat16 [512, 512], replicated, may hold values from -0.25 to 0.25
- content_projector: bfloat16 [512, 512], replicated, may hold values from -0.25 to 0.25
- final_projector: bfloat16 [512, 512], replicated, may hold values from -0.25 to 0.25
- passing_inner_coefficients: bfloat16 [512, 1024], replicated, may hold values from -0.25 to 0.25
- passing_outer_coefficients: bfloat16 [1024, 512], replicated, may hold values from -0.1875 to 0.1875
- softness_per_subspace: float32 [8], replicated, may hold values from 0.5 to 2
- mixing_layer_gain: float32 [512], replicated, may hold values from 0.5 to 1.5
Outputs:
- result: bfloat16 [4096, 512], P(('dom', 'head'))
Inputs may be any that keep to these rules, and one draw needn't show every extreme that they name: `adjacent_group_bank_ids`: -1 marks a block without edges. The entry of a block for itself is never -1, nor is at least one entry for each neighbouring partition.
All inputs are finite; a program needn't handle non-finite values.
Results may differ from a plain program's by a relative error of at most 0.0054.
Values may be sent and summed in bfloat16 or wider, within the bound.
No kernel may reach another device: no remote copies, remote signals or barrier semaphores. Data moves between devices by JAX's collectives and lax.ppermute only.
A program may use at most 64 MiB of HBM per device.

v0:
```python
import math

import jax
import jax.numpy as jnp
from jax import lax
from jax.sharding import PartitionSpec as P

NUM_SUBSPACES = 8
SUBSPACE_WIDTH = 64


norm_eps = 1e-06


def extended(shard, sides, width):
    for axis, dim in sides:
        devices, length = (lax.axis_size(axis), shard.shape[dim])
        up = [(i, (i + 1) % devices) for i in range(devices - 1)]
        down = [(j, i) for i, j in up]
        last = lax.slice_in_dim(shard, length - width, length, axis=dim)
        first = lax.slice_in_dim(shard, 0, width, axis=dim)
        before = lax.ppermute(last, axis, up)
        after = lax.ppermute(first, axis, down)
        shard = jnp.concatenate([before, shard, after], axis=dim)
    return shard


def head_norm(projected, scales):
    rows = projected.shape[0]
    grouped = projected.reshape(rows, -1, SUBSPACE_WIDTH)
    mean_square = jnp.mean(grouped * grouped, axis=-1, keepdims=True)
    scaled = grouped * lax.rsqrt(mean_square + norm_eps)
    if scales is not None:
        scaled = scaled * scales[None, :, None]
    return scaled.reshape(rows, -1).astype(jnp.bfloat16)


def shards(
    vertex_embeddings,
    adjacent_group_bank_ids,
    coupling_strength_panels,
    asking_projector,
    lookup_projector,
    content_projector,
    final_projector,
    passing_inner_coefficients,
    passing_outer_coefficients,
    softness_per_subspace,
    mixing_layer_gain,
):
    block_len = vertex_embeddings.shape[0]
    group_size = lax.axis_size("head")
    heads_here = NUM_SUBSPACES // group_size
    head_cols = heads_here * SUBSPACE_WIDTH
    slot_ids = adjacent_group_bank_ids.reshape(-1)
    halo_rows = extended(vertex_embeddings, (("dom", 0),), block_len)
    nearby = lax.all_gather(halo_rows, "head", axis=0, tiled=True)
    slot_order = slot_ids.reshape(3, group_size).T.reshape(-1)
    asking_vector_multiplier = softness_per_subspace / math.sqrt(SUBSPACE_WIDTH)
    queries = head_norm(
        jnp.dot(vertex_embeddings, asking_projector, preferred_element_type=jnp.float32),
        asking_vector_multiplier,
    )
    keys_all = head_norm(
        jnp.dot(vertex_embeddings, lookup_projector, preferred_element_type=jnp.float32), None
    )
    values_all = jnp.dot(
        vertex_embeddings, content_projector, preferred_element_type=jnp.float32
    ).astype(jnp.bfloat16)
    queries, keys_all, values_all = (
        lax.all_to_all(queries, "head", split_axis=1, concat_axis=0, tiled=True),
        lax.all_to_all(keys_all, "head", split_axis=1, concat_axis=0, tiled=True),
        lax.all_to_all(values_all, "head", split_axis=1, concat_axis=0, tiled=True),
    )
    selected = jnp.take(coupling_strength_panels, jnp.maximum(slot_order, 0), axis=0)
    selected = jnp.where((slot_order >= 0)[:, None, None], selected, jnp.zeros_like(selected))
    wide_tiles = jnp.transpose(selected, (1, 0, 2)).reshape(block_len, -1)
    aggregate = jnp.dot(wide_tiles, nearby, preferred_element_type=jnp.float32).astype(jnp.bfloat16)
    hidden = jax.nn.gelu(
        jnp.dot(aggregate, passing_inner_coefficients, preferred_element_type=jnp.float32)
    ).astype(jnp.bfloat16)
    local_term = jnp.dot(hidden, passing_outer_coefficients, preferred_element_type=jnp.float32)
    query_rows = queries.shape[0]
    start_totals = (
        jnp.zeros((query_rows, head_cols), jnp.float32),
        jnp.zeros((query_rows, heads_here), jnp.float32),
    )
    keys_in = lax.all_gather(keys_all, "dom", axis=0, tiled=True)
    values_in = lax.all_gather(values_all, "dom", axis=0, tiled=True)
    key_count = keys_in.shape[0]
    block_step = key_count
    while block_step > 2048 and block_step % 2 == 0:
        block_step = block_step // 2

    def accumulate(turn_index, totals):
        numerator, denominator = totals
        key_block = lax.dynamic_slice_in_dim(keys_in, turn_index * block_step, block_step, 0)
        value_block = lax.dynamic_slice_in_dim(values_in, turn_index * block_step, block_step, 0)
        new_numer = []
        new_denom = []
        for head_id in range(heads_here):
            cols = slice(head_id * SUBSPACE_WIDTH, (head_id + 1) * SUBSPACE_WIDTH)
            scores = jnp.einsum(
                "qd,kd->qk",
                queries[:, cols],
                key_block[:, cols],
                preferred_element_type=jnp.float32,
            )
            weights = jnp.exp(scores).astype(jnp.bfloat16)
            new_denom.append(jnp.sum(weights, axis=1, dtype=jnp.float32))
            new_numer.append(
                jnp.dot(weights, value_block[:, cols], preferred_element_type=jnp.float32)
            )
        return (
            numerator + jnp.concatenate(new_numer, axis=1),
            denominator + jnp.stack(new_denom, axis=1),
        )

    numerator, denominator = lax.fori_loop(0, key_count // block_step, accumulate, start_totals)
    merged = (
        (numerator.reshape(query_rows, heads_here, SUBSPACE_WIDTH) / denominator[:, :, None])
        .reshape(query_rows, head_cols)
        .astype(jnp.bfloat16)
    )
    node_heads = lax.all_to_all(merged, "head", split_axis=0, concat_axis=1, tiled=True)
    attended = jnp.dot(node_heads, final_projector, preferred_element_type=jnp.float32)
    normed = (
        attended
        * lax.rsqrt(jnp.mean(attended * attended, axis=-1, keepdims=True) + norm_eps)
        * mixing_layer_gain
    )
    return (vertex_embeddings.astype(jnp.float32) + local_term + normed).astype(jnp.bfloat16)


def solution(mesh):
    in_specs = (
        P(("dom", "head"), None),
        P("dom", "head", None),
        P(),
        P(),
        P(),
        P(),
        P(),
        P(),
        P(),
        P(),
        P(),
    )
    out_specs = P(("dom", "head"), None)
    return jax.shard_map(shards, mesh=mesh, in_specs=in_specs, out_specs=out_specs, check_vma=False)
```

profile of v0, /device:TPU:0, one launch (start us, length us, event | category | flops | bytes accessed | tf_op | source)
XLA Modules:
  0.0 130.3 jit_solution(14132911110758012199)
XLA Ops:
  6.5 1.5 %fusion.25 = (f32[128,512]{1,0:T(8,128)S(1)}, f32[128,512]{1,0:T(8,128)S(1)}) fusion(bf16[128,512]{1,0:T(8,128)(2,1)} %param.13, bf16[512,512]{1,0:T(8,128)(2,1)} %param.17), kind=kOutput, calls=%fused_computation.55 | convolution fusion | flops 67174400 | bytes 1179648 | tf_op jit(solution)/shard_map/dot_general | solution.py:65
  8.0 0.1 copy.59
  8.2 0.1 copy.60
  8.4 8.8 %all_to_all.76 = bf16[128,4,128]{2,0,1:T(8,128)(2,1)} all-to-all(bf16[128,4,128]{2,0,1:T(8,128)(2,1)S(1)} %copy_bitcast_fusion.2), channel_id=1, replica_groups=mesh['dom'=8,'head'=4] {'head'}, dimensions={1} | all-to-all | bytes 262144 | tf_op jit(solution)/shard_map/all_to_all | solution.py:72
  17.3 0.2 fusion.12
  17.6 7.8 %all_to_all.77 = bf16[128,4,128]{2,0,1:T(8,128)(2,1)} all-to-all(bf16[128,4,128]{2,0,1:T(8,128)(2,1)S(1)} %bitcast.74), channel_id=1, replica_groups=mesh['dom'=8,'head'=4] {'head'}, dimensions={1} | all-to-all | bytes 262144 | tf_op jit(solution)/shard_map/all_to_all | solution.py:73
  25.4 3.8 %collective-permute-start = (bf16[128,512]{1,0:T(8,128)(2,1)S(1)}, bf16[128,512]{1,0:T(8,128)(2,1)S(1)}, u32[]{:S(2)}, u32[]{:S(2)}) collective-permute-start(bf16[128,512]{1,0:T(8,128)(2,1)S(1)} %copy-done.2), channel_id=1, source_target_pairs={{0,4},{4,8},{8,12},{12,16},{16,20},{20,24},{24,28},{1,5},{5,9},{9,... | collective-permute-start | bytes 393224 | tf_op jit(solution)/shard_map/ppermute | solution.py:22
  29.2 1.3 collective-permute-start.1
  30.5 0.2 fusion.26
  30.7 0.1 copy.62
  30.9 0.1 copy.63
  31.2 0.7 copy_bitcast_fusion.1
  31.9 3.3 %all-to-all-start.1 = ((bf16[128,4,128]{2,0,1:T(8,128)(2,1)}), bf16[128,4,128]{2,0,1:T(8,128)(2,1)S(1)}, u32[]{:S(2)}, u32[]{:S(2)}) async-start(bf16[128,4,128]{2,0,1:T(8,128)(2,1)} %copy_bitcast_fusion.1), calls=%async_computation.1 | async-start | bytes 262144 | tf_op jit(solution)/shard_map/all_to_all | solution.py:71
  35.4 0.1 ge.22
  35.5 0.1 copy.55
  35.6 0.1 ge.24
  35.7 0.1 le.17
  35.8 0.1 copy.56
  35.9 0.1 le.19
  36.0 0.1 max.25
  36.0 0.1 copy.57
  36.1 0.1 reshape.95
  36.2 0.6 gather_fusion
  36.9 0.8 pad_maximum_fusion
  37.7 2.2 %all-to-all-done.1 = bf16[128,4,128]{2,0,1:T(8,128)(2,1)S(1)} async-done(((bf16[128,4,128]{2,0,1:T(8,128)(2,1)}), bf16[128,4,128]{2,0,1:T(8,128)(2,1)S(1)}, u32[]{:S(2)}, u32[]{:S(2)}) %all-to-all-start.1) | async-done | bytes 131104 | tf_op jit(solution)/shard_map/all_to_all | solution.py:71
  39.9 18.3 %all-gather.6.cloned.1.call-done = bf16[4096,128]{1,0:T(8,128)(2,1)} async-done(((bf16[512,128]{1,0:T(8,128)(2,1)}), bf16[4096,128]{1,0:T(8,128)(2,1)}) %all-gather.6.cloned.1.call-update) | async-done | bytes 1048592 | tf_op jit(solution)/shard_map/all_gather | solution.py:88
  58.2 41.1 %all-gather.8.cloned.1.call-done = bf16[4096,128]{1,0:T(8,128)(2,1)} async-done(((bf16[512,128]{1,0:T(8,128)(2,1)}), bf16[4096,128]{1,0:T(8,128)(2,1)}) %all-gather.8.cloned.1.call-update) | async-done | bytes 1048592 | tf_op jit(solution)/shard_map/all_gather | solution.py:89
  99.2 8.4 %while.16 = (s32[]{:T(128)}, f32[512,128]{0,1:T(8,128)S(1)}, f32[512,2]{0,1:T(2,128)S(1)}, bf16[4096,128]{1,0:T(8,128)(2,1)}, bf16[512,128]{1,0:T(8,128)(2,1)S(1...) while((s32[]{:T(128)}, f32[512,128]{0,1:T(8,128)S(1)}, ...), condition=%wide.region_5.6_spmd.clone, body=%wide.region_2.5_spmd.clone.sunk | while | flops 543361024 | bytes 20201728 | solution.py:119
  99.2 2.1 %convert_reduce_fusion.4 = (f32[512]{0:T(512)S(1)}, bf16[2048,512]{1,0:T(8,128)(2,1)S(1)}) fusion(bf16[512,128]{1,0:T(8,128)(2,1)S(1)} %get-tuple-element.233, bf16[4096,128]{1,0:T(8,128)(2,1)} %get-tuple-element.232, s32[]{:T(128)S(6)} %select_n.32, s32[]{:T(128)S(6)} %add.150), kind=kOutput, calls=%fused_computation.1.clone.1 | convolution fusion | flops 137362944 | bytes 2754568 | tf_op jit(solution)/shard_map/while/body/eval_jaxpr/qd,kd->qk/dot_general | solution.py:103
  101.3 0.7 fusion.54
  102.0 0.7 convert_reduce_fusion.5
  102.7 0.5 fusion.55
  103.3 0.1 maximum_add_fusion.4
  103.4 2.1 %convert_reduce_fusion.4 = (f32[512]{0:T(512)S(1)}, bf16[2048,512]{1,0:T(8,128)(2,1)S(1)}) fusion(bf16[512,128]{1,0:T(8,128)(2,1)S(1)} %get-tuple-element.233, bf16[4096,128]{1,0:T(8,128)(2,1)} %get-tuple-element.232, s32[]{:T(128)S(6)} %select_n.32, s32[]{:T(128)S(6)} %add.150), kind=kOutput, calls=%fused_computation.1.clone.1 | convolution fusion | flops 137362944 | bytes 2754568 | tf_op jit(solution)/shard_map/while/body/eval_jaxpr/qd,kd->qk/dot_general | solution.py:103
  105.5 0.7 fusion.54
  106.2 0.7 convert_reduce_fusion.5
  106.9 0.5 fusion.55
  107.5 0.1 maximum_add_fusion.4
  107.6 0.8 copy.66
  108.4 3.3 %all-to-all-start.3 = ((bf16[4,128,128]{2,1,0:T(8,128)(2,1)}), bf16[4,128,128]{2,1,0:T(8,128)(2,1)S(1)}, u32[]{:S(2)}, u32[]{:S(2)}) async-start(bf16[4,128,128]{2,1,0:T(8,128)(2,1)} %bitcast.16), calls=%async_computation.3 | async-start | bytes 262144 | tf_op jit(solution)/shard_map/all_to_all | solution.py:125
  111.7 0.1 select_bitcast_fusion
  111.8 0.2 copy.58
  112.1 5.9 %all-to-all-done.3 = bf16[4,128,128]{2,1,0:T(8,128)(2,1)S(1)} async-done(((bf16[4,128,128]{2,1,0:T(8,128)(2,1)}), bf16[4,128,128]{2,1,0:T(8,128)(2,1)S(1)}, u32[]{:S(2)}, u32[]{:S(2)}) %all-to-all-start.3) | async-done | bytes 131104 | tf_op jit(solution)/shard_map/all_to_all | solution.py:125
  118.0 0.1 copy.67
  118.2 0.3 multiply_reduce_fusion
  118.6 2.1 %all-gather.4.cloned.1.call-done = bf16[1536,512]{1,0:T(8,128)(2,1)} async-done(((bf16[384,512]{1,0:T(8,128)(2,1)}), bf16[1536,512]{1,0:T(8,128)(2,1)}) %all-gather.4.cloned.1.call-update) | async-done | bytes 1572880 | tf_op jit(solution)/shard_map/all_gather | solution.py:57
  120.6 2.1 %fusion.21 = bf16[128,1024]{1,0:T(8,128)(2,1)S(1)} fusion(bf16[512,1024]{1,0:T(8,128)(2,1)S(1)} %copy-done, bf16[128,1536]{0,1:T(8,128)(2,1)S(1)} %bitcast.75, bf16[1536,512]{1,0:T(8,128)(2,1)} %all-gather.4.cloned.1.call-done), kind=kOutput, calls=%fused_computation.32 | convolution fusion | flops 336789504 | bytes 3276800 | tf_op jit(solution)/shard_map/dot_general | solution.py:80
  122.8 1.0 fusion.11
  (56 shorter events, 0.6 us)
Async XLA Ops:
  6.5 114.1 %copy-start = (bf16[512,1024]{1,0:T(8,128)(2,1)S(1)}, bf16[512,1024]{1,0:T(8,128)(2,1)}, u32[]{:S(2)}) copy-start(bf16[512,1024]{1,0:T(8,128)(2,1)} %param.20) | copy-start | bytes 3145732
  6.5 10.7 %copy-start.2 = (bf16[128,512]{1,0:T(8,128)(2,1)S(1)}, bf16[128,512]{1,0:T(8,128)(2,1)}, u32[]{:S(2)}) copy-start(bf16[128,512]{1,0:T(8,128)(2,1)} %param.13) | copy-start | bytes 393220
  6.5 10.7 %copy-start.4 = (bf16[512,512]{1,0:T(8,128)(2,1)S(1)}, bf16[512,512]{1,0:T(8,128)(2,1)}, u32[]{:S(2)}) copy-start(bf16[512,512]{1,0:T(8,128)(2,1)} %param.18) | copy-start | bytes 1572868
  6.5 51.6 %all-gather.6.cloned.1.call-start = ((), (), s32[]{:S(2)}) async-start(), calls=%async_computation.5 | async-start | bytes 1179648 | tf_op jit(solution)/shard_map/all_gather | solution.py:88
  8.0 22.5 %copy-start.5 = (bf16[512,512]{1,0:T(8,128)(2,1)S(1)}, bf16[512,512]{1,0:T(8,128)(2,1)}, u32[]{:S(2)}) copy-start(bf16[512,512]{1,0:T(8,128)(2,1)} %param.16) | copy-start | bytes 1572868
  17.2 13.9 %copy-start.10 = (f32[8]{0:T(128)S(1)}, f32[8]{0:T(128)}, u32[]{:S(2)}) copy-start(f32[8]{0:T(128)} %param.22) | copy-start | bytes 100
  17.2 82.0 %all-gather.8.cloned.1.call-start = ((), (), s32[]{:S(2)}) async-start(), calls=%async_computation.6 | async-start | bytes 1179648 | tf_op jit(solution)/shard_map/all_gather | solution.py:89
  17.6 17.8 %copy-start.11 = (s32[1,1,12]{2,1,0:T(1,128)S(1)}, s32[1,1,12]{2,1,0:T(1,128)}, u32[]{:S(2)}) copy-start(s32[1,1,12]{2,1,0:T(1,128)} %param.14) | copy-start | bytes 148
  17.6 18.7 %copy-start.7 = (bf16[16,128,128]{2,1,0:T(8,128)(2,1)S(1)}, bf16[16,128,128]{2,1,0:T(8,128)(2,1)}, u32[]{:S(2)}) copy-start(bf16[16,128,128]{2,1,0:T(8,128)(2,1)} %param.15) | copy-start | bytes 1572868
  25.4 11.5 %collective-permute-start = (bf16[128,512]{1,0:T(8,128)(2,1)S(1)}, bf16[128,512]{1,0:T(8,128)(2,1)S(1)}, u32[]{:S(2)}, u32[]{:S(2)}) collective-permute-start(bf16[128,512]{1,0:T(8,128)(2,1)S(1)} %copy-done.2), channel_id=1, source_target_pairs={{0,4},{4,8},{8,12},{12,16},{16,20},{20,24},{24,28},{1,5},{5,9},{9,... | collective-permute-start | bytes 393224 | tf_op jit(solution)/shard_map/ppermute | solution.py:22
  29.2 7.7 %collective-permute-start.1 = (bf16[128,512]{1,0:T(8,128)(2,1)S(1)}, bf16[128,512]{1,0:T(8,128)(2,1)S(1)}, u32[]{:S(2)}, u32[]{:S(2)}) collective-permute-start(bf16[128,512]{1,0:T(8,128)(2,1)S(1)} %copy-done.2), channel_id=1, source_target_pairs={{4,0},{8,4},{12,8},{16,12},{20,16},{24,20},{28,24},{5,1},{9,5},{13... | collective-permute-start | bytes 393224 | tf_op jit(solution)/shard_map/ppermute | solution.py:23
  31.9 7.9 %all-to-all-start.1 = ((bf16[128,4,128]{2,0,1:T(8,128)(2,1)}), bf16[128,4,128]{2,0,1:T(8,128)(2,1)S(1)}, u32[]{:S(2)}, u32[]{:S(2)}) async-start(bf16[128,4,128]{2,0,1:T(8,128)(2,1)} %copy_bitcast_fusion.1), calls=%async_computation.1 | async-start | bytes 262144 | tf_op jit(solution)/shard_map/all_to_all | solution.py:71
  35.3 85.4 %all-gather.4.cloned.1.call-start = ((), (), s32[]{:S(2)}) async-start(), calls=%async_computation.4 | async-start | bytes 1966080 | tf_op jit(solution)/shard_map/all_gather | solution.py:57
  99.2 2.1 %copy-start.1 = (bf16[4096,128]{1,0:T(8,128)(2,1)S(1)}, bf16[4096,128]{1,0:T(8,128)(2,1)}, u32[]{:S(2)}) copy-start(bf16[4096,128]{1,0:T(8,128)(2,1)} %get-tuple-element.234) | copy-start | bytes 3145732 | tf_op jit(solution)/shard_map/while
  99.2 2.8 %copy-start.9 = (bf16[4096,128]{1,0:T(8,128)(2,1)S(1)}, bf16[4096,128]{1,0:T(8,128)(2,1)}, u32[]{:S(2)}) copy-start(bf16[4096,128]{1,0:T(8,128)(2,1)} %get-tuple-element.232) | copy-start | bytes 3145732 | tf_op jit(solution)/shard_map/while
  103.4 2.1 %copy-start.1 = (bf16[4096,128]{1,0:T(8,128)(2,1)S(1)}, bf16[4096,128]{1,0:T(8,128)(2,1)}, u32[]{:S(2)}) copy-start(bf16[4096,128]{1,0:T(8,128)(2,1)} %get-tuple-element.234) | copy-start | bytes 3145732 | tf_op jit(solution)/shard_map/while
  103.4 2.8 %copy-start.9 = (bf16[4096,128]{1,0:T(8,128)(2,1)S(1)}, bf16[4096,128]{1,0:T(8,128)(2,1)}, u32[]{:S(2)}) copy-start(bf16[4096,128]{1,0:T(8,128)(2,1)} %get-tuple-element.232) | copy-start | bytes 3145732 | tf_op jit(solution)/shard_map/while
  107.6 10.6 %copy-start.6 = (bf16[512,512]{1,0:T(8,128)(2,1)S(1)}, bf16[512,512]{1,0:T(8,128)(2,1)}, u32[]{:S(2)}) copy-start(bf16[512,512]{1,0:T(8,128)(2,1)} %param.19) | copy-start | bytes 1572868
  108.4 9.7 %all-to-all-start.3 = ((bf16[4,128,128]{2,1,0:T(8,128)(2,1)}), bf16[4,128,128]{2,1,0:T(8,128)(2,1)S(1)}, u32[]{:S(2)}, u32[]{:S(2)}) async-start(bf16[4,128,128]{2,1,0:T(8,128)(2,1)} %bitcast.16), calls=%async_computation.3 | async-start | bytes 262144 | tf_op jit(solution)/shard_map/all_to_all | solution.py:125
  118.2 4.6 %copy-start.3 = (bf16[1024,512]{1,0:T(8,128)(2,1)S(1)}, bf16[1024,512]{1,0:T(8,128)(2,1)}, u32[]{:S(2)}) copy-start(bf16[1024,512]{1,0:T(8,128)(2,1)} %param.21) | copy-start | bytes 3145732
  118.2 4.6 %copy-start.8 = (f32[512]{0:T(512)S(1)}, f32[512]{0:T(512)}, u32[]{:S(2)}) copy-start(f32[512]{0:T(512)} %param.23) | copy-start | bytes 6148
Sparse Core Ops, SparseCore 0:
  17.3 40.7 all-gather.5
  60.3 38.8 all-gather.7
  100.8 19.8 all-gather.3
where the time goes:
time: 131 us; the launch traced here: 130 us
  waiting for transfers between devices  69.6 us (53%)
  blocking collectives  16.6 us (13%)
  between operations  13.5 us (10%)
  matrix products  13.4 us (10%)
  starting transfers between devices  11.8 us (9%)
  local copies, waits for them, and re-layouts  3.37 us (3%)
  other arithmetic  1.99 us (2%)
    all_gather x1, waiting for transfers between devices, shards(): values_in = lax.all_gather(values_all, 'dom', axis=0, tiled=True)  41.1 us
    all_gather x1, waiting for transfers between devices, shards(): keys_in = lax.all_gather(keys_all, 'dom', axis=0, tiled=True)  18.3 us
    all_to_all x1, blocking collectives, shards(): lax.all_to_all(keys_all, 'head', split_axis=1, concat_axis=0, tiled=True)  8.78 us
    all_to_all x1, blocking collectives, shards(): lax.all_to_all(values_all, 'head', split_axis=1, concat_axis=0, tiled=True)  7.81 us
    all_to_all x1, waiting for transfers between devices, shards(): lax.all_to_all(merged, 'head', split_axis=0, concat_axis=1, tiled=True)  5.95 us
    dot_general x4, matrix products, accumulate(): jnp.einsum('qd,kd->qk', queries[:, cols], key_block[:, cols], preferred_e...  5.58 us
    ppermute x1, starting transfers between devices, extended(): before = lax.ppermute(last, axis, up)  3.75 us
    all_to_all x1, starting transfers between devices, shards(): lax.all_to_all(queries, 'head', split_axis=1, concat_axis=0, tiled=True)  3.33 us
  transfers between devices with their start and end apart: 7, of which 5 were waited for; matrix products, arithmetic and copies ran while one was open for 11% of the time, Pallas kernels for 0%

commit v1 on v0

v1 whole, which is shorter than its diff:
```python
import math

import jax
import jax.numpy as jnp
from jax import lax
from jax.experimental import pallas as pl
from jax.experimental.pallas import tpu as pltpu
from jax.sharding import PartitionSpec as P

NUM_SUBSPACES = 8
SUBSPACE_WIDTH = 64
PAIRS = NUM_SUBSPACES // 2
LANES = 128
norm_eps = 1e-06
VMEM = pl.BlockSpec(memory_space=pltpu.VMEM)
SMEM = pl.BlockSpec(memory_space=pltpu.SMEM)
F32 = jnp.float32
BF16 = jnp.bfloat16
VMEM_LIMIT = 48 * 1024 * 1024


def params():
    return pltpu.CompilerParams(vmem_limit_bytes=VMEM_LIMIT)


def cost(flops, transcendentals, data):
    return pl.CostEstimate(flops=flops, transcendentals=transcendentals, bytes_accessed=data)


def swap(array, axis, mask):
    devices = lax.axis_size(axis)
    return lax.ppermute(array, axis, [(i, i ^ mask) for i in range(devices)])


def swap_both(array, dom_mask, head_mask):
    doms, heads = lax.axis_size("dom"), lax.axis_size("head")
    pairs = [
        (d * heads + h, (d ^ dom_mask) * heads + (h ^ head_mask))
        for d in range(doms)
        for h in range(heads)
    ]
    return lax.ppermute(array, ("dom", "head"), pairs)


def dot(a, b):
    return jnp.dot(a, b, preferred_element_type=F32)


def dot_t(a, b):
    return lax.dot_general(a, b, (((1,), (1,)), ((), ())), preferred_element_type=F32)


def same_head(rows, cols, value):
    row = lax.broadcasted_iota(jnp.int32, (rows, cols), 0) // SUBSPACE_WIDTH
    col = lax.broadcasted_iota(jnp.int32, (rows, cols), 1) // SUBSPACE_WIDTH
    return jnp.where(row == col, value, 0.0).astype(BF16)


def head_normed(projected):
    block = same_head(256, 256, 1.0 / SUBSPACE_WIDTH)
    squares = (projected * projected).astype(BF16)
    mean = jnp.concatenate(
        [dot(squares[:, i : i + 256], block) for i in range(0, projected.shape[1], 256)], axis=1
    )
    return projected * lax.rsqrt(mean + norm_eps)


def padded_queries(queries, pair):
    both = queries[:, pair * LANES : (pair + 1) * LANES]
    first = lax.broadcasted_iota(jnp.int32, both.shape, 1) < SUBSPACE_WIDTH
    zero = jnp.zeros_like(both)
    return jnp.concatenate([jnp.where(first, both, zero), jnp.where(first, zero, both)], axis=0)


def attend(queries, keys_ref, values_ref):
    rows = queries.shape[0]
    count = keys_ref.shape[0]
    ones = jnp.ones((count, LANES), BF16)
    numer, denom = [], []
    first = lax.broadcasted_iota(jnp.int32, (rows, LANES), 1) < SUBSPACE_WIDTH
    for pair in range(PAIRS):
        cols = slice(pair * LANES, (pair + 1) * LANES)
        scores = dot_t(padded_queries(queries, pair), keys_ref[:, cols])
        weights = jnp.exp2(scores).astype(BF16)
        sums = dot(weights, jnp.concatenate([values_ref[:, cols], ones], axis=1))
        numer.append(jnp.where(first, sums[:rows, :LANES], sums[rows:, :LANES]))
        denom.append(jnp.where(first, sums[:rows, LANES:], sums[rows:, LANES:]))
    return jnp.concatenate(numer, axis=1), jnp.concatenate(denom, axis=1)


def keys_values(blocks, lookup_ref, content_ref, keys_ref, values_ref):
    nodes = jnp.concatenate([block[...] for block in blocks], axis=0)
    keys_ref[...] = head_normed(dot(nodes, lookup_ref[...])).astype(BF16)
    values_ref[...] = dot(nodes, content_ref[...]).astype(BF16)


def near_kernel(softness_ref, mine_ref, other_ref, *refs):
    blocks, (asking_ref, lookup_ref, content_ref) = refs[:8], refs[8:11]
    queries_ref, numer_ref, denom_ref, keys_ref, values_ref = refs[11:]
    width = asking_ref.shape[1]
    head = lax.broadcasted_iota(jnp.int32, (1, width), 1) // SUBSPACE_WIDTH
    scale = jnp.zeros((1, width), F32)
    for h in range(NUM_SUBSPACES):
        scale = jnp.where(head == h, softness_ref[h], scale)
    scale = scale * (math.log2(math.e) / math.sqrt(SUBSPACE_WIDTH))
    rows = jnp.concatenate([mine_ref[...], other_ref[...]], axis=0)
    queries = (head_normed(dot(rows, asking_ref[...])) * scale).astype(BF16)
    queries_ref[...] = queries
    keys_values(blocks, lookup_ref, content_ref, keys_ref, values_ref)
    numer_ref[...], denom_ref[...] = attend(queries, keys_ref, values_ref)


def near(softness, mine, other, blocks, asking, lookup, content):
    rows, width = 2 * mine.shape[0], mine.shape[1]
    count = len(blocks) * mine.shape[0]
    return pl.pallas_call(
        near_kernel,
        out_shape=(
            jax.ShapeDtypeStruct((rows, width), BF16),
            jax.ShapeDtypeStruct((rows, width), F32),
            jax.ShapeDtypeStruct((rows, width), F32),
        ),
        in_specs=[SMEM] + [VMEM] * 13,
        out_specs=(VMEM,) * 3,
        scratch_shapes=[pltpu.VMEM((count, width), BF16)] * 2,
        compiler_params=params(),
        cost_estimate=cost(8 * rows * count * width, rows * count * NUM_SUBSPACES, 4 << 20),
        name="near",
    )(softness, mine, other, *blocks, asking, lookup, content)


def packing(width, wide):
    lane = lax.broadcasted_iota(jnp.int32, (width, LANES), 1)
    col = lax.broadcasted_iota(jnp.int32, (width, LANES), 0)
    if wide:
        return lane, col // SUBSPACE_WIDTH
    return lane * SUBSPACE_WIDTH, col


def pack(numer, denom):
    width = numer.shape[1]
    high = denom.astype(BF16)
    low = (denom - high.astype(F32)).astype(BF16)
    lane, col = packing(width, False)
    to_high = jnp.where((lane == col), 1.0, 0.0).astype(BF16)
    to_low = jnp.where((lane == col + width), 1.0, 0.0).astype(BF16)
    sums = dot(high, to_high) + dot(low, to_low)
    return jnp.concatenate([numer.astype(BF16), sums.astype(BF16)], axis=1)


def unpack_denom(packed, width):
    lane, head = packing(width, True)
    spread = ((lane == head) | (lane == head + NUM_SUBSPACES)) & (lane < 2 * NUM_SUBSPACES)
    return dot_t(packed, jnp.where(spread, 1.0, 0.0).astype(BF16))


def far_kernel(*refs):
    blocks, (lookup_ref, content_ref, queries_ref, numer_ref, denom_ref) = refs[:8], refs[8:13]
    keys_ref, values_ref, packed_ref, numer_sum, denom_sum = refs[13:]
    step = pl.program_id(0)
    half = queries_ref.shape[0] // 2

    @pl.when(step == 0)
    def _():
        numer_sum[...] = numer_ref[half:, :]
        denom_sum[...] = denom_ref[half:, :]

    keys_values(blocks, lookup_ref, content_ref, keys_ref, values_ref)
    numer, denom = attend(queries_ref[half:, :], keys_ref, values_ref)
    numer_sum[...] += numer
    denom_sum[...] += denom

    @pl.when(step == pl.num_programs(0) - 1)
    def _():
        packed_ref[...] = pack(numer_sum[...], denom_sum[...])


def far(blocks, block_len, lookup, content, queries, numer, denom):
    steps = blocks[0].shape[0] // block_len
    rows, width = queries.shape
    half = rows // 2
    count = len(blocks) * block_len
    whole = lambda shape: pl.BlockSpec(shape, lambda i: (0, 0))
    part = lambda size: pl.BlockSpec((size, width), lambda i: (i, 0))
    return pl.pallas_call(
        far_kernel,
        grid=(steps,),
        out_shape=(
            jax.ShapeDtypeStruct((steps * count, width), BF16),
            jax.ShapeDtypeStruct((steps * count, width), BF16),
            jax.ShapeDtypeStruct((half, width + LANES), BF16),
        ),
        in_specs=[part(block_len)] * 8
        + [whole((width, width))] * 2
        + [whole((rows, width))] * 3,
        out_specs=(part(count), part(count), whole((half, width + LANES))),
        scratch_shapes=[pltpu.VMEM((half, width), F32)] * 2,
        compiler_params=params(),
        cost_estimate=cost(
            6 * half * steps * count * width, half * steps * count * NUM_SUBSPACES, 4 << 20
        ),
        name="far",
    )(*blocks, lookup, content, queries, numer, denom)


def own_kernel(keys_ref, values_ref, queries_ref, numer_ref, denom_ref, numer_out, denom_out):
    half = queries_ref.shape[0] // 2

    @pl.when(pl.program_id(0) == 0)
    def _():
        numer_out[...] = numer_ref[:half, :]
        denom_out[...] = denom_ref[:half, :]

    numer, denom = attend(queries_ref[:half, :], keys_ref, values_ref)
    numer_out[...] += numer
    denom_out[...] += denom


def own(keys, values, count, queries, numer, denom):
    steps = keys.shape[0] // count
    rows, width = queries.shape
    half = rows // 2
    whole = lambda shape: pl.BlockSpec(shape, lambda i: (0, 0))
    part = lambda size: pl.BlockSpec((size, width), lambda i: (i, 0))
    return pl.pallas_call(
        own_kernel,
        grid=(steps,),
        out_shape=(jax.ShapeDtypeStruct((half, width), F32),) * 2,
        in_specs=[part(count)] * 2 + [whole((rows, width))] * 3,
        out_specs=(whole((half, width)),) * 2,
        compiler_params=params(),
        cost_estimate=cost(
            4 * half * steps * count * width, half * steps * count * NUM_SUBSPACES, 4 << 20
        ),
        name="own",
    )(keys, values, queries, numer, denom)


def message_kernel(slots_ref, place_ref, tiles_ref, *refs):
    blocks, (inner_ref, outer_ref, local_ref) = refs[:12], refs[12:]
    group = slots_ref.shape[0] // 3
    me, odd = place_ref[0], place_ref[1]
    sides = (1, 2 - 2 * odd, 2 * odd)
    tiles = []
    for i in range(12):
        tile_id = slots_ref[sides[i // 4] * group + (me ^ (i % 4))]
        tile = tiles_ref[jnp.maximum(tile_id, 0)]
        tiles.append(jnp.where(tile_id >= 0, tile, jnp.zeros_like(tile)))
    nodes = jnp.concatenate([block[...] for block in blocks], axis=0)
    aggregate = dot(jnp.concatenate(tiles, axis=1), nodes).astype(BF16)
    hidden = jax.nn.gelu(dot(aggregate, inner_ref[...])).astype(BF16)
    local_ref[...] = dot(hidden, outer_ref[...])


def message(slots, place, tiles, blocks, inner, outer):
    rows, width = blocks[0].shape
    hidden = inner.shape[1]
    return pl.pallas_call(
        message_kernel,
        out_shape=jax.ShapeDtypeStruct((rows, width), F32),
        in_specs=[SMEM, SMEM] + [VMEM] * 15,
        out_specs=VMEM,
        compiler_params=params(),
        cost_estimate=cost(
            2 * rows * width * (12 * rows + 2 * hidden), rows * hidden, 4 << 20
        ),
        name="message",
    )(slots, place, tiles, *blocks, inner, outer)


def finish_kernel(
    numer_ref, denom_ref, packed_ref, final_ref, gain_ref, local_ref, nodes_ref, out_ref
):
    width = numer_ref.shape[1]
    numer = numer_ref[...] + packed_ref[:, :width].astype(F32)
    denom = denom_ref[...] + unpack_denom(packed_ref[:, width:], width)
    mixed = (numer / denom).astype(BF16)
    attended = dot(mixed, final_ref[...])
    mean = jnp.mean(attended * attended, axis=-1, keepdims=True)
    normed = attended * lax.rsqrt(mean + norm_eps) * gain_ref[...]
    out_ref[...] = (nodes_ref[...].astype(F32) + local_ref[...] + normed).astype(BF16)


def finish(numer, denom, packed, final, gain, local, nodes):
    rows, width = nodes.shape
    return pl.pallas_call(
        finish_kernel,
        out_shape=jax.ShapeDtypeStruct((rows, width), BF16),
        in_specs=[VMEM] * 7,
        out_specs=VMEM,
        compiler_params=params(),
        cost_estimate=cost(2 * rows * width * width, rows, 2 << 20),
        name="finish",
    )(numer, denom, packed, final, gain, local, nodes)


def shards(
    vertex_embeddings,
    adjacent_group_bank_ids,
    coupling_strength_panels,
    asking_projector,
    lookup_projector,
    content_projector,
    final_projector,
    passing_inner_coefficients,
    passing_outer_coefficients,
    softness_per_subspace,
    mixing_layer_gain,
):
    block_len = vertex_embeddings.shape[0]
    doms = lax.axis_size("dom")
    nodes = vertex_embeddings

    distant = nodes[:0]
    mask = 4
    while mask < doms:
        held = jnp.concatenate([nodes, distant], axis=0) if mask > 4 else nodes
        arrived = swap(held, "dom", mask)
        distant = jnp.concatenate([distant, arrived], axis=0) if mask > 4 else arrived
        mask *= 2

    def plane(block):
        side = swap(block, "dom", 1)
        below = swap(block, "head", 2)
        across = swap_both(block, 1, 2)
        return block, below, side, across

    others = swap(nodes, "dom", 2)
    near_blocks = plane(nodes)
    near_twins = [swap(block, "head", 1) for block in near_blocks]
    pairs = [(p, p + 2) for p in range(0, doms - 2, 2)] + [(p, p - 2) for p in range(3, doms, 2)]
    halo = [lax.ppermute(block, "dom", pairs) for block in near_blocks[2:]]
    halo_twins = [swap(block, "head", 1) for block in halo]
    far_blocks = plane(distant)
    far_twins = [swap(block, "head", 1) for block in far_blocks]

    interleave = lambda a, b: [block for both in zip(a, b) for block in both]
    queries, numer, denom = near(
        softness_per_subspace,
        nodes,
        others,
        interleave(near_blocks, near_twins),
        asking_projector,
        lookup_projector,
        content_projector,
    )
    place = jnp.stack([lax.axis_index("head"), lax.axis_index("dom") % 2]).astype(jnp.int32)
    local = message(
        adjacent_group_bank_ids.reshape(-1),
        place,
        coupling_strength_panels,
        interleave(near_blocks, near_twins) + interleave(halo, halo_twins),
        passing_inner_coefficients,
        passing_outer_coefficients,
    )
    keys, values, packed = far(
        interleave(far_blocks, far_twins),
        block_len,
        lookup_projector,
        content_projector,
        queries,
        numer,
        denom,
    )
    packed = swap(packed, "dom", 2)
    numer, denom = own(keys, values, 8 * block_len, queries, numer, denom)
    return finish(
        numer,
        denom,
        packed,
        final_projector,
        mixing_layer_gain.reshape(1, -1),
        local,
        nodes,
    )


def solution(mesh):
    in_specs = (P(("dom", "head"), None), P("dom", "head", None)) + (P(),) * 9
    out_specs = P(("dom", "head"), None)
    return jax.shard_map(shards, mesh=mesh, in_specs=in_specs, out_specs=out_specs, check_vma=False)
```

time: 131 us -> 48.3 us (0.37)
  waiting for transfers between devices: 69.6 us -> 5.27 us
  blocking collectives: 16.6 us -> 0 us
  matrix products: 13.4 us -> 0 us
  between operations: 13.5 us -> 0.19 us
  starting transfers between devices: 11.8 us -> 24.6 us
  Pallas kernels: 0 us -> 11.7 us
  local copies, waits for them, and re-layouts: 3.37 us -> 6.08 us
  other arithmetic: 1.99 us -> 0.07 us
    all_gather x3 -> x0, waiting for transfers between devices: 61.4 us -> none  [the longest x1 41.1 us: shards(): values_in = lax.all_gather(values_all, 'dom', axis=0, tiled=True)]
    ppermute x2 -> x21, starting transfers between devices: 5.05 us -> 24.6 us  [the longest x17 9.95 us: swap(): return lax.ppermute(array, axis, [(i, i ^ mask) for i in range(devices)])]
    all_to_all x2 -> x0, blocking collectives: 16.6 us -> none  [the longest x1 8.78 us: shards(): lax.all_to_all(keys_all, 'head', split_axis=1, concat_axis=0, tiled=True)]
    dot_general x14 -> x0, matrix products: 13.4 us -> none  [the longest x4 5.58 us: accumulate(): jnp.einsum('qd,kd->qk', queries[:, cols], key_block[:, cols], preferred_e...]
    pallas_call x0 -> x5, Pallas kernels: none -> 11.7 us  [the longest x1 4.84 us: near(): pl.pallas_call(near_kernel, out_shape=(jax.ShapeDtypeStruct((rows, width)...]
    all_to_all x2 -> x0, waiting for transfers between devices: 8.12 us -> none  [the longest x1 5.95 us: shards(): lax.all_to_all(merged, 'head', split_axis=0, concat_axis=1, tiled=True)]
    all_to_all x2 -> x0, starting transfers between devices: 6.65 us -> none  [the longest x1 3.33 us: shards(): lax.all_to_all(queries, 'head', split_axis=1, concat_axis=0, tiled=True)]
    unnamed x20 -> x28, local copies, waits for them, and re-layouts: 0.06 us -> 6.08 us
  transfers between devices with their start and end apart: 7 -> 21, of which waited for: 5 -> 3; matrix products, arithmetic and copies ran while one was open for 11% -> 0% of each run, Pallas kernels for 0% -> 22%
where the time goes in v1:
time: 48.3 us; the launch traced here: 47.9 us
  starting transfers between devices  24.6 us (51%)
  Pallas kernels  11.7 us (24%)
  local copies, waits for them, and re-layouts  6.08 us (13%)
  waiting for transfers between devices  5.27 us (11%)
    ppermute x17, starting transfers between devices, swap(): return lax.ppermute(array, axis, [(i, i ^ mask) for i in range(devices)])  9.95 us
    ppermute x2, starting transfers between devices, swap_both(): return lax.ppermute(array, ('dom', 'head'), pairs)  7.75 us
    ppermute x2, starting transfers between devices, shards(): halo = [lax.ppermute(block, 'dom', pairs) for block in near_blocks[2:]]  6.86 us
    unnamed x28, local copies, waits for them, and re-layouts  6.08 us
    pallas_call x1, Pallas kernels, near(): pl.pallas_call(near_kernel, out_shape=(jax.ShapeDtypeStruct((rows, width)...  4.84 us
    ppermute x17, waiting for transfers between devices, swap(): return lax.ppermute(array, axis, [(i, i ^ mask) for i in range(devices)])  3.36 us
    pallas_call x1, Pallas kernels, far(): pl.pallas_call(far_kernel, grid=(steps,), out_shape=(jax.ShapeDtypeStruct...  2.96 us
    ppermute x2, waiting for transfers between devices, swap_both(): return lax.ppermute(array, ('dom', 'head'), pairs)  1.91 us
  transfers between devices with their start and end apart: 21, of which 3 were waited for; matrix products, arithmetic and copies ran while one was open for 0% of the time, Pallas kernels for 22%

profile of v1, /device:TPU:0, one launch (start us, length us, event | category | flops | bytes accessed | tf_op | source)
XLA Modules:
  0.0 47.9 jit_solution(13859936012450019387)
XLA Ops:
  0.0 3.9 %collective-permute-start.14 = (bf16[128,512]{1,0:T(8,128)(2,1)}, bf16[128,512]{1,0:T(8,128)(2,1)S(1)}, u32[]{:S(2)}, u32[]{:S(2)}) collective-permute-start(bf16[128,512]{1,0:T(8,128)(2,1)} %nodes_ref.1), channel_id=1, source_target_pairs={{0,6},{1,7},{2,4},{3,5},{4,2},{5,3},{6,0},{7,1},{8,14},{9,15},{10,... | collective-permute-start | bytes 393224 | tf_op jit(solution)/shard_map/ppermute | solution.py:42
  3.9 0.5 %collective-permute-start.12 = (bf16[128,512]{1,0:T(8,128)(2,1)}, bf16[128,512]{1,0:T(8,128)(2,1)S(1)}, u32[]{:S(2)}, u32[]{:S(2)}) collective-permute-start(bf16[128,512]{1,0:T(8,128)(2,1)} %nodes_ref.1), channel_id=1, source_target_pairs={{0,4},{4,0},{8,12},{12,8},{16,20},{20,16},{24,28},{28,24},{1,5},{5... | collective-permute-start | bytes 393224 | tf_op jit(solution)/shard_map/ppermute | solution.py:32
  4.4 0.0 collective-permute-start.10
  4.5 0.0 collective-permute-start.9
  4.5 2.1 %collective-permute-start.8 = (bf16[128,512]{1,0:T(8,128)(2,1)}, bf16[128,512]{1,0:T(8,128)(2,1)S(1)}, u32[]{:S(2)}, u32[]{:S(2)}) collective-permute-start(bf16[128,512]{1,0:T(8,128)(2,1)} %nodes_ref.1), channel_id=1, source_target_pairs={{0,8},{4,12},{8,0},{12,4},{16,24},{20,28},{24,16},{28,20},{1,9},{5... | collective-permute-start | bytes 393224 | tf_op jit(solution)/shard_map/ppermute | solution.py:32
  6.5 1.9 %collective-permute-done.14.refs_6_ = bf16[128,512]{1,0:T(8,128)(2,1)S(1)} collective-permute-done((bf16[128,512]{1,0:T(8,128)(2,1)}, bf16[128,512]{1,0:T(8,128)(2,1)S(1)}, u32[]{:S(2)}, u32[]{:S(2)}) %collective-permute-start.14) | collective-permute-done | bytes 131104 | tf_op jit(solution)/shard_map/ppermute | solution.py:42
  8.4 3.1 %collective-permute-start = (bf16[128,512]{1,0:T(8,128)(2,1)}, bf16[128,512]{1,0:T(8,128)(2,1)S(1)}, u32[]{:S(2)}, u32[]{:S(2)}) collective-permute-start(bf16[128,512]{1,0:T(8,128)(2,1)} %nodes_ref.1), channel_id=1, source_target_pairs={{0,16},{4,20},{8,24},{12,28},{16,0},{20,4},{24,8},{28,12},{1,17},{... | collective-permute-start | bytes 393224 | tf_op jit(solution)/shard_map/ppermute | solution.py:32
  11.5 0.0 collective-permute-done.12.refs_4_
  11.5 3.5 %collective-permute-start.19 = (bf16[128,512]{1,0:T(8,128)(2,1)S(1)}, bf16[128,512]{1,0:T(8,128)(2,1)S(1)}, u32[]{:S(2)}, u32[]{:S(2)}) collective-permute-start(bf16[128,512]{1,0:T(8,128)(2,1)S(1)} %collective-permute-done.14.refs_6_), channel_id=1, source_target_pairs={{0,8},{8,16},{16,24},{12,4},{20,12},{28,20},{1,9},{9,17},{17,25},{... | collective-permute-start | bytes 393224 | tf_op jit(solution)/shard_map/ppermute | solution.py:332
  15.0 0.0 collective-permute-done.10.refs_2_
  15.0 0.1 collective-permute-start.15
  15.1 0.5 %collective-permute-start.13 = (bf16[128,512]{1,0:T(8,128)(2,1)S(1)}, bf16[128,512]{1,0:T(8,128)(2,1)S(1)}, u32[]{:S(2)}, u32[]{:S(2)}) collective-permute-start(bf16[128,512]{1,0:T(8,128)(2,1)S(1)} %collective-permute-done.12.refs_4_), channel_id=1, source_target_pairs={{0,1},{1,0},{2,3},{3,2},{4,5},{5,4},{6,7},{7,6},{8,9},{9,8},{10,11... | collective-permute-start | bytes 393224 | tf_op jit(solution)/shard_map/ppermute | solution.py:32
  15.6 0.0 collective-permute-done.8.other_ref
  15.6 0.1 collective-permute-start.11
  15.7 1.5 %collective-permute-done.refs_0_ = bf16[128,512]{1,0:T(8,128)(2,1)S(1)} collective-permute-done((bf16[128,512]{1,0:T(8,128)(2,1)}, bf16[128,512]{1,0:T(8,128)(2,1)S(1)}, u32[]{:S(2)}, u32[]{:S(2)}) %collective-permute-start) | collective-permute-done | bytes 131104 | tf_op jit(solution)/shard_map/ppermute | solution.py:32
  17.2 3.9 %collective-permute-start.6 = (bf16[128,512]{1,0:T(8,128)(2,1)S(1)}, bf16[128,512]{1,0:T(8,128)(2,1)S(1)}, u32[]{:S(2)}, u32[]{:S(2)}) collective-permute-start(bf16[128,512]{1,0:T(8,128)(2,1)S(1)} %collective-permute-done.refs_0_), channel_id=1, source_target_pairs={{0,6},{1,7},{2,4},{3,5},{4,2},{5,3},{6,0},{7,1},{8,14},{9,15},{10,... | collective-permute-start | bytes 393224 | tf_op jit(solution)/shard_map/ppermute | solution.py:42
  21.1 0.0 collective-permute-done.15.refs_7_
  21.1 1.1 %collective-permute-start.2 = (bf16[128,512]{1,0:T(8,128)(2,1)S(1)}, bf16[128,512]{1,0:T(8,128)(2,1)S(1)}, u32[]{:S(2)}, u32[]{:S(2)}) collective-permute-start(bf16[128,512]{1,0:T(8,128)(2,1)S(1)} %collective-permute-done.refs_0_), channel_id=1, source_target_pairs={{0,2},{1,3},{2,0},{3,1},{4,6},{5,7},{6,4},{7,5},{8,10},{9,11},{10,... | collective-permute-start | bytes 393224 | tf_op jit(solution)/shard_map/ppermute | solution.py:32
  22.2 3.4 %collective-permute-start.17 = (bf16[128,512]{1,0:T(8,128)(2,1)S(1)}, bf16[128,512]{1,0:T(8,128)(2,1)S(1)}, u32[]{:S(2)}, u32[]{:S(2)}) collective-permute-start(bf16[128,512]{1,0:T(8,128)(2,1)S(1)} %collective-permute-done.12.refs_4_), channel_id=1, source_target_pairs={{0,8},{8,16},{16,24},{12,4},{20,12},{28,20},{1,9},{9,17},{17,25},{... | collective-permute-start | bytes 393224 | tf_op jit(solution)/shard_map/ppermute | solution.py:332
  25.6 0.0 collective-permute-done.11.refs_3_
  25.6 0.1 collective-permute-start.1
  25.7 0.5 %collective-permute-start.7 = (bf16[128,512]{1,0:T(8,128)(2,1)S(1)}, bf16[128,512]{1,0:T(8,128)(2,1)S(1)}, u32[]{:S(2)}, u32[]{:S(2)}) collective-permute-start(bf16[128,512]{1,0:T(8,128)(2,1)S(1)} %collective-permute-done.6.refs_6_), channel_id=1, source_target_pairs={{0,1},{1,0},{2,3},{3,2},{4,5},{5,4},{6,7},{7,6},{8,9},{9,8},{10,11... | collective-permute-start | bytes 393224 | tf_op jit(solution)/shard_map/ppermute | solution.py:32
  26.2 0.0 collective-permute-done.4.refs_4_
  26.2 0.1 collective-permute-start.5
  26.3 0.0 collective-permute-done.2.refs_2_
  26.3 0.4 collective-permute-start.3
  26.7 0.7 %copy-done.13 = f32[8]{0:T(128)S(1)} copy-done((f32[8]{0:T(128)S(1)}, f32[8]{0:T(128)}, u32[]{:S(2)}) %copy-start.13) | copy-done | bytes 56
  27.4 1.0 %copy-done.3 = bf16[512,512]{1,0:T(8,128)(2,1)S(1)} copy-done((bf16[512,512]{1,0:T(8,128)(2,1)S(1)}, bf16[512,512]{1,0:T(8,128)(2,1)}, u32[]{:S(2)}) %copy-start.3) | copy-done | bytes 524312
  28.4 1.0 %copy-done.5 = bf16[512,512]{1,0:T(8,128)(2,1)S(1)} copy-done((bf16[512,512]{1,0:T(8,128)(2,1)S(1)}, bf16[512,512]{1,0:T(8,128)(2,1)}, u32[]{:S(2)}) %copy-start.5) | copy-done | bytes 524312
  29.4 0.9 %copy-done.8 = bf16[128,512]{1,0:T(8,128)(2,1)S(1)} copy-done((bf16[128,512]{1,0:T(8,128)(2,1)S(1)}, bf16[128,512]{1,0:T(8,128)(2,1)}, u32[]{:S(2)}) %copy-start.8) | copy-done | bytes 131096
  30.4 1.0 %copy-done.12 = bf16[512,512]{1,0:T(8,128)(2,1)S(1)} copy-done((bf16[512,512]{1,0:T(8,128)(2,1)S(1)}, bf16[512,512]{1,0:T(8,128)(2,1)}, u32[]{:S(2)}) %copy-start.12) | copy-done | bytes 524312
  31.4 4.8 %near.1 = (bf16[256,512]{1,0:T(8,128)(2,1)S(1)}, f32[256,512]{1,0:T(8,128)S(1)}, f32[256,512]{1,0:T(8,128)S(1)}) custom-call(f32[8]{0:T(128)S(1)} %copy-done.13, bf16[128,512]{1,0:T(8,128)(2,1)S(1)} %copy-done.8, bf16[128,512]{1,0:T(8,128)(2,1)S(1)} %collective-permute-done.8.other_ref, bf16[128,512]{1,0:T(8,128)(2,1)S(1)} %copy-done.8, ...), custom_call_target="tpu_custom_call" | custom-call | flops 1073741824 | bytes 4194304 | tf_op jit(solution)/shard_map/near/pallas_call | solution.py:116
  36.3 0.2 collective-permute-start.20
  36.4 0.4 collective-permute-start.18
  36.8 0.0 collective-permute-done.7.refs_7_
  36.9 3.0 %far.1 = (bf16[1024,512]{1,0:T(8,128)(2,1)S(1)}, bf16[1024,512]{1,0:T(8,128)(2,1)S(1)}, bf16[128,640]{1,0:T(8,128)(2,1)S(1)}) custom-call(bf16[128,512]{1,0:T(8,128)(2,1)S(1)} %collective-permute-done.refs_0_, bf16[128,512]{1,0:T(8,128)(2,1)S(1)} %collective-permute-done.1.refs_1_, bf16[128,512]{1,0:T(8,128)(2,1)S(1)} %collective-permute-done.2.refs_2_, ...), custom_call_target="tpu_custom_call" | custom-call | flops 402653184 | bytes 4194304 | tf_op jit(solution)/shard_map/far/pallas_call | solution.py:185
  39.8 0.8 %collective-permute-start.16 = (bf16[128,640]{1,0:T(8,128)(2,1)S(1)}, bf16[128,640]{1,0:T(8,128)(2,1)S(1)}, u32[]{:S(2)}, u32[]{:S(2)}) collective-permute-start(bf16[128,640]{1,0:T(8,128)(2,1)S(1)} %get-tuple-element.20), channel_id=1, source_target_pairs={{0,8},{4,12},{8,0},{12,4},{16,24},{20,28},{24,16},{28,20},{1,9},{5... | collective-permute-start | bytes 491528 | tf_op jit(solution)/shard_map/ppermute | solution.py:32
  40.6 0.1 pad_add_fusion.place_ref
  40.7 1.4 %own.1 = (f32[128,512]{1,0:T(8,128)S(1)}, f32[128,512]{1,0:T(8,128)S(1)}) custom-call(bf16[1024,512]{1,0:T(8,128)(2,1)S(1)} %get-tuple-element.16.keys_ref, bf16[1024,512]{1,0:T(8,128)(2,1)S(1)} %get-tuple-element.17.values_ref, bf16[256,512]{1,0:T(8,128)(2,1)S(1)} %get-tuple-element.13.refs_10_.queries_ref, ...), custom_call_target="tpu_custom_call" | custom-call | flops 268435456 | bytes 4194304 | tf_op jit(solution)/shard_map/own/pallas_call | solution.py:225
  42.1 0.0 copy-start.11
  42.1 0.1 copy-done.1
  42.3 0.1 copy-done.2
  42.4 0.0 copy-done.9
  42.4 0.4 copy-done.11
  42.8 1.4 %message.1.local_ref = f32[128,512]{1,0:T(8,128)S(1)} custom-call(s32[12]{0:T(128)S(1)} %bitcast.5, s32[2]{0:T(128)S(1)} %pad_add_fusion.place_ref, bf16[16,128,128]{2,1,0:T(8,128)(2,1)S(1)} %copy-done.2, bf16[128,512]{1,0:T(8,128)(2,1)S(1)} %copy-done.9, bf16[128,512]{1,0:T(8,128)(2,1)S(1)} %collective-permute-done.9.refs_1_, ...), custom_call_target="tpu_custom_call" | custom-call | flops 469762048 | bytes 4194304 | tf_op jit(solution)/shard_map/message/pallas_call | solution.py:258
  44.3 1.8 %collective-permute-done.16.packed_ref = bf16[128,640]{1,0:T(8,128)(2,1)S(1)} collective-permute-done((bf16[128,640]{1,0:T(8,128)(2,1)S(1)}, bf16[128,640]{1,0:T(8,128)(2,1)S(1)}, u32[]{:S(2)}, u32[]{:S(2)}) %collective-permute-start.16) | collective-permute-done | bytes 163872 | tf_op jit(solution)/shard_map/ppermute | solution.py:32
  46.1 0.7 %copy-done.10 = f32[512]{0:T(512)S(1)} copy-done((f32[512]{0:T(512)S(1)}, f32[512]{0:T(512)}, u32[]{:S(2)}) %copy-start.10) | copy-done | bytes 2072
  46.8 1.1 %finish.1 = bf16[128,512]{1,0:T(8,128)(2,1)} custom-call(f32[128,512]{1,0:T(8,128)S(1)} %get-tuple-element.18.numer_ref, f32[128,512]{1,0:T(8,128)S(1)} %get-tuple-element.19.denom_ref, bf16[128,640]{1,0:T(8,128)(2,1)S(1)} %collective-permute-done.16.packed_ref, bf16[512,512]{1,0:T(8,128)(2,1)S(1)} %copy-done.7, f32[1,512]{1,0:T(1,128)S(1)} %bitcast.4, ...), custom_call_target="tpu_custom_call" | custom-call | flops 67108864 | bytes 2097152 | tf_op jit(solution)/shard_map/finish/pallas_call | solution.py:286
  (28 shorter events, 0.1 us)
Async XLA Ops:
  0.0 8.4 %collective-permute-start.14 = (bf16[128,512]{1,0:T(8,128)(2,1)}, bf16[128,512]{1,0:T(8,128)(2,1)S(1)}, u32[]{:S(2)}, u32[]{:S(2)}) collective-permute-start(bf16[128,512]{1,0:T(8,128)(2,1)} %nodes_ref.1), channel_id=1, source_target_pairs={{0,6},{1,7},{2,4},{3,5},{4,2},{5,3},{6,0},{7,1},{8,14},{9,15},{10,... | collective-permute-start | bytes 393224 | tf_op jit(solution)/shard_map/ppermute | solution.py:42
  3.9 7.6 %collective-permute-start.12 = (bf16[128,512]{1,0:T(8,128)(2,1)}, bf16[128,512]{1,0:T(8,128)(2,1)S(1)}, u32[]{:S(2)}, u32[]{:S(2)}) collective-permute-start(bf16[128,512]{1,0:T(8,128)(2,1)} %nodes_ref.1), channel_id=1, source_target_pairs={{0,4},{4,0},{8,12},{12,8},{16,20},{20,16},{24,28},{28,24},{1,5},{5... | collective-permute-start | bytes 393224 | tf_op jit(solution)/shard_map/ppermute | solution.py:32
  4.4 10.6 %collective-permute-start.10 = (bf16[128,512]{1,0:T(8,128)(2,1)}, bf16[128,512]{1,0:T(8,128)(2,1)S(1)}, u32[]{:S(2)}, u32[]{:S(2)}) collective-permute-start(bf16[128,512]{1,0:T(8,128)(2,1)} %nodes_ref.1), channel_id=1, source_target_pairs={{0,2},{1,3},{2,0},{3,1},{4,6},{5,7},{6,4},{7,5},{8,10},{9,11},{10,... | collective-permute-start | bytes 393224 | tf_op jit(solution)/shard_map/ppermute | solution.py:32
  4.5 10.6 %collective-permute-start.9 = (bf16[128,512]{1,0:T(8,128)(2,1)}, bf16[128,512]{1,0:T(8,128)(2,1)S(1)}, u32[]{:S(2)}, u32[]{:S(2)}) collective-permute-start(bf16[128,512]{1,0:T(8,128)(2,1)} %nodes_ref.1), channel_id=1, source_target_pairs={{0,1},{1,0},{2,3},{3,2},{4,5},{5,4},{6,7},{7,6},{8,9},{9,8},{10,11... | collective-permute-start | bytes 393224 | tf_op jit(solution)/shard_map/ppermute | solution.py:32
  4.5 11.1 %collective-permute-start.8 = (bf16[128,512]{1,0:T(8,128)(2,1)}, bf16[128,512]{1,0:T(8,128)(2,1)S(1)}, u32[]{:S(2)}, u32[]{:S(2)}) collective-permute-start(bf16[128,512]{1,0:T(8,128)(2,1)} %nodes_ref.1), channel_id=1, source_target_pairs={{0,8},{4,12},{8,0},{12,4},{16,24},{20,28},{24,16},{28,20},{1,9},{5... | collective-permute-start | bytes 393224 | tf_op jit(solution)/shard_map/ppermute | solution.py:32
  8.4 8.8 %collective-permute-start = (bf16[128,512]{1,0:T(8,128)(2,1)}, bf16[128,512]{1,0:T(8,128)(2,1)S(1)}, u32[]{:S(2)}, u32[]{:S(2)}) collective-permute-start(bf16[128,512]{1,0:T(8,128)(2,1)} %nodes_ref.1), channel_id=1, source_target_pairs={{0,16},{4,20},{8,24},{12,28},{16,0},{20,4},{24,8},{28,12},{1,17},{... | collective-permute-start | bytes 393224 | tf_op jit(solution)/shard_map/ppermute | solution.py:32
  11.5 9.5 %collective-permute-start.19 = (bf16[128,512]{1,0:T(8,128)(2,1)S(1)}, bf16[128,512]{1,0:T(8,128)(2,1)S(1)}, u32[]{:S(2)}, u32[]{:S(2)}) collective-permute-start(bf16[128,512]{1,0:T(8,128)(2,1)S(1)} %collective-permute-done.14.refs_6_), channel_id=1, source_target_pairs={{0,8},{8,16},{16,24},{12,4},{20,12},{28,20},{1,9},{9,17},{17,25},{... | collective-permute-start | bytes 393224 | tf_op jit(solution)/shard_map/ppermute | solution.py:332
  15.0 6.0 %collective-permute-start.15 = (bf16[128,512]{1,0:T(8,128)(2,1)S(1)}, bf16[128,512]{1,0:T(8,128)(2,1)S(1)}, u32[]{:S(2)}, u32[]{:S(2)}) collective-permute-start(bf16[128,512]{1,0:T(8,128)(2,1)S(1)} %collective-permute-done.14.refs_6_), channel_id=1, source_target_pairs={{0,1},{1,0},{2,3},{3,2},{4,5},{5,4},{6,7},{7,6},{8,9},{9,8},{10,11... | collective-permute-start | bytes 393224 | tf_op jit(solution)/shard_map/ppermute | solution.py:32
  15.1 7.1 %collective-permute-start.13 = (bf16[128,512]{1,0:T(8,128)(2,1)S(1)}, bf16[128,512]{1,0:T(8,128)(2,1)S(1)}, u32[]{:S(2)}, u32[]{:S(2)}) collective-permute-start(bf16[128,512]{1,0:T(8,128)(2,1)S(1)} %collective-permute-done.12.refs_4_), channel_id=1, source_target_pairs={{0,1},{1,0},{2,3},{3,2},{4,5},{5,4},{6,7},{7,6},{8,9},{9,8},{10,11... | collective-permute-start | bytes 393224 | tf_op jit(solution)/shard_map/ppermute | solution.py:32
  15.6 10.0 %collective-permute-start.11 = (bf16[128,512]{1,0:T(8,128)(2,1)S(1)}, bf16[128,512]{1,0:T(8,128)(2,1)S(1)}, u32[]{:S(2)}, u32[]{:S(2)}) collective-permute-start(bf16[128,512]{1,0:T(8,128)(2,1)S(1)} %collective-permute-done.10.refs_2_), channel_id=1, source_target_pairs={{0,1},{1,0},{2,3},{3,2},{4,5},{5,4},{6,7},{7,6},{8,9},{9,8},{10,11... | collective-permute-start | bytes 393224 | tf_op jit(solution)/shard_map/ppermute | solution.py:32
  17.2 8.5 %collective-permute-start.6 = (bf16[128,512]{1,0:T(8,128)(2,1)S(1)}, bf16[128,512]{1,0:T(8,128)(2,1)S(1)}, u32[]{:S(2)}, u32[]{:S(2)}) collective-permute-start(bf16[128,512]{1,0:T(8,128)(2,1)S(1)} %collective-permute-done.refs_0_), channel_id=1, source_target_pairs={{0,6},{1,7},{2,4},{3,5},{4,2},{5,3},{6,0},{7,1},{8,14},{9,15},{10,... | collective-permute-start | bytes 393224 | tf_op jit(solution)/shard_map/ppermute | solution.py:42
  21.1 5.1 %collective-permute-start.4 = (bf16[128,512]{1,0:T(8,128)(2,1)S(1)}, bf16[128,512]{1,0:T(8,128)(2,1)S(1)}, u32[]{:S(2)}, u32[]{:S(2)}) collective-permute-start(bf16[128,512]{1,0:T(8,128)(2,1)S(1)} %collective-permute-done.refs_0_), channel_id=1, source_target_pairs={{0,4},{4,0},{8,12},{12,8},{16,20},{20,16},{24,28},{28,24},{1,5},{5... | collective-permute-start | bytes 393224 | tf_op jit(solution)/shard_map/ppermute | solution.py:32
  21.1 5.2 %collective-permute-start.2 = (bf16[128,512]{1,0:T(8,128)(2,1)S(1)}, bf16[128,512]{1,0:T(8,128)(2,1)S(1)}, u32[]{:S(2)}, u32[]{:S(2)}) collective-permute-start(bf16[128,512]{1,0:T(8,128)(2,1)S(1)} %collective-permute-done.refs_0_), channel_id=1, source_target_pairs={{0,2},{1,3},{2,0},{3,1},{4,6},{5,7},{6,4},{7,5},{8,10},{9,11},{10,... | collective-permute-start | bytes 393224 | tf_op jit(solution)/shard_map/ppermute | solution.py:32
  22.2 14.0 %collective-permute-start.17 = (bf16[128,512]{1,0:T(8,128)(2,1)S(1)}, bf16[128,512]{1,0:T(8,128)(2,1)S(1)}, u32[]{:S(2)}, u32[]{:S(2)}) collective-permute-start(bf16[128,512]{1,0:T(8,128)(2,1)S(1)} %collective-permute-done.12.refs_4_), channel_id=1, source_target_pairs={{0,8},{8,16},{16,24},{12,4},{20,12},{28,20},{1,9},{9,17},{17,25},{... | collective-permute-start | bytes 393224 | tf_op jit(solution)/shard_map/ppermute | solution.py:332
  25.6 10.8 %collective-permute-start.1 = (bf16[128,512]{1,0:T(8,128)(2,1)S(1)}, bf16[128,512]{1,0:T(8,128)(2,1)S(1)}, u32[]{:S(2)}, u32[]{:S(2)}) collective-permute-start(bf16[128,512]{1,0:T(8,128)(2,1)S(1)} %collective-permute-done.refs_0_), channel_id=1, source_target_pairs={{0,1},{1,0},{2,3},{3,2},{4,5},{5,4},{6,7},{7,6},{8,9},{9,8},{10,11... | collective-permute-start | bytes 393224 | tf_op jit(solution)/shard_map/ppermute | solution.py:32
  25.7 11.1 %collective-permute-start.7 = (bf16[128,512]{1,0:T(8,128)(2,1)S(1)}, bf16[128,512]{1,0:T(8,128)(2,1)S(1)}, u32[]{:S(2)}, u32[]{:S(2)}) collective-permute-start(bf16[128,512]{1,0:T(8,128)(2,1)S(1)} %collective-permute-done.6.refs_6_), channel_id=1, source_target_pairs={{0,1},{1,0},{2,3},{3,2},{4,5},{5,4},{6,7},{7,6},{8,9},{9,8},{10,11... | collective-permute-start | bytes 393224 | tf_op jit(solution)/shard_map/ppermute | solution.py:32
  26.2 10.7 %collective-permute-start.5 = (bf16[128,512]{1,0:T(8,128)(2,1)S(1)}, bf16[128,512]{1,0:T(8,128)(2,1)S(1)}, u32[]{:S(2)}, u32[]{:S(2)}) collective-permute-start(bf16[128,512]{1,0:T(8,128)(2,1)S(1)} %collective-permute-done.4.refs_4_), channel_id=1, source_target_pairs={{0,1},{1,0},{2,3},{3,2},{4,5},{5,4},{6,7},{7,6},{8,9},{9,8},{10,11... | collective-permute-start | bytes 393224 | tf_op jit(solution)/shard_map/ppermute | solution.py:32
  26.3 10.6 %collective-permute-start.3 = (bf16[128,512]{1,0:T(8,128)(2,1)S(1)}, bf16[128,512]{1,0:T(8,128)(2,1)S(1)}, u32[]{:S(2)}, u32[]{:S(2)}) collective-permute-start(bf16[128,512]{1,0:T(8,128)(2,1)S(1)} %collective-permute-done.2.refs_2_), channel_id=1, source_target_pairs={{0,1},{1,0},{2,3},{3,2},{4,5},{5,4},{6,7},{7,6},{8,9},{9,8},{10,11... | collective-permute-start | bytes 393224 | tf_op jit(solution)/shard_map/ppermute | solution.py:32
  26.7 0.7 %copy-start.13 = (f32[8]{0:T(128)S(1)}, f32[8]{0:T(128)}, u32[]{:S(2)}) copy-start(f32[8]{0:T(128)} %softness_ref.1) | copy-start | bytes 100
  27.4 1.0 %copy-start.3 = (bf16[512,512]{1,0:T(8,128)(2,1)S(1)}, bf16[512,512]{1,0:T(8,128)(2,1)}, u32[]{:S(2)}) copy-start(bf16[512,512]{1,0:T(8,128)(2,1)} %refs_8_.3) | copy-start | bytes 1572868
  28.4 1.0 %copy-start.5 = (bf16[512,512]{1,0:T(8,128)(2,1)S(1)}, bf16[512,512]{1,0:T(8,128)(2,1)}, u32[]{:S(2)}) copy-start(bf16[512,512]{1,0:T(8,128)(2,1)} %refs_9_.3) | copy-start | bytes 1572868
  29.4 0.9 %copy-start.8 = (bf16[128,512]{1,0:T(8,128)(2,1)S(1)}, bf16[128,512]{1,0:T(8,128)(2,1)}, u32[]{:S(2)}) copy-start(bf16[128,512]{1,0:T(8,128)(2,1)} %nodes_ref.1) | copy-start | bytes 393220
  30.4 1.0 %copy-start.12 = (bf16[512,512]{1,0:T(8,128)(2,1)S(1)}, bf16[512,512]{1,0:T(8,128)(2,1)}, u32[]{:S(2)}) copy-start(bf16[512,512]{1,0:T(8,128)(2,1)} %refs_8_.2) | copy-start | bytes 1572868
  31.4 5.5 %copy-start.4 = (bf16[512,512]{1,0:T(8,128)(2,1)S(1)}, bf16[512,512]{1,0:T(8,128)(2,1)}, u32[]{:S(2)}) copy-start(bf16[512,512]{1,0:T(8,128)(2,1)} %refs_8_.3) | copy-start | bytes 1572868
  31.4 5.5 %copy-start.6 = (bf16[512,512]{1,0:T(8,128)(2,1)S(1)}, bf16[512,512]{1,0:T(8,128)(2,1)}, u32[]{:S(2)}) copy-start(bf16[512,512]{1,0:T(8,128)(2,1)} %refs_9_.3) | copy-start | bytes 1572868
  36.3 5.9 %collective-permute-start.20 = (bf16[128,512]{1,0:T(8,128)(2,1)S(1)}, bf16[128,512]{1,0:T(8,128)(2,1)S(1)}, u32[]{:S(2)}, u32[]{:S(2)}) collective-permute-start(bf16[128,512]{1,0:T(8,128)(2,1)S(1)} %collective-permute-done.19.refs_10_), channel_id=1, source_target_pairs={{0,1},{1,0},{2,3},{3,2},{4,5},{5,4},{6,7},{7,6},{8,9},{9,8},{10,11... | collective-permute-start | bytes 393224 | tf_op jit(solution)/shard_map/ppermute | solution.py:32
  36.4 5.7 %collective-permute-start.18 = (bf16[128,512]{1,0:T(8,128)(2,1)S(1)}, bf16[128,512]{1,0:T(8,128)(2,1)S(1)}, u32[]{:S(2)}, u32[]{:S(2)}) collective-permute-start(bf16[128,512]{1,0:T(8,128)(2,1)S(1)} %collective-permute-done.17.refs_8_), channel_id=1, source_target_pairs={{0,1},{1,0},{2,3},{3,2},{4,5},{5,4},{6,7},{7,6},{8,9},{9,8},{10,11... | collective-permute-start | bytes 393224 | tf_op jit(solution)/shard_map/ppermute | solution.py:32
  39.8 6.3 %collective-permute-start.16 = (bf16[128,640]{1,0:T(8,128)(2,1)S(1)}, bf16[128,640]{1,0:T(8,128)(2,1)S(1)}, u32[]{:S(2)}, u32[]{:S(2)}) collective-permute-start(bf16[128,640]{1,0:T(8,128)(2,1)S(1)} %get-tuple-element.20), channel_id=1, source_target_pairs={{0,8},{4,12},{8,0},{12,4},{16,24},{20,28},{24,16},{28,20},{1,9},{5... | collective-permute-start | bytes 491528 | tf_op jit(solution)/shard_map/ppermute | solution.py:32
  40.7 1.4 %copy-start = (bf16[512,1024]{1,0:T(8,128)(2,1)S(1)}, bf16[512,1024]{1,0:T(8,128)(2,1)}, u32[]{:S(2)}) copy-start(bf16[512,1024]{1,0:T(8,128)(2,1)} %refs_12_.1) | copy-start | bytes 3145732
  40.7 1.5 %copy-start.1 = (bf16[1024,512]{1,0:T(8,128)(2,1)S(1)}, bf16[1024,512]{1,0:T(8,128)(2,1)}, u32[]{:S(2)}) copy-start(bf16[1024,512]{1,0:T(8,128)(2,1)} %refs_13_.1) | copy-start | bytes 3145732
  40.7 1.7 %copy-start.2 = (bf16[16,128,128]{2,1,0:T(8,128)(2,1)S(1)}, bf16[16,128,128]{2,1,0:T(8,128)(2,1)}, u32[]{:S(2)}) copy-start(bf16[16,128,128]{2,1,0:T(8,128)(2,1)} %tiles_ref.1) | copy-start | bytes 1572868
  40.7 1.7 %copy-start.9 = (bf16[128,512]{1,0:T(8,128)(2,1)S(1)}, bf16[128,512]{1,0:T(8,128)(2,1)}, u32[]{:S(2)}) copy-start(bf16[128,512]{1,0:T(8,128)(2,1)} %nodes_ref.1) | copy-start | bytes 393220
  42.1 0.7 %copy-start.11 = (s32[1,1,12]{2,1,0:T(1,128)S(1)}, s32[1,1,12]{2,1,0:T(1,128)}, u32[]{:S(2)}) copy-start(s32[1,1,12]{2,1,0:T(1,128)} %param.12) | copy-start | bytes 148
  42.8 3.3 %copy-start.7 = (bf16[512,512]{1,0:T(8,128)(2,1)S(1)}, bf16[512,512]{1,0:T(8,128)(2,1)}, u32[]{:S(2)}) copy-start(bf16[512,512]{1,0:T(8,128)(2,1)} %final_ref.1) | copy-start | bytes 1572868
  46.1 0.7 %copy-start.10 = (f32[512]{0:T(512)S(1)}, f32[512]{0:T(512)}, u32[]{:S(2)}) copy-start(f32[512]{0:T(512)} %param.21) | copy-start | bytes 6148

commit v2 on v1

--- a/solution.py
+++ b/solution.py
@@ -14,6 +14,7 @@
 norm_eps = 1e-06
 VMEM = pl.BlockSpec(memory_space=pltpu.VMEM)
 SMEM = pl.BlockSpec(memory_space=pltpu.SMEM)
+ANY = pl.BlockSpec(memory_space=pl.ANY)
 F32 = jnp.float32
 BF16 = jnp.bfloat16
 VMEM_LIMIT = 48 * 1024 * 1024
@@ -94,25 +95,55 @@
     values_ref[...] = dot(nodes, content_ref[...]).astype(BF16)
 
 
-def near_kernel(softness_ref, mine_ref, other_ref, *refs):
-    blocks, (asking_ref, lookup_ref, content_ref) = refs[:8], refs[8:11]
-    queries_ref, numer_ref, denom_ref, keys_ref, values_ref = refs[11:]
+def prep_kernel(*refs):
+    count = (len(refs) - 1) // 2
+    sources, targets, sems = refs[:count], refs[count:-1], refs[-1]
+    copies = [
+        pltpu.make_async_copy(source, target, sems.at[i])
+        for i, (source, target) in enumerate(zip(sources, targets))
+    ]
+    for copy in copies:
+        copy.start()
+    for copy in copies:
+        copy.wait()
+
+
+def prep(*arrays):
+    return pl.pallas_call(
+        prep_kernel,
+        out_shape=tuple(jax.ShapeDtypeStruct(a.shape, a.dtype) for a in arrays),
+        in_specs=[ANY] * len(arrays),
+        out_specs=(VMEM,) * len(arrays),
+        scratch_shapes=[pltpu.SemaphoreType.DMA((len(arrays),))],
+        compiler_params=params(),
+        cost_estimate=cost(0, 0, 9 << 20),
+        name="prep",
+    )(*arrays)
+
+
+def near_kernel(softness_ref, mine_ref, other_ref, twins_ref, *refs):
+    blocks, (asking_ref, lookup_ref, content_ref) = refs[:3], refs[3:6]
+    queries_ref, numer_ref, denom_ref, keys_ref, values_ref, temper, sem = refs[6:]
+    copy = pltpu.make_async_copy(softness_ref, temper, sem)
+    copy.start()
+    keys_values((mine_ref,) + blocks, lookup_ref, content_ref, keys_ref, values_ref)
+    rows = jnp.concatenate([twins_ref[...], mine_ref[...], other_ref[...]], axis=0)
+    projected = head_normed(dot(rows, asking_ref[...]))
+    copy.wait()
     width = asking_ref.shape[1]
     head = lax.broadcasted_iota(jnp.int32, (1, width), 1) // SUBSPACE_WIDTH
     scale = jnp.zeros((1, width), F32)
     for h in range(NUM_SUBSPACES):
-        scale = jnp.where(head == h, softness_ref[h], scale)
+        scale = jnp.where(head == h, temper[h], scale)
     scale = scale * (math.log2(math.e) / math.sqrt(SUBSPACE_WIDTH))
-    rows = jnp.concatenate([mine_ref[...], other_ref[...]], axis=0)
-    queries = (head_normed(dot(rows, asking_ref[...])) * scale).astype(BF16)
+    queries = (projected * scale).astype(BF16)
     queries_ref[...] = queries
-    keys_values(blocks, lookup_ref, content_ref, keys_ref, values_ref)
     numer_ref[...], denom_ref[...] = attend(queries, keys_ref, values_ref)
 
 
-def near(softness, mine, other, blocks, asking, lookup, content):
-    rows, width = 2 * mine.shape[0], mine.shape[1]
-    count = len(blocks) * mine.shape[0]
+def near(softness, mine, other, twins, blocks, asking, lookup, content):
+    rows, width = 4 * mine.shape[0], mine.shape[1]
+    count = 4 * mine.shape[0]
     return pl.pallas_call(
         near_kernel,
         out_shape=(
@@ -120,13 +151,14 @@
             jax.ShapeDtypeStruct((rows, width), F32),
             jax.ShapeDtypeStruct((rows, width), F32),
         ),
-        in_specs=[SMEM] + [VMEM] * 13,
+        in_specs=[ANY] + [VMEM] * 9,
         out_specs=(VMEM,) * 3,
-        scratch_shapes=[pltpu.VMEM((count, width), BF16)] * 2,
+        scratch_shapes=[pltpu.VMEM((count, width), BF16)] * 2
+        + [pltpu.SMEM(softness.shape, F32), pltpu.SemaphoreType.DMA],
         compiler_params=params(),
         cost_estimate=cost(8 * rows * count * width, rows * count * NUM_SUBSPACES, 4 << 20),
         name="near",
-    )(softness, mine, other, *blocks, asking, lookup, content)
+    )(softness, mine, other, twins, *blocks, asking, lookup, content)
 
 
 def packing(width, wide):
@@ -155,18 +187,18 @@
 
 
 def far_kernel(*refs):
-    blocks, (lookup_ref, content_ref, queries_ref, numer_ref, denom_ref) = refs[:8], refs[8:13]
-    keys_ref, values_ref, packed_ref, numer_sum, denom_sum = refs[13:]
+    blocks, (lookup_ref, content_ref, queries_ref, numer_ref, denom_ref) = refs[:4], refs[4:9]
+    keys_ref, values_ref, packed_ref, numer_sum, denom_sum = refs[9:]
+    half = queries_ref.shape[0] // 2
     step = pl.program_id(0)
-    half = queries_ref.shape[0] // 2
 
     @pl.when(step == 0)
     def _():
-        numer_sum[...] = numer_ref[half:, :]
-        denom_sum[...] = denom_ref[half:, :]
+        numer_sum[...] = numer_ref[:half, :]
+        denom_sum[...] = denom_ref[:half, :]
 
     keys_values(blocks, lookup_ref, content_ref, keys_ref, values_ref)
-    numer, denom = attend(queries_ref[half:, :], keys_ref, values_ref)
+    numer, denom = attend(queries_ref[:half, :], keys_ref, values_ref)
     numer_sum[...] += numer
     denom_sum[...] += denom
 
@@ -190,7 +222,7 @@
             jax.ShapeDtypeStruct((steps * count, width), BF16),
             jax.ShapeDtypeStruct((half, width + LANES), BF16),
         ),
-        in_specs=[part(block_len)] * 8
+        in_specs=[part(block_len)] * 4
         + [whole((width, width))] * 2
         + [whole((rows, width))] * 3,
         out_specs=(part(count), part(count), whole((half, width + LANES))),
@@ -203,27 +235,27 @@
     )(*blocks, lookup, content, queries, numer, denom)
 
 
-def own_kernel(keys_ref, values_ref, queries_ref, numer_ref, denom_ref, numer_out, denom_out):
+def rest_kernel(keys_ref, values_ref, queries_ref, numer_ref, denom_ref, numer_out, denom_out):
     half = queries_ref.shape[0] // 2
 
     @pl.when(pl.program_id(0) == 0)
     def _():
-        numer_out[...] = numer_ref[:half, :]
-        denom_out[...] = denom_ref[:half, :]
-
-    numer, denom = attend(queries_ref[:half, :], keys_ref, values_ref)
+        numer_out[...] = numer_ref[half:, :]
+        denom_out[...] = denom_ref[half:, :]
+
+    numer, denom = attend(queries_ref[half:, :], keys_ref, values_ref)
     numer_out[...] += numer
     denom_out[...] += denom
 
 
-def own(keys, values, count, queries, numer, denom):
+def rest(keys, values, count, queries, numer, denom):
     steps = keys.shape[0] // count
     rows, width = queries.shape
     half = rows // 2
     whole = lambda shape: pl.BlockSpec(shape, lambda i: (0, 0))
     part = lambda size: pl.BlockSpec((size, width), lambda i: (i, 0))
     return pl.pallas_call(
-        own_kernel,
+        rest_kernel,
         grid=(steps,),
         out_shape=(jax.ShapeDtypeStruct((half, width), F32),) * 2,
         in_specs=[part(count)] * 2 + [whole((rows, width))] * 3,
@@ -232,18 +264,49 @@
         cost_estimate=cost(
             4 * half * steps * count * width, half * steps * count * NUM_SUBSPACES, 4 << 20
         ),
-        name="own",
+        name="rest",
     )(keys, values, queries, numer, denom)
 
 
+def combine_kernel(numer_ref, denom_ref, packed_ref, numer_out, denom_out, packed_out):
+    rows, width = numer_out.shape
+    numer = numer_ref[...] + packed_ref[:, :width].astype(F32)
+    denom = denom_ref[...] + unpack_denom(packed_ref[:, width:], width)
+    numer_out[...] = numer[:rows]
+    denom_out[...] = denom[:rows]
+    packed_out[...] = pack(numer[rows:], denom[rows:])
+
+
+def combine(numer, denom, packed):
+    rows, width = numer.shape[0] // 2, numer.shape[1]
+    return pl.pallas_call(
+        combine_kernel,
+        out_shape=(
+            jax.ShapeDtypeStruct((rows, width), F32),
+            jax.ShapeDtypeStruct((rows, width), F32),
+            jax.ShapeDtypeStruct((rows, width + LANES), BF16),
+        ),
+        in_specs=[VMEM] * 3,
+        out_specs=(VMEM,) * 3,
+        compiler_params=params(),
+        cost_estimate=cost(4 * rows * width * LANES, 0, 1 << 20),
+        name="combine",
+    )(numer, denom, packed)
+
+
 def message_kernel(slots_ref, place_ref, tiles_ref, *refs):
-    blocks, (inner_ref, outer_ref, local_ref) = refs[:12], refs[12:]
+    blocks, (inner_ref, outer_ref, local_ref, slots, sem) = refs[:7], refs[7:]
+    copy = pltpu.make_async_copy(slots_ref, slots, sem)
+    copy.start()
     group = slots_ref.shape[0] // 3
     me, odd = place_ref[0], place_ref[1]
-    sides = (1, 2 - 2 * odd, 2 * odd)
+    beside, beyond = 2 - 2 * odd, 2 * odd
+    order = [(1, 0), (1, 1), (1, 2), (beside, 0), (beside, 2), (beyond, 0), (beyond, 2)]
+    order += [(1, 3), (beside, 1), (beside, 3), (beyond, 1), (beyond, 3)]
+    copy.wait()
     tiles = []
-    for i in range(12):
-        tile_id = slots_ref[sides[i // 4] * group + (me ^ (i % 4))]
+    for side, offset in order:
+        tile_id = slots[side * group + (me ^ offset)]
         tile = tiles_ref[jnp.maximum(tile_id, 0)]
         tiles.append(jnp.where(tile_id >= 0, tile, jnp.zeros_like(tile)))
     nodes = jnp.concatenate([block[...] for block in blocks], axis=0)
@@ -258,8 +321,9 @@
     return pl.pallas_call(
         message_kernel,
         out_shape=jax.ShapeDtypeStruct((rows, width), F32),
-        in_specs=[SMEM, SMEM] + [VMEM] * 15,
+        in_specs=[ANY, SMEM] + [VMEM] * 10,
         out_specs=VMEM,
+        scratch_shapes=[pltpu.SMEM(slots.shape, jnp.int32), pltpu.SemaphoreType.DMA],
         compiler_params=params(),
         cost_estimate=cost(
             2 * rows * width * (12 * rows + 2 * hidden), rows * hidden, 4 << 20
@@ -310,69 +374,67 @@
     block_len = vertex_embeddings.shape[0]
     doms = lax.axis_size("dom")
     nodes = vertex_embeddings
-
-    distant = nodes[:0]
-    mask = 4
+    stacked = lambda *arrays: jnp.concatenate(arrays, axis=0)
+
+    distant = swap(nodes, "dom", 4)
+    mask = 8
     while mask < doms:
-        held = jnp.concatenate([nodes, distant], axis=0) if mask > 4 else nodes
-        arrived = swap(held, "dom", mask)
-        distant = jnp.concatenate([distant, arrived], axis=0) if mask > 4 else arrived
+        distant = stacked(distant, swap(stacked(nodes, distant), "dom", mask))
         mask *= 2
 
     def plane(block):
         side = swap(block, "dom", 1)
         below = swap(block, "head", 2)
         across = swap_both(block, 1, 2)
-        return block, below, side, across
-
-    others = swap(nodes, "dom", 2)
+        return below, side, across
+
     near_blocks = plane(nodes)
-    near_twins = [swap(block, "head", 1) for block in near_blocks]
-    pairs = [(p, p + 2) for p in range(0, doms - 2, 2)] + [(p, p - 2) for p in range(3, doms, 2)]
-    halo = [lax.ppermute(block, "dom", pairs) for block in near_blocks[2:]]
-    halo_twins = [swap(block, "head", 1) for block in halo]
-    far_blocks = plane(distant)
-    far_twins = [swap(block, "head", 1) for block in far_blocks]
-
-    interleave = lambda a, b: [block for both in zip(a, b) for block in both]
-    queries, numer, denom = near(
-        softness_per_subspace,
-        nodes,
-        others,
-        interleave(near_blocks, near_twins),
+    other = swap(nodes, "dom", 2)
+    twins = swap(stacked(nodes, other), "head", 1)
+    far_blocks = (distant,) + plane(distant)
+
+    (
+        asking,
+        lookup,
+        content,
+        final,
+        inner,
+        outer,
+        tiles,
+        gain,
+    ) = prep(
         asking_projector,
         lookup_projector,
         content_projector,
+        final_projector,
+        passing_inner_coefficients,
+        passing_outer_coefficients,
+        coupling_strength_panels,
+        mixing_layer_gain.reshape(1, -1),
     )
+    queries, numer, denom = near(
+        softness_per_subspace, nodes, other, twins, near_blocks, asking, lookup, content
+    )
+
+    below, side, across = near_blocks
+    pairs = [(p, p + 2) for p in range(0, doms - 2, 2)] + [(p, p - 2) for p in range(3, doms, 2)]
+    halo = lax.ppermute(stacked(side, across), "dom", pairs)
+    halo_twins = swap(stacked(below, side, across, halo), "head", 1)
     place = jnp.stack([lax.axis_index("head"), lax.axis_index("dom") % 2]).astype(jnp.int32)
     local = message(
         adjacent_group_bank_ids.reshape(-1),
         place,
-        coupling_strength_panels,
-        interleave(near_blocks, near_twins) + interleave(halo, halo_twins),
-        passing_inner_coefficients,
-        passing_outer_coefficients,
+        tiles,
+        (nodes, twins[:block_len], below, side, across, halo, halo_twins),
+        inner,
+        outer,
     )
-    keys, values, packed = far(
-        interleave(far_blocks, far_twins),
-        block_len,
-        lookup_projector,
-        content_projector,
-        queries,
-        numer,
-        denom,
-    )
+    keys, values, packed = far(far_blocks, block_len, lookup, content, queries, numer, denom)
+    packed = swap(packed, "head", 1)
+    numer, denom = rest(keys, values, 4 * block_len, queries, numer, denom)
+    numer, denom, packed = combine(numer, denom, packed)
     packed = swap(packed, "dom", 2)
-    numer, denom = own(keys, values, 8 * block_len, queries, numer, denom)
-    return finish(
-        numer,
-        denom,
-        packed,
-        final_projector,
-        mixing_layer_gain.reshape(1, -1),
-        local,
-        nodes,
-    )
+    return finish(numer, denom, packed, final, gain, local, nodes)
 
 
 def solution(mesh):

time: 48.3 us -> 53.3 us (1.10)
  waiting for transfers between devices: 5.27 us -> 13.4 us
  starting transfers between devices: 24.6 us -> 17.1 us
  Pallas kernels: 11.7 us -> 15.7 us
  other arithmetic: 0.07 us -> 1.93 us
  local copies, waits for them, and re-layouts: 6.08 us -> 4.45 us
    ppermute x17 -> x10, waiting for transfers between devices: 3.36 us -> 9.9 us  [swap(): return lax.ppermute(array, axis, [(i, i ^ mask) for i in range(devices)])]
    ppermute x2, starting transfers between devices: 7.75 us -> 2.45 us  [swap_both(): return lax.ppermute(array, ('dom', 'head'), pairs)]
    pallas_call x1 -> x3, Pallas kernels: 1.36 us -> 5.61 us  [the longest x1 3.11 us: prep(): pl.pallas_call(prep_kernel, out_shape=tuple((jax.ShapeDtypeStruct(a.shape...]
    ppermute x2 -> x1, starting transfers between devices: 6.86 us -> 3.63 us  [shards(): halo = lax.ppermute(stacked(side, across), 'dom', pairs)]
    unnamed x28 -> x40, local copies, waits for them, and re-layouts: 6.08 us -> 3.54 us
    concatenate x0 -> x3, other arithmetic: none -> 1.86 us  [shards(): stacked = lambda *arrays: jnp.concatenate(arrays, axis=0)]
    ppermute x2, waiting for transfers between devices: 1.91 us -> 3.5 us  [swap_both(): return lax.ppermute(array, ('dom', 'head'), pairs)]
    pallas_call x1, Pallas kernels: 4.84 us -> 3.75 us  [near(): pl.pallas_call(near_kernel, out_shape=(jax.ShapeDtypeStruct((rows, width)...]
  transfers between devices with their start and end apart: 21 -> 13, of which waited for: 3 -> 6; matrix products, arithmetic and copies ran while one was open for 0% -> 5% of each run, Pallas kernels for 22% -> 26%
where the time goes in v2:
time: 53.3 us; the launch traced here: 53 us
  starting transfers between devices  17.1 us (32%)
  Pallas kernels  15.7 us (29%)
  waiting for transfers between devices  13.4 us (25%)
  local copies, waits for them, and re-layouts  4.45 us (8%)
  other arithmetic  1.93 us (4%)
    ppermute x10, starting transfers between devices, swap(): return lax.ppermute(array, axis, [(i, i ^ mask) for i in range(devices)])  11 us
    ppermute x10, waiting for transfers between devices, swap(): return lax.ppermute(array, axis, [(i, i ^ mask) for i in range(devices)])  9.9 us
    pallas_call x1, Pallas kernels, near(): pl.pallas_call(near_kernel, out_shape=(jax.ShapeDtypeStruct((rows, width)...  3.75 us
    ppermute x1, starting transfers between devices, shards(): halo = lax.ppermute(stacked(side, across), 'dom', pairs)  3.63 us
    unnamed x40, local copies, waits for them, and re-layouts  3.54 us
    ppermute x2, waiting for transfers between devices, swap_both(): return lax.ppermute(array, ('dom', 'head'), pairs)  3.5 us
    pallas_call x1, Pallas kernels, prep(): pl.pallas_call(prep_kernel, out_shape=tuple((jax.ShapeDtypeStruct(a.shape...  3.11 us
    ppermute x2, starting transfers between devices, swap_both(): return lax.ppermute(array, ('dom', 'head'), pairs)  2.45 us
  transfers between devices with their start and end apart: 13, of which 6 were waited for; matrix products, arithmetic and copies ran while one was open for 5% of the time, Pallas kernels for 26%

profile of v2, /device:TPU:0, one launch (start us, length us, event | category | flops | bytes accessed | tf_op | source)
XLA Modules:
  0.0 53.0 jit_solution(16778242955399061535)
XLA Ops:
  0.0 2.9 %collective-permute-start.7 = (bf16[128,512]{1,0:T(8,128)(2,1)}, bf16[128,512]{1,0:T(8,128)(2,1)S(1)}, u32[]{:S(2)}, u32[]{:S(2)}) collective-permute-start(bf16[128,512]{1,0:T(8,128)(2,1)} %nodes_ref.1), channel_id=1, source_target_pairs={{0,4},{4,0},{8,12},{12,8},{16,20},{20,16},{24,28},{28,24},{1,5},{5... | collective-permute-start | bytes 393224 | tf_op jit(solution)/shard_map/ppermute | solution.py:33
  2.9 1.5 %collective-permute-start.8 = (bf16[128,512]{1,0:T(8,128)(2,1)}, bf16[128,512]{1,0:T(8,128)(2,1)S(1)}, u32[]{:S(2)}, u32[]{:S(2)}) collective-permute-start(bf16[128,512]{1,0:T(8,128)(2,1)} %nodes_ref.1), channel_id=1, source_target_pairs={{0,6},{1,7},{2,4},{3,5},{4,2},{5,3},{6,0},{7,1},{8,14},{9,15},{10,... | collective-permute-start | bytes 393224 | tf_op jit(solution)/shard_map/ppermute | solution.py:43
  4.4 1.6 %collective-permute-start.4 = (bf16[128,512]{1,0:T(8,128)(2,1)}, bf16[128,512]{1,0:T(8,128)(2,1)S(1)}, u32[]{:S(2)}, u32[]{:S(2)}) collective-permute-start(bf16[128,512]{1,0:T(8,128)(2,1)} %nodes_ref.1), channel_id=1, source_target_pairs={{0,8},{4,12},{8,0},{12,4},{16,24},{20,28},{24,16},{28,20},{1,9},{5... | collective-permute-start | bytes 393224 | tf_op jit(solution)/shard_map/ppermute | solution.py:33
  6.0 1.1 %collective-permute-done.7.refs_1_.refs_3_ = bf16[128,512]{1,0:T(8,128)(2,1)S(1)} collective-permute-done((bf16[128,512]{1,0:T(8,128)(2,1)}, bf16[128,512]{1,0:T(8,128)(2,1)S(1)}, u32[]{:S(2)}, u32[]{:S(2)}) %collective-permute-start.7) | collective-permute-done | bytes 131104 | tf_op jit(solution)/shard_map/ppermute | solution.py:33
  7.2 3.5 %collective-permute-done.8.refs_2_.refs_4_ = bf16[128,512]{1,0:T(8,128)(2,1)S(1)} collective-permute-done((bf16[128,512]{1,0:T(8,128)(2,1)}, bf16[128,512]{1,0:T(8,128)(2,1)S(1)}, u32[]{:S(2)}, u32[]{:S(2)}) %collective-permute-start.8) | collective-permute-done | bytes 131104 | tf_op jit(solution)/shard_map/ppermute | solution.py:43
  10.7 0.0 copy-start.3
  10.7 0.0 copy-start.4
  10.7 0.0 copy-start.5
  10.7 0.0 copy-start.17
  10.7 3.6 %collective-permute-start.11 = (bf16[256,512]{1,0:T(8,128)(2,1)S(1)}, bf16[256,512]{1,0:T(8,128)(2,1)S(1)}, u32[]{:S(2)}, u32[]{:S(2)}) collective-permute-start(bf16[256,512]{1,0:T(8,128)(2,1)S(1)} %pad_maximum_fusion.2), channel_id=1, source_target_pairs={{0,8},{8,16},{16,24},{12,4},{20,12},{28,20},{1,9},{9,17},{17,25},{... | collective-permute-start | bytes 786440 | tf_op jit(solution)/shard_map/ppermute | solution.py:421
  14.4 0.6 %collective-permute-start.6 = (bf16[128,512]{1,0:T(8,128)(2,1)}, bf16[128,512]{1,0:T(8,128)(2,1)S(1)}, u32[]{:S(2)}, u32[]{:S(2)}) collective-permute-start(bf16[128,512]{1,0:T(8,128)(2,1)} %nodes_ref.1), channel_id=1, source_target_pairs={{0,2},{1,3},{2,0},{3,1},{4,6},{5,7},{6,4},{7,5},{8,10},{9,11},{10,... | collective-permute-start | bytes 393224 | tf_op jit(solution)/shard_map/ppermute | solution.py:33
  14.9 0.0 collective-permute-done.4.other_ref
  14.9 1.0 %pad_maximum_fusion.1 = bf16[256,512]{1,0:T(8,128)(2,1)S(1)} fusion(bf16[128,512]{1,0:T(8,128)(2,1)S(1)} %collective-permute-done.4.other_ref, bf16[128,512]{1,0:T(8,128)(2,1)} %nodes_ref.1), kind=kLoop, calls=%fused_computation.1 | loop fusion | flops 524288 | bytes 524288 | tf_op jit(solution)/shard_map/concatenate | solution.py:377
  15.9 0.1 collective-permute-start.5
  16.0 2.6 %collective-permute-start = (bf16[128,512]{1,0:T(8,128)(2,1)S(1)}, bf16[128,512]{1,0:T(8,128)(2,1)S(1)}, u32[]{:S(2)}, u32[]{:S(2)}) collective-permute-start(bf16[128,512]{1,0:T(8,128)(2,1)S(1)} %copy-done), channel_id=1, source_target_pairs={{0,16},{4,20},{8,24},{12,28},{16,0},{20,4},{24,8},{28,12},{1,17},{... | collective-permute-start | bytes 393224 | tf_op jit(solution)/shard_map/ppermute | solution.py:33
  18.6 1.0 %collective-permute-done.6.refs_0_.refs_2_ = bf16[128,512]{1,0:T(8,128)(2,1)S(1)} collective-permute-done((bf16[128,512]{1,0:T(8,128)(2,1)}, bf16[128,512]{1,0:T(8,128)(2,1)S(1)}, u32[]{:S(2)}, u32[]{:S(2)}) %collective-permute-start.6) | collective-permute-done | bytes 131104 | tf_op jit(solution)/shard_map/ppermute | solution.py:33
  19.6 0.0 collective-permute-done.11.refs_5_
  19.6 0.9 %pad_maximum_fusion = bf16[640,512]{1,0:T(8,128)(2,1)} fusion(bf16[256,512]{1,0:T(8,128)(2,1)S(1)} %collective-permute-done.11.refs_5_, bf16[128,512]{1,0:T(8,128)(2,1)S(1)} %collective-permute-done.8.refs_2_.refs_4_, bf16[128,512]{1,0:T(8,128)(2,1)S(1)} %collective-permute-done.7.refs_1_.refs_3_, bf16[128,512]{1,0:T(8,128)(2,1)S(1)} %collective-permute-done.6.refs_0_.refs_2_), kind=kLoop, calls=%fused_computation | loop fusion | flops 2621440 | bytes 1310720 | tf_op jit(solution)/shard_map/concatenate | solution.py:377
  20.5 0.0 collective-permute-start.12
  20.5 5.1 %collective-permute-done.refs_0_ = bf16[128,512]{1,0:T(8,128)(2,1)S(1)} collective-permute-done((bf16[128,512]{1,0:T(8,128)(2,1)S(1)}, bf16[128,512]{1,0:T(8,128)(2,1)S(1)}, u32[]{:S(2)}, u32[]{:S(2)}) %collective-permute-start) | collective-permute-done | bytes 131104 | tf_op jit(solution)/shard_map/ppermute | solution.py:33
  25.6 1.5 %collective-permute-start.1 = (bf16[128,512]{1,0:T(8,128)(2,1)S(1)}, bf16[128,512]{1,0:T(8,128)(2,1)S(1)}, u32[]{:S(2)}, u32[]{:S(2)}) collective-permute-start(bf16[128,512]{1,0:T(8,128)(2,1)S(1)} %collective-permute-done.refs_0_), channel_id=1, source_target_pairs={{0,2},{1,3},{2,0},{3,1},{4,6},{5,7},{6,4},{7,5},{8,10},{9,11},{10,... | collective-permute-start | bytes 393224 | tf_op jit(solution)/shard_map/ppermute | solution.py:33
  27.1 1.4 %collective-permute-start.2 = (bf16[128,512]{1,0:T(8,128)(2,1)S(1)}, bf16[128,512]{1,0:T(8,128)(2,1)S(1)}, u32[]{:S(2)}, u32[]{:S(2)}) collective-permute-start(bf16[128,512]{1,0:T(8,128)(2,1)S(1)} %collective-permute-done.refs_0_), channel_id=1, source_target_pairs={{0,4},{4,0},{8,12},{12,8},{16,20},{20,16},{24,28},{28,24},{1,5},{5... | collective-permute-start | bytes 393224 | tf_op jit(solution)/shard_map/ppermute | solution.py:33
  28.6 1.0 %collective-permute-start.3 = (bf16[128,512]{1,0:T(8,128)(2,1)S(1)}, bf16[128,512]{1,0:T(8,128)(2,1)S(1)}, u32[]{:S(2)}, u32[]{:S(2)}) collective-permute-start(bf16[128,512]{1,0:T(8,128)(2,1)S(1)} %collective-permute-done.refs_0_), channel_id=1, source_target_pairs={{0,6},{1,7},{2,4},{3,5},{4,2},{5,3},{6,0},{7,1},{8,14},{9,15},{10,... | collective-permute-start | bytes 393224 | tf_op jit(solution)/shard_map/ppermute | solution.py:43
  29.5 0.0 copy-start.7
  29.6 1.0 %copy-done.7 = bf16[16,128,128]{2,1,0:T(8,128)(2,1)S(1)} copy-done((bf16[16,128,128]{2,1,0:T(8,128)(2,1)S(1)}, bf16[16,128,128]{2,1,0:T(8,128)(2,1)}, u32[]{:S(2)}) %copy-start.7) | copy-done | bytes 524312
  30.6 3.1 %prep.1 = (bf16[512,512]{1,0:T(8,128)(2,1)S(1)}, bf16[512,512]{1,0:T(8,128)(2,1)S(1)}, bf16[512,512]{1,0:T(8,128)(2,1)S(1)}, bf16[512,512]{1,0:T(8,128)(2,1)S(1)...) custom-call(bf16[512,512]{1,0:T(8,128)(2,1)S(1)} %copy-done.3, ...), custom_call_target="tpu_custom_call" | custom-call | bytes 9437184 | tf_op jit(solution)/shard_map/prep/pallas_call | solution.py:112
  33.7 0.0 copy-start.8
  33.7 0.0 collective-permute-done.5.twins_ref
  33.8 3.7 %near.1 = (bf16[512,512]{1,0:T(8,128)(2,1)S(1)}, f32[512,512]{1,0:T(8,128)S(1)}, f32[512,512]{1,0:T(8,128)S(1)}) custom-call(f32[8]{0:T(128)S(1)} %copy-done.19, bf16[128,512]{1,0:T(8,128)(2,1)S(1)} %copy-done, bf16[128,512]{1,0:T(8,128)(2,1)S(1)} %collective-permute-done.4.other_ref, bf16[256,512]{1,0:T(8,128)(2,1)S(1)} %collective-permute-done.5.twins_ref, ...), custom_call_target="tpu_custom_call" | custom-call | flops 1073741824 | bytes 4194304 | tf_op jit(solution)/shard_map/near/pallas_call | solution.py:147
  37.5 0.0 collective-permute-done.1.refs_1_
  37.6 0.0 collective-permute-done.2.refs_2_
  37.6 0.0 collective-permute-done.3.refs_3_
  37.6 2.4 %far.1 = (bf16[512,512]{1,0:T(8,128)(2,1)S(1)}, bf16[512,512]{1,0:T(8,128)(2,1)S(1)}, bf16[256,640]{1,0:T(8,128)(2,1)S(1)}) custom-call(bf16[128,512]{1,0:T(8,128)(2,1)S(1)} %collective-permute-done.refs_0_, bf16[128,512]{1,0:T(8,128)(2,1)S(1)} %collective-permute-done.1.refs_1_, bf16[128,512]{1,0:T(8,128)(2,1)S(1)} %collective-permute-done.2.refs_2_, ...), custom_call_target="tpu_custom_call" | custom-call | flops 402653184 | bytes 4194304 | tf_op jit(solution)/shard_map/far/pallas_call | solution.py:217
  40.0 0.1 collective-permute-start.9
  40.0 1.4 %rest.1 = (f32[256,512]{1,0:T(8,128)S(1)}, f32[256,512]{1,0:T(8,128)S(1)}) custom-call(bf16[512,512]{1,0:T(8,128)(2,1)S(1)} %get-tuple-element.30.keys_ref, bf16[512,512]{1,0:T(8,128)(2,1)S(1)} %get-tuple-element.31.values_ref, bf16[512,512]{1,0:T(8,128)(2,1)S(1)} %get-tuple-element.27.refs_6_.queries_ref, ...), custom_call_target="tpu_custom_call" | custom-call | flops 268435456 | bytes 4194304 | tf_op jit(solution)/shard_map/rest/pallas_call | solution.py:257
  41.4 0.0 copy-start.18
  41.4 0.2 collective-permute-done.9.packed_ref
  41.6 1.1 %combine.1 = (f32[128,512]{1,0:T(8,128)S(1)}, f32[128,512]{1,0:T(8,128)S(1)}, bf16[128,640]{1,0:T(8,128)(2,1)}) custom-call(f32[256,512]{1,0:T(8,128)S(1)} %get-tuple-element.32.numer_ref, f32[256,512]{1,0:T(8,128)S(1)} %get-tuple-element.33.denom_ref, bf16[256,640]{1,0:T(8,128)(2,1)S(1)} %collective-permute-done.9.packed_ref), custom_call_target="tpu_custom_call" | custom-call | flops 33554432 | bytes 1048576 | tf_op jit(solution)/shard_map/combine/pallas_call | solution.py:282
  42.8 0.7 %copy-done.12 = f32[128,512]{1,0:T(8,128)} copy-done((f32[128,512]{1,0:T(8,128)}, f32[128,512]{1,0:T(8,128)S(1)}, u32[]{:S(2)}) %copy-start.12) | copy-done | bytes 262168
  43.5 0.7 %copy-done.14 = f32[128,512]{1,0:T(8,128)} copy-done((f32[128,512]{1,0:T(8,128)}, f32[128,512]{1,0:T(8,128)S(1)}, u32[]{:S(2)}) %copy-start.14) | copy-done | bytes 262168
  44.2 0.2 collective-permute-start.10
  44.4 0.1 pad_add_fusion.place_ref
  44.5 0.9 %slice.4.refs_1_ = bf16[128,512]{1,0:T(8,128)(2,1)S(1)} slice(bf16[256,512]{1,0:T(8,128)(2,1)} %copy-done.16), slice={[0:128], [0:512]} | slice | bytes 262144 | tf_op jit(solution)/shard_map/slice | solution.py:428
  45.4 0.0 collective-permute-done.12.refs_6_
  45.4 1.0 %copy-done.9 = bf16[16,128,128]{2,1,0:T(8,128)(2,1)S(1)} copy-done((bf16[16,128,128]{2,1,0:T(8,128)(2,1)S(1)}, bf16[16,128,128]{2,1,0:T(8,128)(2,1)}, u32[]{:S(2)}) %copy-start.9) | copy-done | bytes 524312
  46.5 2.0 %message.1.local_ref = f32[128,512]{1,0:T(8,128)S(1)} custom-call(s32[12]{0:T(128)S(1)} %bitcast.5, s32[2]{0:T(128)S(1)} %pad_add_fusion.place_ref, bf16[16,128,128]{2,1,0:T(8,128)(2,1)S(1)} %copy-done.9, bf16[128,512]{1,0:T(8,128)(2,1)S(1)} %copy-done, bf16[128,512]{1,0:T(8,128)(2,1)S(1)} %slice.4.refs_1_, ...), custom_call_target="tpu_custom_call" | custom-call | flops 469762048 | bytes 4194304 | tf_op jit(solution)/shard_map/message/pallas_call | solution.py:321
  48.4 2.5 %collective-permute-done.10.packed_ref = bf16[128,640]{1,0:T(8,128)(2,1)} collective-permute-done((bf16[128,640]{1,0:T(8,128)(2,1)}, bf16[128,640]{1,0:T(8,128)(2,1)}, u32[]{:S(2)}, u32[]{:S(2)}) %collective-permute-start.10) | collective-permute-done | bytes 163872 | tf_op jit(solution)/shard_map/ppermute | solution.py:33
  50.9 2.0 %finish.1 = bf16[128,512]{1,0:T(8,128)(2,1)} custom-call(f32[128,512]{1,0:T(8,128)S(1)} %copy-done.13, f32[128,512]{1,0:T(8,128)S(1)} %copy-done.15, bf16[128,640]{1,0:T(8,128)(2,1)} %collective-permute-done.10.packed_ref, bf16[512,512]{1,0:T(8,128)(2,1)S(1)} %copy-done.11, f32[1,512]{1,0:T(1,128)S(1)} %get-tuple-element.39.gain_ref, ...), custom_call_target="tpu_custom_call" | custom-call | flops 67108864 | bytes 2097152 | tf_op jit(solution)/shard_map/finish/pallas_call | solution.py:350
  (30 shorter events, 0.1 us)
Async XLA Ops:
  0.0 16.0 %copy-start = (bf16[128,512]{1,0:T(8,128)(2,1)S(1)}, bf16[128,512]{1,0:T(8,128)(2,1)}, u32[]{:S(2)}) copy-start(bf16[128,512]{1,0:T(8,128)(2,1)} %nodes_ref.1) | copy-start | bytes 393220
  0.0 7.2 %collective-permute-start.7 = (bf16[128,512]{1,0:T(8,128)(2,1)}, bf16[128,512]{1,0:T(8,128)(2,1)S(1)}, u32[]{:S(2)}, u32[]{:S(2)}) collective-permute-start(bf16[128,512]{1,0:T(8,128)(2,1)} %nodes_ref.1), channel_id=1, source_target_pairs={{0,4},{4,0},{8,12},{12,8},{16,20},{20,16},{24,28},{28,24},{1,5},{5... | collective-permute-start | bytes 393224 | tf_op jit(solution)/shard_map/ppermute | solution.py:33
  2.9 7.7 %collective-permute-start.8 = (bf16[128,512]{1,0:T(8,128)(2,1)}, bf16[128,512]{1,0:T(8,128)(2,1)S(1)}, u32[]{:S(2)}, u32[]{:S(2)}) collective-permute-start(bf16[128,512]{1,0:T(8,128)(2,1)} %nodes_ref.1), channel_id=1, source_target_pairs={{0,6},{1,7},{2,4},{3,5},{4,2},{5,3},{6,0},{7,1},{8,14},{9,15},{10,... | collective-permute-start | bytes 393224 | tf_op jit(solution)/shard_map/ppermute | solution.py:43
  4.4 10.5 %collective-permute-start.4 = (bf16[128,512]{1,0:T(8,128)(2,1)}, bf16[128,512]{1,0:T(8,128)(2,1)S(1)}, u32[]{:S(2)}, u32[]{:S(2)}) collective-permute-start(bf16[128,512]{1,0:T(8,128)(2,1)} %nodes_ref.1), channel_id=1, source_target_pairs={{0,8},{4,12},{8,0},{12,4},{16,24},{20,28},{24,16},{28,20},{1,9},{5... | collective-permute-start | bytes 393224 | tf_op jit(solution)/shard_map/ppermute | solution.py:33
  10.7 18.9 %copy-start.6 = (bf16[512,512]{1,0:T(8,128)(2,1)S(1)}, bf16[512,512]{1,0:T(8,128)(2,1)}, u32[]{:S(2)}) copy-start(bf16[512,512]{1,0:T(8,128)(2,1)} %refs_3_.1) | copy-start | bytes 1572868
  10.7 18.8 %copy-start.3 = (bf16[512,512]{1,0:T(8,128)(2,1)S(1)}, bf16[512,512]{1,0:T(8,128)(2,1)}, u32[]{:S(2)}) copy-start(bf16[512,512]{1,0:T(8,128)(2,1)} %refs_0_.2) | copy-start | bytes 1572868
  10.7 18.8 %copy-start.4 = (bf16[512,512]{1,0:T(8,128)(2,1)S(1)}, bf16[512,512]{1,0:T(8,128)(2,1)}, u32[]{:S(2)}) copy-start(bf16[512,512]{1,0:T(8,128)(2,1)} %refs_1_.1) | copy-start | bytes 1572868
  10.7 18.8 %copy-start.5 = (bf16[512,512]{1,0:T(8,128)(2,1)S(1)}, bf16[512,512]{1,0:T(8,128)(2,1)}, u32[]{:S(2)}) copy-start(bf16[512,512]{1,0:T(8,128)(2,1)} %refs_2_.1) | copy-start | bytes 1572868
  10.7 18.8 %copy-start.17 = (f32[512]{0:T(512)S(1)}, f32[512]{0:T(512)}, u32[]{:S(2)}) copy-start(f32[512]{0:T(512)} %param.21) | copy-start | bytes 6148
  10.7 8.9 %collective-permute-start.11 = (bf16[256,512]{1,0:T(8,128)(2,1)S(1)}, bf16[256,512]{1,0:T(8,128)(2,1)S(1)}, u32[]{:S(2)}, u32[]{:S(2)}) collective-permute-start(bf16[256,512]{1,0:T(8,128)(2,1)S(1)} %pad_maximum_fusion.2), channel_id=1, source_target_pairs={{0,8},{8,16},{16,24},{12,4},{20,12},{28,20},{1,9},{9,17},{17,25},{... | collective-permute-start | bytes 786440 | tf_op jit(solution)/shard_map/ppermute | solution.py:421
  14.4 5.2 %collective-permute-start.6 = (bf16[128,512]{1,0:T(8,128)(2,1)}, bf16[128,512]{1,0:T(8,128)(2,1)S(1)}, u32[]{:S(2)}, u32[]{:S(2)}) collective-permute-start(bf16[128,512]{1,0:T(8,128)(2,1)} %nodes_ref.1), channel_id=1, source_target_pairs={{0,2},{1,3},{2,0},{3,1},{4,6},{5,7},{6,4},{7,5},{8,10},{9,11},{10,... | collective-permute-start | bytes 393224 | tf_op jit(solution)/shard_map/ppermute | solution.py:33
  15.9 17.8 %collective-permute-start.5 = (bf16[256,512]{1,0:T(8,128)(2,1)S(1)}, bf16[256,512]{1,0:T(8,128)(2,1)S(1)}, u32[]{:S(2)}, u32[]{:S(2)}) collective-permute-start(bf16[256,512]{1,0:T(8,128)(2,1)S(1)} %pad_maximum_fusion.1), channel_id=1, source_target_pairs={{0,1},{1,0},{2,3},{3,2},{4,5},{5,4},{6,7},{7,6},{8,9},{9,8},{10,11... | collective-permute-start | bytes 786440 | tf_op jit(solution)/shard_map/ppermute | solution.py:33
  16.0 9.6 %collective-permute-start = (bf16[128,512]{1,0:T(8,128)(2,1)S(1)}, bf16[128,512]{1,0:T(8,128)(2,1)S(1)}, u32[]{:S(2)}, u32[]{:S(2)}) collective-permute-start(bf16[128,512]{1,0:T(8,128)(2,1)S(1)} %copy-done), channel_id=1, source_target_pairs={{0,16},{4,20},{8,24},{12,28},{16,0},{20,4},{24,8},{28,12},{1,17},{... | collective-permute-start | bytes 393224 | tf_op jit(solution)/shard_map/ppermute | solution.py:33
  20.5 24.9 %collective-permute-start.12 = (bf16[640,512]{1,0:T(8,128)(2,1)}, bf16[640,512]{1,0:T(8,128)(2,1)S(1)}, u32[]{:S(2)}, u32[]{:S(2)}) collective-permute-start(bf16[640,512]{1,0:T(8,128)(2,1)} %pad_maximum_fusion), channel_id=1, source_target_pairs={{0,1},{1,0},{2,3},{3,2},{4,5},{5,4},{6,7},{7,6},{8,9},{9,8},{10,11... | collective-permute-start | bytes 1966088 | tf_op jit(solution)/shard_map/ppermute | solution.py:33
  25.6 11.9 %collective-permute-start.1 = (bf16[128,512]{1,0:T(8,128)(2,1)S(1)}, bf16[128,512]{1,0:T(8,128)(2,1)S(1)}, u32[]{:S(2)}, u32[]{:S(2)}) collective-permute-start(bf16[128,512]{1,0:T(8,128)(2,1)S(1)} %collective-permute-done.refs_0_), channel_id=1, source_target_pairs={{0,2},{1,3},{2,0},{3,1},{4,6},{5,7},{6,4},{7,5},{8,10},{9,11},{10,... | collective-permute-start | bytes 393224 | tf_op jit(solution)/shard_map/ppermute | solution.py:33
  27.1 10.4 %collective-permute-start.2 = (bf16[128,512]{1,0:T(8,128)(2,1)S(1)}, bf16[128,512]{1,0:T(8,128)(2,1)S(1)}, u32[]{:S(2)}, u32[]{:S(2)}) collective-permute-start(bf16[128,512]{1,0:T(8,128)(2,1)S(1)} %collective-permute-done.refs_0_), channel_id=1, source_target_pairs={{0,4},{4,0},{8,12},{12,8},{16,20},{20,16},{24,28},{28,24},{1,5},{5... | collective-permute-start | bytes 393224 | tf_op jit(solution)/shard_map/ppermute | solution.py:33
  28.6 9.0 %collective-permute-start.3 = (bf16[128,512]{1,0:T(8,128)(2,1)S(1)}, bf16[128,512]{1,0:T(8,128)(2,1)S(1)}, u32[]{:S(2)}, u32[]{:S(2)}) collective-permute-start(bf16[128,512]{1,0:T(8,128)(2,1)S(1)} %collective-permute-done.refs_0_), channel_id=1, source_target_pairs={{0,6},{1,7},{2,4},{3,5},{4,2},{5,3},{6,0},{7,1},{8,14},{9,15},{10,... | collective-permute-start | bytes 393224 | tf_op jit(solution)/shard_map/ppermute | solution.py:43
  29.5 1.0 %copy-start.7 = (bf16[16,128,128]{2,1,0:T(8,128)(2,1)S(1)}, bf16[16,128,128]{2,1,0:T(8,128)(2,1)}, u32[]{:S(2)}) copy-start(bf16[16,128,128]{2,1,0:T(8,128)(2,1)} %refs_6_.1) | copy-start | bytes 1572868
  30.6 3.2 %copy-start.19 = (f32[8]{0:T(128)S(1)}, f32[8]{0:T(128)}, u32[]{:S(2)}) copy-start(f32[8]{0:T(128)} %softness_ref.1) | copy-start | bytes 100
  33.7 3.8 %copy-start.8 = (bf16[16,128,128]{2,1,0:T(8,128)(2,1)}, bf16[16,128,128]{2,1,0:T(8,128)(2,1)S(1)}, u32[]{:S(2)}) copy-start(bf16[16,128,128]{2,1,0:T(8,128)(2,1)S(1)} %get-tuple-element.40.tiles_ref) | copy-start | bytes 1572868
  33.7 3.8 %copy-start.10 = (bf16[512,512]{1,0:T(8,128)(2,1)}, bf16[512,512]{1,0:T(8,128)(2,1)S(1)}, u32[]{:S(2)}) copy-start(bf16[512,512]{1,0:T(8,128)(2,1)S(1)} %get-tuple-element.38.final_ref) | copy-start | bytes 1572868
  33.7 3.8 %copy-start.16 = (bf16[256,512]{1,0:T(8,128)(2,1)}, bf16[256,512]{1,0:T(8,128)(2,1)S(1)}, u32[]{:S(2)}) copy-start(bf16[256,512]{1,0:T(8,128)(2,1)S(1)} %collective-permute-done.5.twins_ref) | copy-start | bytes 786436
  40.0 1.7 %collective-permute-start.9 = (bf16[256,640]{1,0:T(8,128)(2,1)S(1)}, bf16[256,640]{1,0:T(8,128)(2,1)S(1)}, u32[]{:S(2)}, u32[]{:S(2)}) collective-permute-start(bf16[256,640]{1,0:T(8,128)(2,1)S(1)} %get-tuple-element.34), channel_id=1, source_target_pairs={{0,1},{1,0},{2,3},{3,2},{4,5},{5,4},{6,7},{7,6},{8,9},{9,8},{10,11... | collective-permute-start | bytes 983048 | tf_op jit(solution)/shard_map/ppermute | solution.py:33
  40.0 5.4 %copy-start.2 = (bf16[1024,512]{1,0:T(8,128)(2,1)S(1)}, bf16[1024,512]{1,0:T(8,128)(2,1)}, u32[]{:S(2)}) copy-start(bf16[1024,512]{1,0:T(8,128)(2,1)} %get-tuple-element.42.refs_8_) | copy-start | bytes 3145732
  41.4 4.0 %copy-start.1 = (bf16[512,1024]{1,0:T(8,128)(2,1)S(1)}, bf16[512,1024]{1,0:T(8,128)(2,1)}, u32[]{:S(2)}) copy-start(bf16[512,1024]{1,0:T(8,128)(2,1)} %get-tuple-element.41.refs_7_) | copy-start | bytes 3145732
  41.4 4.0 %copy-start.18 = (s32[1,1,12]{2,1,0:T(1,128)S(1)}, s32[1,1,12]{2,1,0:T(1,128)}, u32[]{:S(2)}) copy-start(s32[1,1,12]{2,1,0:T(1,128)} %param.12) | copy-start | bytes 148
  42.8 0.7 %copy-start.12 = (f32[128,512]{1,0:T(8,128)}, f32[128,512]{1,0:T(8,128)S(1)}, u32[]{:S(2)}) copy-start(f32[128,512]{1,0:T(8,128)S(1)} %get-tuple-element.35.numer_ref) | copy-start | bytes 786436
  43.5 0.7 %copy-start.14 = (f32[128,512]{1,0:T(8,128)}, f32[128,512]{1,0:T(8,128)S(1)}, u32[]{:S(2)}) copy-start(f32[128,512]{1,0:T(8,128)S(1)} %get-tuple-element.36.denom_ref) | copy-start | bytes 786436
  44.2 6.7 %collective-permute-start.10 = (bf16[128,640]{1,0:T(8,128)(2,1)}, bf16[128,640]{1,0:T(8,128)(2,1)}, u32[]{:S(2)}, u32[]{:S(2)}) collective-permute-start(bf16[128,640]{1,0:T(8,128)(2,1)} %get-tuple-element.37), channel_id=1, source_target_pairs={{0,8},{4,12},{8,0},{12,4},{16,24},{20,28},{24,16},{28,20},{1,9},{5... | collective-permute-start | bytes 491528 | tf_op jit(solution)/shard_map/ppermute | solution.py:33
  45.4 1.0 %copy-start.9 = (bf16[16,128,128]{2,1,0:T(8,128)(2,1)S(1)}, bf16[16,128,128]{2,1,0:T(8,128)(2,1)}, u32[]{:S(2)}) copy-start(bf16[16,128,128]{2,1,0:T(8,128)(2,1)} %copy-done.8) | copy-start | bytes 1572868
  46.5 4.4 %copy-start.11 = (bf16[512,512]{1,0:T(8,128)(2,1)S(1)}, bf16[512,512]{1,0:T(8,128)(2,1)}, u32[]{:S(2)}) copy-start(bf16[512,512]{1,0:T(8,128)(2,1)} %copy-done.10) | copy-start | bytes 1572868
  46.5 4.4 %copy-start.13 = (f32[128,512]{1,0:T(8,128)S(1)}, f32[128,512]{1,0:T(8,128)}, u32[]{:S(2)}) copy-start(f32[128,512]{1,0:T(8,128)} %copy-done.12) | copy-start | bytes 786436
  46.5 4.4 %copy-start.15 = (f32[128,512]{1,0:T(8,128)S(1)}, f32[128,512]{1,0:T(8,128)}, u32[]{:S(2)}) copy-start(f32[128,512]{1,0:T(8,128)} %copy-done.14) | copy-start | bytes 786436

commit v3 on v2

v3 whole, which is shorter than its diff:
```python
import functools
import math

import jax
import jax.numpy as jnp
from jax import lax
from jax.experimental import pallas as pl
from jax.experimental.pallas import tpu as pltpu
from jax.sharding import PartitionSpec as P

NUM_SUBSPACES = 8
SUBSPACE_WIDTH = 64
PAIRS = NUM_SUBSPACES // 2
LANES = 128
norm_eps = 1e-06
VMEM = pl.BlockSpec(memory_space=pltpu.VMEM)
ANY = pl.BlockSpec(memory_space=pl.ANY)
F32 = jnp.float32
BF16 = jnp.bfloat16


def params(mebibytes):
    return pltpu.CompilerParams(vmem_limit_bytes=mebibytes << 20)


def cost(flops, transcendentals, data):
    return pl.CostEstimate(
        flops=flops // 16, transcendentals=transcendentals // 16, bytes_accessed=data // 16
    )


def swap(array, axis, mask):
    devices = lax.axis_size(axis)
    return lax.ppermute(array, axis, [(i, i ^ mask) for i in range(devices)])


def swap_both(array, dom_mask, head_mask):
    doms, heads = lax.axis_size("dom"), lax.axis_size("head")
    pairs = [
        (d * heads + h, (d ^ dom_mask) * heads + (h ^ head_mask))
        for d in range(doms)
        for h in range(heads)
    ]
    return lax.ppermute(array, ("dom", "head"), pairs)


def dot(a, b):
    return jnp.dot(a, b, preferred_element_type=F32)


def dot_t(a, b):
    return lax.dot_general(a, b, (((1,), (1,)), ((), ())), preferred_element_type=F32)


def same_head(rows, cols, value):
    row = lax.broadcasted_iota(jnp.int32, (rows, cols), 0) // SUBSPACE_WIDTH
    col = lax.broadcasted_iota(jnp.int32, (rows, cols), 1) // SUBSPACE_WIDTH
    return jnp.where(row == col, value, 0.0).astype(BF16)


def head_normed(projected):
    block = same_head(256, 256, 1.0 / SUBSPACE_WIDTH)
    squares = (projected * projected).astype(BF16)
    mean = jnp.concatenate(
        [dot(squares[:, i : i + 256], block) for i in range(0, projected.shape[1], 256)], axis=1
    )
    return projected * lax.rsqrt(mean + norm_eps)


def padded_queries(queries, pair):
    both = queries[:, pair * LANES : (pair + 1) * LANES]
    first = lax.broadcasted_iota(jnp.int32, both.shape, 1) < SUBSPACE_WIDTH
    zero = jnp.zeros_like(both)
    return jnp.concatenate([jnp.where(first, both, zero), jnp.where(first, zero, both)], axis=0)


def attend(queries, keys_ref, values_ref):
    rows = queries.shape[0]
    count = keys_ref.shape[0]
    ones = jnp.ones((count, LANES), BF16)
    numer, denom = [], []
    first = lax.broadcasted_iota(jnp.int32, (rows, LANES), 1) < SUBSPACE_WIDTH
    for pair in range(PAIRS):
        cols = slice(pair * LANES, (pair + 1) * LANES)
        scores = dot_t(padded_queries(queries, pair), keys_ref[:, cols])
        weights = jnp.exp2(scores).astype(BF16)
        sums = dot(weights, jnp.concatenate([values_ref[:, cols], ones], axis=1))
        numer.append(jnp.where(first, sums[:rows, :LANES], sums[rows:, :LANES]))
        denom.append(jnp.where(first, sums[:rows, LANES:], sums[rows:, LANES:]))
    return jnp.concatenate(numer, axis=1), jnp.concatenate(denom, axis=1)


def keys_values(blocks, lookup_ref, content_ref, keys_ref, values_ref):
    nodes = jnp.concatenate([block[...] for block in blocks], axis=0)
    keys_ref[...] = head_normed(dot(nodes, lookup_ref[...])).astype(BF16)
    values_ref[...] = dot(nodes, content_ref[...]).astype(BF16)


def lineup_kernel(count, *refs):
    row = 0
    for block in refs[:count]:
        refs[-1][row : row + block.shape[0], :] = block[...]
        row += block.shape[0]


def lineup(blocks, after=()):
    rows = sum(block.shape[0] for block in blocks)
    width = blocks[0].shape[1]
    return pl.pallas_call(
        functools.partial(lineup_kernel, len(blocks)),
        out_shape=jax.ShapeDtypeStruct((rows, width), BF16),
        in_specs=[VMEM] * len(blocks) + [ANY] * len(after),
        out_specs=VMEM,
        compiler_params=params(4),
        cost_estimate=cost(0, 0, 1 << 19),
        name="lineup",
    )(*blocks, *after)


def prep_kernel(*refs):
    count = (len(refs) - 1) // 2
    sources, targets, sems = refs[:count], refs[count:-1], refs[-1]
    copies = [
        pltpu.make_async_copy(source, target, sems.at[i])
        for i, (source, target) in enumerate(zip(sources, targets))
    ]
    for copy in copies:
        copy.start()
    for copy in copies:
        copy.wait()


def prep(*arrays):
    return pl.pallas_call(
        prep_kernel,
        out_shape=tuple(jax.ShapeDtypeStruct(a.shape, a.dtype) for a in arrays),
        in_specs=[ANY] * len(arrays),
        out_specs=(VMEM,) * len(arrays),
        scratch_shapes=[pltpu.SemaphoreType.DMA((len(arrays),))],
        compiler_params=params(4),
        cost_estimate=cost(0, 0, 4 << 20),
        name="prep",
    )(*arrays)


def near_kernel(softness_ref, *refs):
    askers, blocks, (asking_ref, lookup_ref, content_ref) = refs[:4], refs[4:-10], refs[-10:-7]
    queries_ref, numer_ref, denom_ref, keys_ref, values_ref, temper, sem = refs[-7:]
    copy = pltpu.make_async_copy(softness_ref, temper, sem)
    copy.start()
    keys_values((askers[2],) + blocks, lookup_ref, content_ref, keys_ref, values_ref)
    rows = jnp.concatenate([block[...] for block in askers], axis=0)
    projected = head_normed(dot(rows, asking_ref[...]))
    copy.wait()
    width = asking_ref.shape[1]
    head = lax.broadcasted_iota(jnp.int32, (1, width), 1) // SUBSPACE_WIDTH
    scale = jnp.zeros((1, width), F32)
    for h in range(NUM_SUBSPACES):
        scale = jnp.where(head == h, temper[h], scale)
    scale = scale * (math.log2(math.e) / math.sqrt(SUBSPACE_WIDTH))
    queries = (projected * scale).astype(BF16)
    queries_ref[...] = queries
    numer_ref[...], denom_ref[...] = attend(queries, keys_ref, values_ref)


def near(softness, askers, blocks, asking, lookup, content):
    length, width = askers[0].shape
    rows, count = len(askers) * length, (1 + len(blocks)) * length
    return pl.pallas_call(
        near_kernel,
        out_shape=(
            jax.ShapeDtypeStruct((rows, width), BF16),
            jax.ShapeDtypeStruct((rows, width), F32),
            jax.ShapeDtypeStruct((rows, width), F32),
        ),
        in_specs=[ANY] + [VMEM] * (7 + len(blocks)),
        out_specs=(VMEM,) * 3,
        scratch_shapes=[pltpu.VMEM((count, width), BF16)] * 2
        + [pltpu.SMEM(softness.shape, F32), pltpu.SemaphoreType.DMA],
        compiler_params=params(16),
        cost_estimate=cost(8 * rows * count * width, rows * count * NUM_SUBSPACES, 4 << 20),
        name="near",
    )(softness, *askers, *blocks, asking, lookup, content)


def pack(numer, denom):
    lane = lax.broadcasted_iota(jnp.int32, (denom.shape[0], LANES), 1)
    sums = denom[:, :LANES]
    for pair in range(1, PAIRS):
        held = (lane % SUBSPACE_WIDTH) // 16 == pair
        sums = jnp.where(held, denom[:, pair * LANES : (pair + 1) * LANES], sums)
    high = sums.astype(BF16).astype(F32)
    sums = jnp.where(lane % 16 < 8, high, sums - high)
    return jnp.concatenate([numer.astype(BF16), sums.astype(BF16)], axis=1)


def unpack_denom(packed, width):
    lane = lax.broadcasted_iota(jnp.int32, (LANES, width), 0)
    col = lax.broadcasted_iota(jnp.int32, (LANES, width), 1)
    half = (col % LANES) // SUBSPACE_WIDTH
    source = half * SUBSPACE_WIDTH + (col // LANES) * 16
    spread = jnp.where((lane == source) | (lane == source + 8), 1.0, 0.0).astype(BF16)
    return dot(packed, spread)


def call(kernel, steps, parts, wholes, out_parts, out_wholes, scratch, estimate, name, after=()):
    taken = len(parts) + len(wholes)

    def body(*refs):
        kernel(steps, *refs[:taken], *refs[taken + len(after) :])

    if steps == 1:
        grid, part, whole = (), lambda a: VMEM, lambda a: VMEM
    else:
        grid = (steps,)
        part = lambda a: pl.BlockSpec((a.shape[0] // steps,) + a.shape[1:], lambda i: (i, 0))
        whole = lambda a: pl.BlockSpec(a.shape, lambda i: (0, 0))
    return pl.pallas_call(
        body,
        grid=grid,
        out_shape=tuple(out_parts) + tuple(out_wholes),
        in_specs=[part(a) for a in parts] + [whole(a) for a in wholes] + [ANY] * len(after),
        out_specs=tuple(part(a) for a in out_parts) + tuple(whole(a) for a in out_wholes),
        scratch_shapes=scratch,
        compiler_params=params(16),
        cost_estimate=estimate,
        name=name,
    )(*parts, *wholes, *after)


def at_step(steps, step, body):
    if steps == 1:
        body()
    else:
        pl.when(pl.program_id(0) == step)(body)


def far_kernel(steps, *refs):
    blocks, (lookup_ref, content_ref, queries_ref, numer_ref, denom_ref) = refs[:-10], refs[-10:-5]
    keys_ref, values_ref, packed_ref, numer_sum, denom_sum = refs[-5:]
    half = queries_ref.shape[0] // 2

    def start():
        numer_sum[...] = numer_ref[:half, :]
        denom_sum[...] = denom_ref[:half, :]

    def end():
        packed_ref[...] = pack(numer_sum[...], denom_sum[...])

    at_step(steps, 0, start)
    keys_values(blocks, lookup_ref, content_ref, keys_ref, values_ref)
    numer, denom = attend(queries_ref[:half, :], keys_ref, values_ref)
    numer_sum[...] += numer
    denom_sum[...] += denom
    at_step(steps, steps - 1, end)


def far(blocks, block_len, lookup, content, queries, numer, denom, after):
    rows, width = queries.shape
    half = rows // 2
    count = len(blocks) * blocks[0].shape[0]
    kept = jax.ShapeDtypeStruct((count, width), BF16)
    return call(
        far_kernel,
        blocks[0].shape[0] // block_len,
        blocks,
        (lookup, content, queries, numer, denom),
        (kept, kept),
        (jax.ShapeDtypeStruct((half, width + LANES), BF16),),
        [pltpu.VMEM((half, width), F32)] * 2,
        cost(6 * half * count * width, half * count * NUM_SUBSPACES, 4 << 20),
        "far",
        after,
    )


def rest_kernel(steps, keys_ref, values_ref, queries_ref, numer_ref, denom_ref, numer_out, denom_out):
    half = queries_ref.shape[0] // 2

    def start():
        numer_out[...] = numer_ref[half:, :]
        denom_out[...] = denom_ref[half:, :]

    at_step(steps, 0, start)
    numer, denom = attend(queries_ref[half:, :], keys_ref, values_ref)
    numer_out[...] += numer
    denom_out[...] += denom


def rest(keys, values, steps, queries, numer, denom):
    rows, width = queries.shape
    half = rows // 2
    count = keys.shape[0]
    return call(
        rest_kernel,
        steps,
        (keys, values),
        (queries, numer, denom),
        (),
        (jax.ShapeDtypeStruct((half, width), F32),) * 2,
        [],
        cost(4 * half * count * width, half * count * NUM_SUBSPACES, 4 << 20),
        "rest",
    )


def combine_kernel(numer_ref, denom_ref, packed_ref, numer_out, denom_out, packed_out):
    rows, width = numer_out.shape
    numer = numer_ref[...] + packed_ref[:, :width].astype(F32)
    denom = denom_ref[...] + unpack_denom(packed_ref[:, width:], width)
    numer_out[...] = numer[:rows]
    denom_out[...] = denom[:rows]
    packed_out[...] = pack(numer[rows:], denom[rows:])


def combine(numer, denom, packed):
    rows, width = numer.shape[0] // 2, numer.shape[1]
    return pl.pallas_call(
        combine_kernel,
        out_shape=(
            jax.ShapeDtypeStruct((rows, width), F32),
            jax.ShapeDtypeStruct((rows, width), F32),
            jax.ShapeDtypeStruct((rows, width + LANES), BF16),
        ),
        in_specs=[VMEM] * 3,
        out_specs=(VMEM,) * 3,
        compiler_params=params(16),
        cost_estimate=cost(4 * rows * width * LANES, 0, 1 << 20),
        name="combine",
    )(numer, denom, packed)


def message_kernel(slots_ref, tiles_ref, *refs):
    blocks, (inner_ref, outer_ref, local_ref, slots, sem) = refs[:7], refs[7:]
    copy = pltpu.make_async_copy(slots_ref, slots, sem)
    copy.start()
    group = slots_ref.shape[0] // 3
    me, odd = lax.axis_index("head"), lax.axis_index("dom") % 2
    beside, beyond = 2 - 2 * odd, 2 * odd
    order = [(1, 0), (1, 1), (1, 2), (beside, 0), (beside, 2), (beyond, 0), (beyond, 2)]
    order += [(1, 3), (beside, 1), (beside, 3), (beyond, 1), (beyond, 3)]
    copy.wait()
    tiles = []
    for side, offset in order:
        tile_id = slots[side * group + (me ^ offset)]
        tile = tiles_ref[jnp.maximum(tile_id, 0)]
        tiles.append(jnp.where(tile_id >= 0, tile, jnp.zeros_like(tile)))
    nodes = jnp.concatenate([block[...] for block in blocks], axis=0)
    aggregate = dot(jnp.concatenate(tiles, axis=1), nodes).astype(BF16)
    hidden = jax.nn.gelu(dot(aggregate, inner_ref[...])).astype(BF16)
    local_ref[...] = dot(hidden, outer_ref[...])


def message(slots, tiles, blocks, inner, outer):
    rows, width = blocks[0].shape
    hidden = inner.shape[1]
    return pl.pallas_call(
        message_kernel,
        out_shape=jax.ShapeDtypeStruct((rows, width), F32),
        in_specs=[ANY] + [VMEM] * 10,
        out_specs=VMEM,
        scratch_shapes=[pltpu.SMEM(slots.shape, jnp.int32), pltpu.SemaphoreType.DMA],
        compiler_params=params(16),
        cost_estimate=cost(
            2 * rows * width * (12 * rows + 2 * hidden), rows * hidden, 4 << 20
        ),
        name="message",
    )(slots, tiles, *blocks, inner, outer)


def finish_kernel(
    numer_ref, denom_ref, packed_ref, final_ref, gain_ref, local_ref, nodes_ref, out_ref
):
    width = numer_ref.shape[1]
    numer = numer_ref[...] + packed_ref[:, :width].astype(F32)
    denom = denom_ref[...] + unpack_denom(packed_ref[:, width:], width)
    mixed = (numer / denom).astype(BF16)
    attended = dot(mixed, final_ref[...])
    mean = jnp.mean(attended * attended, axis=-1, keepdims=True)
    normed = attended * lax.rsqrt(mean + norm_eps) * gain_ref[...]
    out_ref[...] = (nodes_ref[...].astype(F32) + local_ref[...] + normed).astype(BF16)


def finish(numer, denom, packed, final, gain, local, nodes):
    rows, width = nodes.shape
    return pl.pallas_call(
        finish_kernel,
        out_shape=jax.ShapeDtypeStruct((rows, width), BF16),
        in_specs=[VMEM] * 7,
        out_specs=VMEM,
        compiler_params=params(16),
        cost_estimate=cost(2 * rows * width * width, rows, 2 << 20),
        name="finish",
    )(numer, denom, packed, final, gain, local, nodes)


def shards(
    vertex_embeddings,
    adjacent_group_bank_ids,
    coupling_strength_panels,
    asking_projector,
    lookup_projector,
    content_projector,
    final_projector,
    passing_inner_coefficients,
    passing_outer_coefficients,
    softness_per_subspace,
    mixing_layer_gain,
):
    block_len = vertex_embeddings.shape[0]
    doms = lax.axis_size("dom")
    nodes = vertex_embeddings
    stacked = lambda *arrays: jnp.concatenate(arrays, axis=0)

    distant = swap(nodes, "dom", 4)
    mask = 8
    while mask < doms:
        distant = stacked(distant, swap(stacked(nodes, distant), "dom", mask))
        mask *= 2

    def plane(block):
        side = swap(block, "dom", 1)
        below = swap(block, "head", 2)
        across = swap_both(block, 1, 2)
        return below, side, across

    near_blocks = plane(nodes)
    other = swap(nodes, "dom", 2)
    twin = swap(nodes, "head", 1)
    other_twin = swap_both(nodes, 2, 1)
    far_blocks = plane(distant)
    steps = distant.shape[0] // block_len
    if steps == 1:
        early = near_blocks + (distant,)
    else:
        early, far_blocks = near_blocks, (distant,) + far_blocks
    asking, lookup, content = prep(asking_projector, lookup_projector, content_projector)
    queries, numer, denom = near(
        softness_per_subspace, (twin, other_twin, nodes, other), early, asking, lookup, content
    )

    below, side, across = near_blocks
    pairs = [(p, p + 2) for p in range(0, doms - 2, 2)] + [(p, p - 2) for p in range(3, doms, 2)]
    halo = lax.ppermute(lineup((side, across), (distant, below)), "dom", pairs)
    keys, values, packed = far(
        far_blocks, block_len, lookup, content, queries, numer, denom, (halo,)
    )
    packed = swap(packed, "head", 1)
    numer, denom = rest(keys, values, steps, queries, numer, denom)
    numer, denom, packed = combine(numer, denom, packed)
    packed = swap(packed, "dom", 2)
    halo_twins = swap(lineup((below, side, across, halo), (numer,)), "head", 1)
    local = message(
        adjacent_group_bank_ids.reshape(-1),
        coupling_strength_panels,
        (nodes, twin, below, side, across, halo, halo_twins),
        passing_inner_coefficients,
        passing_outer_coefficients,
    )
    return finish(
        numer, denom, packed, final_projector, mixing_layer_gain.reshape(1, -1), local, nodes
    )


def solution(mesh):
    in_specs = (P(("dom", "head"), None), P("dom", "head", None)) + (P(),) * 9
    out_specs = P(("dom", "head"), None)
    return jax.shard_map(shards, mesh=mesh, in_specs=in_specs, out_specs=out_specs, check_vma=False)
```

time: 53.3 us -> 39.4 us (0.74)
  Pallas kernels: 15.7 us -> 10.8 us
  waiting for transfers between devices: 13.4 us -> 8.67 us
  other arithmetic: 1.93 us -> 0 us
  local copies, waits for them, and re-layouts: 4.45 us -> 2.77 us
    ppermute x2 -> x3, waiting for transfers between devices: 3.5 us -> 0.01 us  [swap_both(): return lax.ppermute(array, ('dom', 'head'), pairs)]
    pallas_call x1, Pallas kernels: 3.11 us -> 0.14 us  [prep(): pl.pallas_call(prep_kernel, out_shape=tuple((jax.ShapeDtypeStruct(a.shape...]
    ppermute x2 -> x3, starting transfers between devices: 2.45 us -> 5.09 us  [swap_both(): return lax.ppermute(array, ('dom', 'head'), pairs)]
    ppermute x10, starting transfers between devices: 11 us -> 8.95 us  [swap(): return lax.ppermute(array, axis, [(i, i ^ mask) for i in range(devices)])]
    concatenate x3 -> x0, other arithmetic: 1.86 us -> none  [shards(): stacked = lambda *arrays: jnp.concatenate(arrays, axis=0)]
    ppermute x10, waiting for transfers between devices: 9.9 us -> 8.66 us  [swap(): return lax.ppermute(array, axis, [(i, i ^ mask) for i in range(devices)])]
    pallas_call x1, Pallas kernels: 3.75 us -> 4.94 us  [near(): pl.pallas_call(near_kernel, out_shape=(jax.ShapeDtypeStruct((rows, width)...]
    ppermute x1, starting transfers between devices: 3.63 us -> 2.65 us  [shards(): halo = lax.ppermute(lineup((side, across), (distant, below)), 'dom', pairs)]
  transfers between devices with their start and end apart: 13 -> 14, of which waited for: 6 -> 5; matrix products, arithmetic and copies ran while one was open for 5% -> 0% of each run, Pallas kernels for 26% -> 20%
where the time goes in v3:
time: 39.4 us; the launch traced here: 39.1 us
  starting transfers between devices  16.7 us (42%)
  Pallas kernels  10.8 us (27%)
  waiting for transfers between devices  8.67 us (22%)
  local copies, waits for them, and re-layouts  2.77 us (7%)
    ppermute x10, starting transfers between devices, swap(): return lax.ppermute(array, axis, [(i, i ^ mask) for i in range(devices)])  8.95 us
    ppermute x10, waiting for transfers between devices, swap(): return lax.ppermute(array, axis, [(i, i ^ mask) for i in range(devices)])  8.66 us
    ppermute x3, starting transfers between devices, swap_both(): return lax.ppermute(array, ('dom', 'head'), pairs)  5.09 us
    pallas_call x1, Pallas kernels, near(): pl.pallas_call(near_kernel, out_shape=(jax.ShapeDtypeStruct((rows, width)...  4.94 us
    pallas_call x2, Pallas kernels, call(): pl.pallas_call(body, grid=grid, out_shape=tuple(out_parts) + tuple(out_wh...  2.82 us
    unnamed x22, local copies, waits for them, and re-layouts  2.77 us
    ppermute x1, starting transfers between devices, shards(): halo = lax.ppermute(lineup((side, across), (distant, below)), 'dom', pairs)  2.65 us
    pallas_call x1, Pallas kernels, message(): pl.pallas_call(message_kernel, out_shape=jax.ShapeDtypeStruct((rows, widt...  1.45 us
  transfers between devices with their start and end apart: 14, of which 5 were waited for; matrix products, arithmetic and copies ran while one was open for 0% of the time, Pallas kernels for 20%

profile of v3, /device:TPU:0, one launch (start us, length us, event | category | flops | bytes accessed | tf_op | source)
XLA Modules:
  0.0 39.1 jit_solution(12683242137445387691)
XLA Ops:
  0.0 3.9 %collective-permute-start.9 = (bf16[128,512]{1,0:T(8,128)(2,1)}, bf16[128,512]{1,0:T(8,128)(2,1)S(1)}, u32[]{:S(2)}, u32[]{:S(2)}) collective-permute-start(bf16[128,512]{1,0:T(8,128)(2,1)} %nodes_ref.1), channel_id=1, source_target_pairs={{0,6},{1,7},{2,4},{3,5},{4,2},{5,3},{6,0},{7,1},{8,14},{9,15},{10,... | collective-permute-start | bytes 393224 | tf_op jit(solution)/shard_map/ppermute | solution.py:44
  3.9 0.5 %collective-permute-start.8 = (bf16[128,512]{1,0:T(8,128)(2,1)}, bf16[128,512]{1,0:T(8,128)(2,1)S(1)}, u32[]{:S(2)}, u32[]{:S(2)}) collective-permute-start(bf16[128,512]{1,0:T(8,128)(2,1)} %nodes_ref.1), channel_id=1, source_target_pairs={{0,4},{4,0},{8,12},{12,8},{16,20},{20,16},{24,28},{28,24},{1,5},{5... | collective-permute-start | bytes 393224 | tf_op jit(solution)/shard_map/ppermute | solution.py:34
  4.4 0.1 collective-permute-start.7
  4.5 3.0 %collective-permute-start = (bf16[128,512]{1,0:T(8,128)(2,1)}, bf16[128,512]{1,0:T(8,128)(2,1)S(1)}, u32[]{:S(2)}, u32[]{:S(2)}) collective-permute-start(bf16[128,512]{1,0:T(8,128)(2,1)} %nodes_ref.1), channel_id=1, source_target_pairs={{0,16},{4,20},{8,24},{12,28},{16,0},{20,4},{24,8},{28,12},{1,17},{... | collective-permute-start | bytes 393224 | tf_op jit(solution)/shard_map/ppermute | solution.py:34
  7.5 1.6 %collective-permute-start.6 = (bf16[128,512]{1,0:T(8,128)(2,1)}, bf16[128,512]{1,0:T(8,128)(2,1)S(1)}, u32[]{:S(2)}, u32[]{:S(2)}) collective-permute-start(bf16[128,512]{1,0:T(8,128)(2,1)} %nodes_ref.1), channel_id=1, source_target_pairs={{0,8},{4,12},{8,0},{12,4},{16,24},{20,28},{24,16},{28,20},{1,9},{5... | collective-permute-start | bytes 393224 | tf_op jit(solution)/shard_map/ppermute | solution.py:34
  9.1 0.0 collective-permute-done.9.refs_6_.refs_1_.refs_2_.refs_4_
  9.1 0.0 collective-permute-start.5
  9.1 1.6 %collective-permute-done.8.refs_5_.refs_0_.refs_1_.refs_3_ = bf16[128,512]{1,0:T(8,128)(2,1)S(1)} collective-permute-done((bf16[128,512]{1,0:T(8,128)(2,1)}, bf16[128,512]{1,0:T(8,128)(2,1)S(1)}, u32[]{:S(2)}, u32[]{:S(2)}) %collective-permute-start.8) | collective-permute-done | bytes 131104 | tf_op jit(solution)/shard_map/ppermute | solution.py:34
  10.7 0.0 collective-permute-done.7.refs_4_.refs_3_.refs_0_.refs_2_
  10.7 2.7 %collective-permute-done.refs_7_.refs_2_ = bf16[128,512]{1,0:T(8,128)(2,1)S(1)} collective-permute-done((bf16[128,512]{1,0:T(8,128)(2,1)}, bf16[128,512]{1,0:T(8,128)(2,1)S(1)}, u32[]{:S(2)}, u32[]{:S(2)}) %collective-permute-start) | collective-permute-done | bytes 131104 | tf_op jit(solution)/shard_map/ppermute | solution.py:34
  13.4 2.7 %collective-permute-start.10 = (bf16[256,512]{1,0:T(8,128)(2,1)S(1)}, bf16[256,512]{1,0:T(8,128)(2,1)S(1)}, u32[]{:S(2)}, u32[]{:S(2)}) collective-permute-start(bf16[256,512]{1,0:T(8,128)(2,1)S(1)} %lineup.2), channel_id=1, source_target_pairs={{0,8},{8,16},{16,24},{12,4},{20,12},{28,20},{1,9},{9,17},{17,25},{... | collective-permute-start | bytes 786440 | tf_op jit(solution)/shard_map/ppermute | solution.py:444
  16.0 0.0 copy-done
  16.0 0.1 collective-permute-start.4
  16.1 1.2 %collective-permute-start.3 = (bf16[128,512]{1,0:T(8,128)(2,1)S(1)}, bf16[128,512]{1,0:T(8,128)(2,1)S(1)}, u32[]{:S(2)}, u32[]{:S(2)}) collective-permute-start(bf16[128,512]{1,0:T(8,128)(2,1)S(1)} %collective-permute-done.refs_7_.refs_2_), channel_id=1, source_target_pairs={{0,6},{1,7},{2,4},{3,5},{4,2},{5,3},{6,0},{7,1},{8,14},{9,15},{10,... | collective-permute-start | bytes 393224 | tf_op jit(solution)/shard_map/ppermute | solution.py:44
  17.3 0.0 collective-permute-done.6.refs_3_
  17.3 1.9 %collective-permute-start.2 = (bf16[128,512]{1,0:T(8,128)(2,1)S(1)}, bf16[128,512]{1,0:T(8,128)(2,1)S(1)}, u32[]{:S(2)}, u32[]{:S(2)}) collective-permute-start(bf16[128,512]{1,0:T(8,128)(2,1)S(1)} %collective-permute-done.refs_7_.refs_2_), channel_id=1, source_target_pairs={{0,4},{4,0},{8,12},{12,8},{16,20},{20,16},{24,28},{28,24},{1,5},{5... | collective-permute-start | bytes 393224 | tf_op jit(solution)/shard_map/ppermute | solution.py:34
  19.2 0.0 collective-permute-done.5.refs_1_
  19.2 0.5 %collective-permute-start.1 = (bf16[128,512]{1,0:T(8,128)(2,1)S(1)}, bf16[128,512]{1,0:T(8,128)(2,1)S(1)}, u32[]{:S(2)}, u32[]{:S(2)}) collective-permute-start(bf16[128,512]{1,0:T(8,128)(2,1)S(1)} %collective-permute-done.refs_7_.refs_2_), channel_id=1, source_target_pairs={{0,2},{1,3},{2,0},{3,1},{4,6},{5,7},{6,4},{7,5},{8,10},{9,11},{10,... | collective-permute-start | bytes 393224 | tf_op jit(solution)/shard_map/ppermute | solution.py:34
  19.7 0.0 copy-done.3
  19.7 1.0 %copy-done.4 = bf16[512,512]{1,0:T(8,128)(2,1)S(1)} copy-done((bf16[512,512]{1,0:T(8,128)(2,1)S(1)}, bf16[512,512]{1,0:T(8,128)(2,1)}, u32[]{:S(2)}) %copy-start.4) | copy-done | bytes 524312
  20.7 1.0 %copy-done.5 = bf16[512,512]{1,0:T(8,128)(2,1)S(1)} copy-done((bf16[512,512]{1,0:T(8,128)(2,1)S(1)}, bf16[512,512]{1,0:T(8,128)(2,1)}, u32[]{:S(2)}) %copy-start.5) | copy-done | bytes 524312
  21.8 0.1 prep.1
  21.9 0.0 collective-permute-done.4.refs_0_.refs_1_
  21.9 0.0 copy-start.10
  21.9 0.6 %copy-done.10 = f32[8]{0:T(128)S(1)} copy-done((f32[8]{0:T(128)S(1)}, f32[8]{0:T(128)}, u32[]{:S(2)}) %copy-start.10) | copy-done | bytes 56
  22.6 4.9 %near.1 = (bf16[512,512]{1,0:T(8,128)(2,1)S(1)}, f32[512,512]{1,0:T(8,128)S(1)}, f32[512,512]{1,0:T(8,128)S(1)}) custom-call(f32[8]{0:T(128)S(1)} %copy-done.10, bf16[128,512]{1,0:T(8,128)(2,1)S(1)} %collective-permute-done.4.refs_0_.refs_1_, bf16[128,512]{1,0:T(8,128)(2,1)S(1)} %collective-permute-done.5.refs_1_, bf16[128,512]{1,0:T(8,128)(2,1)S(1)} %copy-done, ...), custom_call_target="tpu_custom_call" | custom-call | flops 83886080 | bytes 262144 | tf_op jit(solution)/shard_map/near/pallas_call | solution.py:169
  27.5 0.0 collective-permute-done.3.refs_2_
  27.5 0.0 collective-permute-done.2.refs_1_
  27.5 0.0 collective-permute-done.1.refs_0_
  27.6 0.0 collective-permute-done.10.refs_8_.refs_3_.refs_5_
  27.6 1.7 %far.1 = (bf16[384,512]{1,0:T(8,128)(2,1)S(1)}, bf16[384,512]{1,0:T(8,128)(2,1)S(1)}, bf16[256,640]{1,0:T(8,128)(2,1)S(1)}) custom-call(bf16[128,512]{1,0:T(8,128)(2,1)S(1)} %collective-permute-done.1.refs_0_, bf16[128,512]{1,0:T(8,128)(2,1)S(1)} %collective-permute-done.2.refs_1_, bf16[128,512]{1,0:T(8,128)(2,1)S(1)} %collective-permute-done.3.refs_2_, ...), custom_call_target="tpu_custom_call" | custom-call | flops 18874368 | bytes 262144 | tf_op jit(solution)/shard_map/far/pallas_call | solution.py:218
  29.3 0.1 collective-permute-start.11
  29.4 1.1 %rest.1 = (f32[256,512]{1,0:T(8,128)S(1)}, f32[256,512]{1,0:T(8,128)S(1)}) custom-call(bf16[384,512]{1,0:T(8,128)(2,1)S(1)} %get-tuple-element.25.refs_0_, bf16[384,512]{1,0:T(8,128)(2,1)S(1)} %get-tuple-element.26.refs_1_, bf16[512,512]{1,0:T(8,128)(2,1)S(1)} %get-tuple-element.22.refs_5_.refs_2_, f32[512,512]{1,0:T(8,128)S(1)} %get-tuple-element.23.refs_6_.refs_3_, ...), custom_call_target="tpu_custom_call" | custom-call | flops 12582912 | bytes 262144 | tf_op jit(solution)/shard_map/rest/pallas_call | solution.py:218
  30.5 0.5 %collective-permute-done.11.packed_ref = bf16[256,640]{1,0:T(8,128)(2,1)S(1)} collective-permute-done((bf16[256,640]{1,0:T(8,128)(2,1)S(1)}, bf16[256,640]{1,0:T(8,128)(2,1)S(1)}, u32[]{:S(2)}, u32[]{:S(2)}) %collective-permute-start.11) | collective-permute-done | bytes 327712 | tf_op jit(solution)/shard_map/ppermute | solution.py:34
  31.0 0.3 combine.1
  31.2 0.0 copy-start.1
  31.3 0.0 copy-start.6
  31.3 0.2 collective-permute-start.13
  31.5 1.0 %collective-permute-start.12 = (bf16[128,640]{1,0:T(8,128)(2,1)S(1)}, bf16[128,640]{1,0:T(8,128)(2,1)S(1)}, u32[]{:S(2)}, u32[]{:S(2)}) collective-permute-start(bf16[128,640]{1,0:T(8,128)(2,1)S(1)} %get-tuple-element.32), channel_id=1, source_target_pairs={{0,8},{4,12},{8,0},{12,4},{16,24},{20,28},{24,16},{28,20},{1,9},{5... | collective-permute-start | bytes 491528 | tf_op jit(solution)/shard_map/ppermute | solution.py:34
  32.6 0.9 %collective-permute-done.13.refs_6_ = bf16[640,512]{1,0:T(8,128)(2,1)S(1)} collective-permute-done((bf16[640,512]{1,0:T(8,128)(2,1)S(1)}, bf16[640,512]{1,0:T(8,128)(2,1)S(1)}, u32[]{:S(2)}, u32[]{:S(2)}) %collective-permute-start.13) | collective-permute-done | bytes 655392 | tf_op jit(solution)/shard_map/ppermute | solution.py:34
  33.5 0.0 copy-done.2
  33.5 0.0 copy-done.1
  33.5 0.0 copy-done.9
  33.5 0.0 copy-start.7
  33.5 1.5 %message.1.local_ref = f32[128,512]{1,0:T(8,128)S(1)} custom-call(s32[12]{0:T(128)S(1)} %bitcast.3, bf16[16,128,128]{2,1,0:T(8,128)(2,1)S(1)} %copy-done.6, bf16[128,512]{1,0:T(8,128)(2,1)S(1)} %copy-done, bf16[128,512]{1,0:T(8,128)(2,1)S(1)} %collective-permute-done.4.refs_0_.refs_1_, ...), custom_call_target="tpu_custom_call" | custom-call | flops 29360128 | bytes 262144 | tf_op jit(solution)/shard_map/message/pallas_call | solution.py:357
  35.0 0.0 copy-start.8
  35.0 3.0 %collective-permute-done.12.packed_ref = bf16[128,640]{1,0:T(8,128)(2,1)S(1)} collective-permute-done((bf16[128,640]{1,0:T(8,128)(2,1)S(1)}, bf16[128,640]{1,0:T(8,128)(2,1)S(1)}, u32[]{:S(2)}, u32[]{:S(2)}) %collective-permute-start.12) | collective-permute-done | bytes 163872 | tf_op jit(solution)/shard_map/ppermute | solution.py:34
  38.0 1.1 %finish.1 = bf16[128,512]{1,0:T(8,128)(2,1)} custom-call(f32[128,512]{1,0:T(8,128)S(1)} %get-tuple-element.30.refs_4_.numer_ref, f32[128,512]{1,0:T(8,128)S(1)} %get-tuple-element.31.denom_ref, bf16[128,640]{1,0:T(8,128)(2,1)S(1)} %collective-permute-done.12.packed_ref, bf16[512,512]{1,0:T(8,128)(2,1)S(1)} %copy-done.7, f32[1,512]{1,0:T(1,128)S(1)} %bitcast.2, ...), custom_call_target="tpu_custom_call" | custom-call | flops 4194304 | bytes 131072 | tf_op jit(solution)/shard_map/finish/pallas_call | solution.py:386
  (11 shorter events, 0.1 us)
Async XLA Ops:
  0.0 16.0 %copy-start = (bf16[128,512]{1,0:T(8,128)(2,1)S(1)}, bf16[128,512]{1,0:T(8,128)(2,1)}, u32[]{:S(2)}) copy-start(bf16[128,512]{1,0:T(8,128)(2,1)} %nodes_ref.1) | copy-start | bytes 393220
  0.0 19.7 %copy-start.3 = (bf16[512,512]{1,0:T(8,128)(2,1)S(1)}, bf16[512,512]{1,0:T(8,128)(2,1)}, u32[]{:S(2)}) copy-start(bf16[512,512]{1,0:T(8,128)(2,1)} %refs_0_.2) | copy-start | bytes 1572868
  0.0 9.1 %collective-permute-start.9 = (bf16[128,512]{1,0:T(8,128)(2,1)}, bf16[128,512]{1,0:T(8,128)(2,1)S(1)}, u32[]{:S(2)}, u32[]{:S(2)}) collective-permute-start(bf16[128,512]{1,0:T(8,128)(2,1)} %nodes_ref.1), channel_id=1, source_target_pairs={{0,6},{1,7},{2,4},{3,5},{4,2},{5,3},{6,0},{7,1},{8,14},{9,15},{10,... | collective-permute-start | bytes 393224 | tf_op jit(solution)/shard_map/ppermute | solution.py:44
  3.9 6.8 %collective-permute-start.8 = (bf16[128,512]{1,0:T(8,128)(2,1)}, bf16[128,512]{1,0:T(8,128)(2,1)S(1)}, u32[]{:S(2)}, u32[]{:S(2)}) collective-permute-start(bf16[128,512]{1,0:T(8,128)(2,1)} %nodes_ref.1), channel_id=1, source_target_pairs={{0,4},{4,0},{8,12},{12,8},{16,20},{20,16},{24,28},{28,24},{1,5},{5... | collective-permute-start | bytes 393224 | tf_op jit(solution)/shard_map/ppermute | solution.py:34
  4.4 6.2 %collective-permute-start.7 = (bf16[128,512]{1,0:T(8,128)(2,1)}, bf16[128,512]{1,0:T(8,128)(2,1)S(1)}, u32[]{:S(2)}, u32[]{:S(2)}) collective-permute-start(bf16[128,512]{1,0:T(8,128)(2,1)} %nodes_ref.1), channel_id=1, source_target_pairs={{0,2},{1,3},{2,0},{3,1},{4,6},{5,7},{6,4},{7,5},{8,10},{9,11},{10,... | collective-permute-start | bytes 393224 | tf_op jit(solution)/shard_map/ppermute | solution.py:34
  4.5 8.8 %collective-permute-start = (bf16[128,512]{1,0:T(8,128)(2,1)}, bf16[128,512]{1,0:T(8,128)(2,1)S(1)}, u32[]{:S(2)}, u32[]{:S(2)}) collective-permute-start(bf16[128,512]{1,0:T(8,128)(2,1)} %nodes_ref.1), channel_id=1, source_target_pairs={{0,16},{4,20},{8,24},{12,28},{16,0},{20,4},{24,8},{28,12},{1,17},{... | collective-permute-start | bytes 393224 | tf_op jit(solution)/shard_map/ppermute | solution.py:34
  7.5 9.8 %collective-permute-start.6 = (bf16[128,512]{1,0:T(8,128)(2,1)}, bf16[128,512]{1,0:T(8,128)(2,1)S(1)}, u32[]{:S(2)}, u32[]{:S(2)}) collective-permute-start(bf16[128,512]{1,0:T(8,128)(2,1)} %nodes_ref.1), channel_id=1, source_target_pairs={{0,8},{4,12},{8,0},{12,4},{16,24},{20,28},{24,16},{28,20},{1,9},{5... | collective-permute-start | bytes 393224 | tf_op jit(solution)/shard_map/ppermute | solution.py:34
  9.1 10.1 %collective-permute-start.5 = (bf16[128,512]{1,0:T(8,128)(2,1)}, bf16[128,512]{1,0:T(8,128)(2,1)S(1)}, u32[]{:S(2)}, u32[]{:S(2)}) collective-permute-start(bf16[128,512]{1,0:T(8,128)(2,1)} %nodes_ref.1), channel_id=1, source_target_pairs={{0,9},{1,8},{2,11},{3,10},{4,13},{5,12},{6,15},{7,14},{8,1},{9,0},... | collective-permute-start | bytes 393224 | tf_op jit(solution)/shard_map/ppermute | solution.py:44
  13.4 14.2 %collective-permute-start.10 = (bf16[256,512]{1,0:T(8,128)(2,1)S(1)}, bf16[256,512]{1,0:T(8,128)(2,1)S(1)}, u32[]{:S(2)}, u32[]{:S(2)}) collective-permute-start(bf16[256,512]{1,0:T(8,128)(2,1)S(1)} %lineup.2), channel_id=1, source_target_pairs={{0,8},{8,16},{16,24},{12,4},{20,12},{28,20},{1,9},{9,17},{17,25},{... | collective-permute-start | bytes 786440 | tf_op jit(solution)/shard_map/ppermute | solution.py:444
  16.0 5.9 %collective-permute-start.4 = (bf16[128,512]{1,0:T(8,128)(2,1)S(1)}, bf16[128,512]{1,0:T(8,128)(2,1)S(1)}, u32[]{:S(2)}, u32[]{:S(2)}) collective-permute-start(bf16[128,512]{1,0:T(8,128)(2,1)S(1)} %copy-done), channel_id=1, source_target_pairs={{0,1},{1,0},{2,3},{3,2},{4,5},{5,4},{6,7},{7,6},{8,9},{9,8},{10,11... | collective-permute-start | bytes 393224 | tf_op jit(solution)/shard_map/ppermute | solution.py:34
  16.1 11.4 %collective-permute-start.3 = (bf16[128,512]{1,0:T(8,128)(2,1)S(1)}, bf16[128,512]{1,0:T(8,128)(2,1)S(1)}, u32[]{:S(2)}, u32[]{:S(2)}) collective-permute-start(bf16[128,512]{1,0:T(8,128)(2,1)S(1)} %collective-permute-done.refs_7_.refs_2_), channel_id=1, source_target_pairs={{0,6},{1,7},{2,4},{3,5},{4,2},{5,3},{6,0},{7,1},{8,14},{9,15},{10,... | collective-permute-start | bytes 393224 | tf_op jit(solution)/shard_map/ppermute | solution.py:44
  17.3 10.2 %collective-permute-start.2 = (bf16[128,512]{1,0:T(8,128)(2,1)S(1)}, bf16[128,512]{1,0:T(8,128)(2,1)S(1)}, u32[]{:S(2)}, u32[]{:S(2)}) collective-permute-start(bf16[128,512]{1,0:T(8,128)(2,1)S(1)} %collective-permute-done.refs_7_.refs_2_), channel_id=1, source_target_pairs={{0,4},{4,0},{8,12},{12,8},{16,20},{20,16},{24,28},{28,24},{1,5},{5... | collective-permute-start | bytes 393224 | tf_op jit(solution)/shard_map/ppermute | solution.py:34
  19.2 8.4 %collective-permute-start.1 = (bf16[128,512]{1,0:T(8,128)(2,1)S(1)}, bf16[128,512]{1,0:T(8,128)(2,1)S(1)}, u32[]{:S(2)}, u32[]{:S(2)}) collective-permute-start(bf16[128,512]{1,0:T(8,128)(2,1)S(1)} %collective-permute-done.refs_7_.refs_2_), channel_id=1, source_target_pairs={{0,2},{1,3},{2,0},{3,1},{4,6},{5,7},{6,4},{7,5},{8,10},{9,11},{10,... | collective-permute-start | bytes 393224 | tf_op jit(solution)/shard_map/ppermute | solution.py:34
  19.7 1.0 %copy-start.4 = (bf16[512,512]{1,0:T(8,128)(2,1)S(1)}, bf16[512,512]{1,0:T(8,128)(2,1)}, u32[]{:S(2)}) copy-start(bf16[512,512]{1,0:T(8,128)(2,1)} %refs_1_.1) | copy-start | bytes 1572868
  20.7 1.0 %copy-start.5 = (bf16[512,512]{1,0:T(8,128)(2,1)S(1)}, bf16[512,512]{1,0:T(8,128)(2,1)}, u32[]{:S(2)}) copy-start(bf16[512,512]{1,0:T(8,128)(2,1)} %refs_2_.2) | copy-start | bytes 1572868
  21.9 0.7 %copy-start.10 = (f32[8]{0:T(128)S(1)}, f32[8]{0:T(128)}, u32[]{:S(2)}) copy-start(f32[8]{0:T(128)} %softness_ref.1) | copy-start | bytes 100
  29.3 1.7 %collective-permute-start.11 = (bf16[256,640]{1,0:T(8,128)(2,1)S(1)}, bf16[256,640]{1,0:T(8,128)(2,1)S(1)}, u32[]{:S(2)}, u32[]{:S(2)}) collective-permute-start(bf16[256,640]{1,0:T(8,128)(2,1)S(1)} %get-tuple-element.29), channel_id=1, source_target_pairs={{0,1},{1,0},{2,3},{3,2},{4,5},{5,4},{6,7},{7,6},{8,9},{9,8},{10,11... | collective-permute-start | bytes 983048 | tf_op jit(solution)/shard_map/ppermute | solution.py:34
  31.0 2.5 %copy-start.2 = (bf16[1024,512]{1,0:T(8,128)(2,1)S(1)}, bf16[1024,512]{1,0:T(8,128)(2,1)}, u32[]{:S(2)}) copy-start(bf16[1024,512]{1,0:T(8,128)(2,1)} %refs_8_.1) | copy-start | bytes 3145732
  31.2 2.2 %copy-start.1 = (bf16[512,1024]{1,0:T(8,128)(2,1)S(1)}, bf16[512,1024]{1,0:T(8,128)(2,1)}, u32[]{:S(2)}) copy-start(bf16[512,1024]{1,0:T(8,128)(2,1)} %refs_7_.1) | copy-start | bytes 3145732
  31.3 2.2 %copy-start.6 = (bf16[16,128,128]{2,1,0:T(8,128)(2,1)S(1)}, bf16[16,128,128]{2,1,0:T(8,128)(2,1)}, u32[]{:S(2)}) copy-start(bf16[16,128,128]{2,1,0:T(8,128)(2,1)} %tiles_ref.1) | copy-start | bytes 1572868
  31.3 2.2 %collective-permute-start.13 = (bf16[640,512]{1,0:T(8,128)(2,1)S(1)}, bf16[640,512]{1,0:T(8,128)(2,1)S(1)}, u32[]{:S(2)}, u32[]{:S(2)}) collective-permute-start(bf16[640,512]{1,0:T(8,128)(2,1)S(1)} %lineup.3), channel_id=1, source_target_pairs={{0,1},{1,0},{2,3},{3,2},{4,5},{5,4},{6,7},{7,6},{8,9},{9,8},{10,11... | collective-permute-start | bytes 1966088 | tf_op jit(solution)/shard_map/ppermute | solution.py:34
  31.5 2.0 %copy-start.9 = (s32[1,1,12]{2,1,0:T(1,128)S(1)}, s32[1,1,12]{2,1,0:T(1,128)}, u32[]{:S(2)}) copy-start(s32[1,1,12]{2,1,0:T(1,128)} %param.12) | copy-start | bytes 148
  31.5 6.5 %collective-permute-start.12 = (bf16[128,640]{1,0:T(8,128)(2,1)S(1)}, bf16[128,640]{1,0:T(8,128)(2,1)S(1)}, u32[]{:S(2)}, u32[]{:S(2)}) collective-permute-start(bf16[128,640]{1,0:T(8,128)(2,1)S(1)} %get-tuple-element.32), channel_id=1, source_target_pairs={{0,8},{4,12},{8,0},{12,4},{16,24},{20,28},{24,16},{28,20},{1,9},{5... | collective-permute-start | bytes 491528 | tf_op jit(solution)/shard_map/ppermute | solution.py:34
  33.5 4.5 %copy-start.7 = (bf16[512,512]{1,0:T(8,128)(2,1)S(1)}, bf16[512,512]{1,0:T(8,128)(2,1)}, u32[]{:S(2)}) copy-start(bf16[512,512]{1,0:T(8,128)(2,1)} %final_ref.1) | copy-start | bytes 1572868
  35.0 3.0 %copy-start.8 = (f32[512]{0:T(512)S(1)}, f32[512]{0:T(512)}, u32[]{:S(2)}) copy-start(f32[512]{0:T(512)} %param.21) | copy-start | bytes 6148

commit v4 on v3

v4 whole, which is shorter than its diff:
```python
import functools
import math

import jax
import jax.numpy as jnp
from jax import lax
from jax.experimental import pallas as pl
from jax.experimental.pallas import tpu as pltpu
from jax.sharding import PartitionSpec as P

NUM_SUBSPACES = 8
SUBSPACE_WIDTH = 64
PAIRS = NUM_SUBSPACES // 2
PARTS = 2 * NUM_SUBSPACES
LANES = 128
norm_eps = 1e-06
VMEM = pl.BlockSpec(memory_space=pltpu.VMEM)
ANY = pl.BlockSpec(memory_space=pl.ANY)
F32 = jnp.float32
BF16 = jnp.bfloat16


def params(mebibytes):
    return pltpu.CompilerParams(vmem_limit_bytes=mebibytes << 20)


def cost(flops, transcendentals, data):
    return pl.CostEstimate(
        flops=flops // 16, transcendentals=transcendentals // 16, bytes_accessed=data // 16
    )


def swap(array, axis, mask):
    devices = lax.axis_size(axis)
    return lax.ppermute(array, axis, [(i, i ^ mask) for i in range(devices)])


def swap_both(array, dom_mask, head_mask):
    doms, heads = lax.axis_size("dom"), lax.axis_size("head")
    pairs = [
        (d * heads + h, (d ^ dom_mask) * heads + (h ^ head_mask))
        for d in range(doms)
        for h in range(heads)
    ]
    return lax.ppermute(array, ("dom", "head"), pairs)


def swap_by_core(array, first, second):
    doms, heads = lax.axis_size("dom"), lax.axis_size("head")
    pairs = []
    for d in range(doms):
        for h in range(heads):
            dom_mask, head_mask = second if h % 2 else first
            pairs.append((d * heads + h, (d ^ dom_mask) * heads + (h ^ head_mask)))
    return lax.ppermute(array, ("dom", "head"), pairs)


def dot(a, b):
    return jnp.dot(a, b, preferred_element_type=F32)


def dot_t(a, b):
    return lax.dot_general(a, b, (((1,), (1,)), ((), ())), preferred_element_type=F32)


def same_head(rows, cols, value):
    row = lax.broadcasted_iota(jnp.int32, (rows, cols), 0) // SUBSPACE_WIDTH
    col = lax.broadcasted_iota(jnp.int32, (rows, cols), 1) // SUBSPACE_WIDTH
    return jnp.where(row == col, value, 0.0).astype(BF16)


def head_normed(projected):
    block = same_head(256, 256, 1.0 / SUBSPACE_WIDTH)
    squares = (projected * projected).astype(BF16)
    mean = jnp.concatenate(
        [dot(squares[:, i : i + 256], block) for i in range(0, projected.shape[1], 256)], axis=1
    )
    return projected * lax.rsqrt(mean + norm_eps)


def padded_queries(queries, pair):
    both = queries[:, pair * LANES : (pair + 1) * LANES]
    first = lax.broadcasted_iota(jnp.int32, both.shape, 1) < SUBSPACE_WIDTH
    zero = jnp.zeros_like(both)
    return jnp.concatenate([jnp.where(first, both, zero), jnp.where(first, zero, both)], axis=0)


def attend(queries, keys_ref, values_ref):
    rows = queries.shape[0]
    count = keys_ref.shape[0]
    ones = jnp.ones((count, LANES), BF16)
    numer, denom = [], []
    first = lax.broadcasted_iota(jnp.int32, (rows, LANES), 1) < SUBSPACE_WIDTH
    for pair in range(PAIRS):
        cols = slice(pair * LANES, (pair + 1) * LANES)
        scores = dot_t(padded_queries(queries, pair), keys_ref[:, cols])
        weights = jnp.exp2(scores).astype(BF16)
        sums = dot(weights, jnp.concatenate([values_ref[:, cols], ones], axis=1))
        numer.append(jnp.where(first, sums[:rows, :LANES], sums[rows:, :LANES]))
        denom.append(jnp.where(first, sums[:rows, LANES:], sums[rows:, LANES:]))
    return jnp.concatenate(numer, axis=1), jnp.concatenate(denom, axis=1)


def keys_values(blocks, lookup_ref, content_ref, keys_ref, values_ref):
    nodes = jnp.concatenate(blocks, axis=0)
    keys_ref[...] = head_normed(dot(nodes, lookup_ref[...])).astype(BF16)
    values_ref[...] = dot(nodes, content_ref[...]).astype(BF16)


def lineup_kernel(count, rows, *refs):
    row = 0
    for block in refs[:count]:
        taken = min(block.shape[0], rows - row)
        refs[-1][row : row + taken, :] = block[:taken, :]
        row += taken


def lineup(blocks, after=(), rows=None, work=1 << 15):
    if rows is None:
        rows = sum(block.shape[0] for block in blocks)
    width = blocks[0].shape[1]
    return pl.pallas_call(
        functools.partial(lineup_kernel, len(blocks), rows),
        out_shape=jax.ShapeDtypeStruct((rows, width), BF16),
        in_specs=[VMEM] * len(blocks) + [ANY] * len(after),
        out_specs=VMEM,
        compiler_params=params(4),
        cost_estimate=pl.CostEstimate(flops=0, transcendentals=0, bytes_accessed=work),
        name="lineup",
    )(*blocks, *after)


def rows_kernel(start, block_ref, *refs):
    refs[-1][...] = block_ref[start : start + refs[-1].shape[0], :]


def rows_of(block, start, count, after=()):
    return pl.pallas_call(
        functools.partial(rows_kernel, start),
        out_shape=jax.ShapeDtypeStruct((count, block.shape[1]), BF16),
        in_specs=[VMEM] + [ANY] * len(after),
        out_specs=VMEM,
        compiler_params=params(4),
        cost_estimate=cost(0, 0, 1 << 19),
        name="rows",
    )(block, *after)


def near_kernel(softness_ref, both_ref, others_ref, *refs):
    blocks, (asking_ref, lookup_ref, content_ref) = refs[:-10], refs[-10:-7]
    queries_ref, keys_ref, values_ref, numer_ref, denom_ref, temper, sem = refs[-7:]
    half = both_ref.shape[0] // 2
    mine, theirs = slice(0, half), slice(half, 2 * half)
    copy = pltpu.make_async_copy(softness_ref, temper, sem)
    copy.start()
    nodes = [both_ref[mine, :]] + [block[...] for block in blocks]
    keys_values(nodes, lookup_ref, content_ref, keys_ref, values_ref)
    rows = jnp.concatenate(
        [others_ref[theirs, :], others_ref[mine, :], both_ref[theirs, :], both_ref[mine, :]], axis=0
    )
    projected = head_normed(dot(rows, asking_ref[...]))
    copy.wait()
    width = asking_ref.shape[1]
    head = lax.broadcasted_iota(jnp.int32, (1, width), 1) // SUBSPACE_WIDTH
    scale = jnp.zeros((1, width), F32)
    for h in range(NUM_SUBSPACES):
        scale = jnp.where(head == h, temper[h], scale)
    scale = scale * (math.log2(math.e) / math.sqrt(SUBSPACE_WIDTH))
    queries = (projected * scale).astype(BF16)
    queries_ref[...] = queries
    numer_ref[...], denom_ref[...] = attend(queries[: 2 * half], keys_ref, values_ref)


def near(softness, both, others, blocks, asking, lookup, content):
    rows, width = both.shape
    count = rows // 2 + sum(block.shape[0] for block in blocks)
    array = lambda n, dtype: jax.ShapeDtypeStruct((n, width), dtype)
    return pl.pallas_call(
        near_kernel,
        out_shape=(array(2 * rows, BF16),) + (array(count, BF16),) * 2 + (array(rows, F32),) * 2,
        in_specs=[ANY] + [VMEM] * (5 + len(blocks)),
        out_specs=(VMEM,) * 5,
        scratch_shapes=[pltpu.SMEM(softness.shape, F32), pltpu.SemaphoreType.DMA],
        compiler_params=params(16),
        cost_estimate=cost(6 * rows * count * width, rows * count * NUM_SUBSPACES, 4 << 20),
        name="near",
    )(softness, both, others, *blocks, asking, lookup, content)


def pack(numer, denom):
    lane = lax.broadcasted_iota(jnp.int32, (denom.shape[0], LANES), 1)
    sums = denom[:, :LANES]
    for pair in range(1, PAIRS):
        held = (lane % SUBSPACE_WIDTH) // 16 == pair
        sums = jnp.where(held, denom[:, pair * LANES : (pair + 1) * LANES], sums)
    high = sums.astype(BF16).astype(F32)
    sums = jnp.where(lane % 16 < 8, high, sums - high)
    return jnp.concatenate([numer.astype(BF16), sums.astype(BF16)], axis=1)


def unpack_denom(packed, width):
    lane = lax.broadcasted_iota(jnp.int32, (LANES, width), 0)
    col = lax.broadcasted_iota(jnp.int32, (LANES, width), 1)
    half = (col % LANES) // SUBSPACE_WIDTH
    source = half * SUBSPACE_WIDTH + (col // LANES) * 16
    spread = jnp.where((lane == source) | (lane == source + 8), 1.0, 0.0).astype(BF16)
    return dot(packed, spread)


def denom_rows(denom):
    row = lax.broadcasted_iota(jnp.int32, (PARTS, denom.shape[1]), 0)
    col = lax.broadcasted_iota(jnp.int32, (PARTS, denom.shape[1]), 1)
    high = denom.astype(BF16)
    low = (denom - high.astype(F32)).astype(BF16)
    first = jnp.where(col == row * SUBSPACE_WIDTH, 1.0, 0.0).astype(BF16)
    second = jnp.where(col == (row - NUM_SUBSPACES) * SUBSPACE_WIDTH, 1.0, 0.0).astype(BF16)
    return (dot_t(first, high) + dot_t(second, low)).astype(BF16)


def spread_denom(rows, width):
    row = lax.broadcasted_iota(jnp.int32, (PARTS, width), 0)
    head = lax.broadcasted_iota(jnp.int32, (PARTS, width), 1) // SUBSPACE_WIDTH
    spread = jnp.where(row % NUM_SUBSPACES == head, 1.0, 0.0).astype(BF16)
    return lax.dot_general(
        rows, spread, (((0,), (0,)), ((), ())), preferred_element_type=F32
    )


def call(kernel, steps, parts, wholes, out_parts, out_wholes, scratch, estimate, name, after=()):
    taken = len(parts) + len(wholes)

    def body(*refs):
        kernel(steps, *refs[:taken], *refs[taken + len(after) :])

    if steps == 1:
        grid, part, whole = (), lambda a: VMEM, lambda a: VMEM
    else:
        grid = (steps,)
        part = lambda a: pl.BlockSpec((a.shape[0] // steps,) + a.shape[1:], lambda i: (i, 0))
        whole = lambda a: pl.BlockSpec(a.shape, lambda i: (0, 0))
    return pl.pallas_call(
        body,
        grid=grid,
        out_shape=tuple(out_parts) + tuple(out_wholes),
        in_specs=[part(a) for a in parts] + [whole(a) for a in wholes] + [ANY] * len(after),
        out_specs=tuple(part(a) for a in out_parts) + tuple(whole(a) for a in out_wholes),
        scratch_shapes=scratch,
        compiler_params=params(16),
        cost_estimate=estimate,
        name=name,
    )(*parts, *wholes, *after)


def at_step(steps, step, body):
    if steps == 1:
        body()
    else:
        pl.when(pl.program_id(0) == step)(body)


def far_kernel(steps, *refs):
    blocks, (lookup_ref, content_ref, queries_ref, numer_ref, denom_ref) = refs[:-12], refs[-12:-7]
    keys_ref, values_ref, packed_ref, numer_out, denom_out, numer_sum, denom_sum = refs[-7:]
    pair = numer_ref.shape[0]
    half = pair // 2

    def start():
        numer_sum[...] = numer_ref[...]
        denom_sum[...] = denom_ref[...]

    def end():
        packed_ref[...] = pack(numer_sum[...], denom_sum[...])
        numer_out[...] = numer_sum[half:, :]
        denom_out[...] = denom_sum[half:, :]

    at_step(steps, 0, start)
    nodes = [block[...] for block in blocks]
    keys_values(nodes, lookup_ref, content_ref, keys_ref, values_ref)
    numer, denom = attend(queries_ref[:pair, :], keys_ref, values_ref)
    numer_sum[...] += numer
    denom_sum[...] += denom
    at_step(steps, steps - 1, end)


def far(blocks, block_len, lookup, content, queries, numer, denom):
    rows, width = numer.shape
    half = rows // 2
    count = len(blocks) * blocks[0].shape[0]
    kept = jax.ShapeDtypeStruct((count, width), BF16)
    return call(
        far_kernel,
        blocks[0].shape[0] // block_len,
        blocks,
        (lookup, content, queries, numer, denom),
        (kept, kept),
        (jax.ShapeDtypeStruct((rows, width + LANES), BF16),)
        + (jax.ShapeDtypeStruct((half, width), F32),) * 2,
        [pltpu.VMEM((rows, width), F32)] * 2,
        cost(6 * rows * count * width, rows * count * NUM_SUBSPACES, 4 << 20),
        "far",
    )


def own_kernel(steps, far_keys, far_values, queries_ref, near_keys, near_values, *refs):
    sent_ref, numer_out, denom_out, numer_sum, denom_sum = refs
    rows, width = numer_sum.shape
    half = rows // 2

    def start():
        numer_sum[...], denom_sum[...] = attend(queries_ref[rows:, :], near_keys, near_values)

    def end():
        sent_ref[:half, :] = numer_sum[:half, :].astype(BF16)
        sent_ref[half:, :] = jnp.zeros((PARTS, width), BF16)
        sent_ref[half:, :half] = denom_rows(denom_sum[:half, :])
        numer_out[...] = numer_sum[half:, :]
        denom_out[...] = denom_sum[half:, :]

    at_step(steps, 0, start)
    numer, denom = attend(queries_ref[rows:, :], far_keys, far_values)
    numer_sum[...] += numer
    denom_sum[...] += denom
    at_step(steps, steps - 1, end)


def own(far_keys, far_values, steps, queries, near_keys, near_values, after):
    rows, width = queries.shape[0] // 2, queries.shape[1]
    half = rows // 2
    return call(
        own_kernel,
        steps,
        (far_keys, far_values),
        (queries, near_keys, near_values),
        (),
        (jax.ShapeDtypeStruct((half + PARTS, width), BF16),)
        + (jax.ShapeDtypeStruct((half, width), F32),) * 2,
        [pltpu.VMEM((rows, width), F32)] * 2,
        cost(4 * rows * near_keys.shape[0] * width, 1 << 20, 4 << 20),
        "own",
        after,
    )


def combine_kernel(numer_ref, denom_ref, packed_ref, packed_out):
    rows, width = numer_ref.shape
    numer = numer_ref[...] + packed_ref[:rows, :width].astype(F32)
    denom = denom_ref[...] + unpack_denom(packed_ref[:rows, width:], width)
    packed_out[...] = pack(numer, denom)


def combine(numer, denom, packed):
    return pl.pallas_call(
        combine_kernel,
        out_shape=jax.ShapeDtypeStruct((numer.shape[0], packed.shape[1]), BF16),
        in_specs=[VMEM] * 3,
        out_specs=VMEM,
        compiler_params=params(8),
        cost_estimate=cost(4 * packed.shape[0] * packed.shape[1] * LANES, 0, 1 << 20),
        name="combine",
    )(numer, denom, packed)


def message_kernel(slots_ref, tiles_ref, *refs):
    both_ref, side_ref, across_ref, halo_ref, got_ref, *got_halo = refs[:8]
    inner_ref, outer_ref, gain_ref, local_ref, gain_out, slots, sem = refs[8:]
    gain_out[...] = gain_ref[...]
    copy = pltpu.make_async_copy(slots_ref, slots, sem)
    copy.start()
    group = slots_ref.shape[0] // 3
    me, core, odd = lax.axis_index("head"), lax.axis_index("head") % 2, lax.axis_index("dom") % 2
    beside, beyond = 2 - 2 * odd, 2 * odd
    part, parts = lax.axis_index("dom"), lax.axis_size("dom")
    outside = (part == 0) | (part == parts - 1)
    pick = lambda first, second: first + core * (second - first)
    order = [(1, 0), (1, 1)]
    order += [(pick(beside, 1), pick(0, 2)), (pick(beside, 1), pick(1, 3)), (beside, 2)]
    order += [(pick(1, beside), pick(3, 1)), (pick(1, beside), pick(2, 0)), (beside, 3)]
    order += [(beyond, core), (beyond, 1 - core), (beyond, 2), (beyond, 3)]
    rows = across_ref.shape[0]
    kept = halo_ref[: 2 * rows, :]
    sent = jnp.concatenate([got_halo[0][...], got_halo[1][...]], axis=0)
    nodes = [both_ref[...], side_ref[...], across_ref[...], got_ref[...]]
    nodes += [jnp.where(core == 0, kept, sent), halo_ref[2 * rows :, :], got_halo[2][...]]
    copy.wait()
    tiles = []
    for side, offset in order:
        tile_id = slots[side * group + (me ^ offset)]
        tile_id = jnp.where(outside & (side == beyond), -1, tile_id)
        tile = tiles_ref[jnp.maximum(tile_id, 0)]
        tiles.append(jnp.where(tile_id >= 0, tile, jnp.zeros_like(tile)))
    aggregate = dot(jnp.concatenate(tiles, axis=1), jnp.concatenate(nodes, axis=0)).astype(BF16)
    hidden = jax.nn.gelu(dot(aggregate, inner_ref[...])).astype(BF16)
    local_ref[...] = dot(hidden, outer_ref[...])


def message(slots, tiles, blocks, inner, outer, gain):
    rows, width, hidden = tiles.shape[1], inner.shape[0], inner.shape[1]
    return pl.pallas_call(
        message_kernel,
        out_shape=(jax.ShapeDtypeStruct((rows, width), F32), jax.ShapeDtypeStruct(gain.shape, F32)),
        in_specs=[ANY] + [VMEM] * (4 + len(blocks)),
        out_specs=(VMEM,) * 2,
        scratch_shapes=[pltpu.SMEM(slots.shape, jnp.int32), pltpu.SemaphoreType.DMA],
        compiler_params=params(16),
        cost_estimate=cost(
            2 * rows * width * (12 * rows + 2 * hidden), rows * hidden, 4 << 20
        ),
        name="message",
    )(slots, tiles, *blocks, inner, outer, gain)


def finish_kernel(
    numer_ref, denom_ref, crossed_ref, packed_ref, final_ref, gain_ref, local_ref, nodes_ref, out_ref
):
    width = numer_ref.shape[1]
    rows = numer_ref.shape[0]
    numer = numer_ref[...] + crossed_ref[:rows, :].astype(F32) + packed_ref[:, :width].astype(F32)
    denom = denom_ref[...] + spread_denom(crossed_ref[rows:, :rows], width)
    denom += unpack_denom(packed_ref[:, width:], width)
    mixed = (numer / denom).astype(BF16)
    attended = dot(mixed, final_ref[...])
    mean = jnp.mean(attended * attended, axis=-1, keepdims=True)
    normed = attended * lax.rsqrt(mean + norm_eps) * gain_ref[...]
    out_ref[...] = (nodes_ref[...].astype(F32) + local_ref[...] + normed).astype(BF16)


def finish(numer, denom, crossed, packed, final, gain, local, nodes):
    rows, width = nodes.shape
    return pl.pallas_call(
        finish_kernel,
        out_shape=jax.ShapeDtypeStruct((rows, width), BF16),
        in_specs=[VMEM] * 8,
        out_specs=VMEM,
        compiler_params=params(16),
        cost_estimate=cost(2 * rows * width * width, rows, 2 << 20),
        name="finish",
    )(numer, denom, crossed, packed, final, gain, local, nodes)


def shards(
    vertex_embeddings,
    adjacent_group_bank_ids,
    coupling_strength_panels,
    asking_projector,
    lookup_projector,
    content_projector,
    final_projector,
    passing_inner_coefficients,
    passing_outer_coefficients,
    softness_per_subspace,
    mixing_layer_gain,
):
    block_len = vertex_embeddings.shape[0]
    doms = lax.axis_size("dom")
    nodes = vertex_embeddings
    stacked = lambda *arrays: jnp.concatenate(arrays, axis=0)

    distant = swap(nodes, "dom", 4)
    mask = 8
    while mask < doms:
        distant = stacked(distant, swap(stacked(nodes, distant), "dom", mask))
        mask *= 2

    def plane(block):
        side = swap(block, "dom", 1)
        below = swap(block, "head", 2)
        across = swap_both(block, 1, 2)
        return below, side, across

    held = lineup((nodes,))
    if distant.shape[0] == block_len:
        distant = lineup((distant,), work=20 << 20)
    both = lineup((held, swap(nodes, "head", 1)))
    side = swap_by_core(both, (1, 0), (0, 2))
    across = swap_by_core(lineup((side,), (), block_len), (0, 2), (1, 0))
    other = swap(nodes, "dom", 2)
    others = lineup((other, swap(other, "head", 1)))
    far_blocks = plane(distant)
    steps = distant.shape[0] // block_len
    if steps == 1:
        early = (side, across, distant)
    else:
        early, far_blocks = (side, across), (distant,) + far_blocks
    queries, keys, values, numer, denom = near(
        softness_per_subspace,
        both,
        others,
        early,
        asking_projector,
        lookup_projector,
        content_projector,
    )

    pairs = [(p, p + 2) for p in range(0, doms - 2, 2)] + [(p, p - 2) for p in range(3, doms, 2)]
    halo = lax.ppermute(lineup((side, across), ()), "dom", pairs)
    far_keys, far_values, packed, numer, denom = far(
        far_blocks, block_len, lookup_projector, content_projector, queries, numer, denom
    )
    packed = packed_here = combine(numer, denom, swap(packed, "head", 1))
    crossed, numer, denom = own(far_keys, far_values, steps, queries, keys, values, (packed,))
    crossed = swap(crossed, "head", 1)
    packed = swap(packed, "dom", 2)
    got = swap(lineup((side, across)), "head", 1)
    got_halo = [
        swap(rows_of(halo, at * block_len, block_len, (numer,)), "head", 1) for at in range(3)
    ]
    local, gain = message(
        adjacent_group_bank_ids.reshape(-1),
        coupling_strength_panels,
        (both, side, across, halo, got, *got_halo),
        passing_inner_coefficients,
        passing_outer_coefficients,
        mixing_layer_gain.reshape(1, -1),
    )
    return finish(
        numer, denom, crossed, packed, final_projector, gain, local, held
    )


def solution(mesh):
    in_specs = (P(("dom", "head"), None), P("dom", "head", None)) + (P(),) * 9
    out_specs = P(("dom", "head"), None)
    return jax.shard_map(shards, mesh=mesh, in_specs=in_specs, out_specs=out_specs, check_vma=False)
```

time: 39.4 us -> 38 us (0.964)
  waiting for transfers between devices: 8.67 us -> 6.59 us
  starting transfers between devices: 16.7 us -> 18 us
  local copies, waits for them, and re-layouts: 2.77 us -> 1.58 us
  Pallas kernels: 10.8 us -> 11.3 us
    ppermute x1 -> x3, starting transfers between devices: 2.65 us -> 7.4 us  [the longest x2 5.03 us: swap_by_core(): return lax.ppermute(array, ('dom', 'head'), pairs)]
    ppermute x3 -> x1, starting transfers between devices: 5.09 us -> 1.49 us  [swap_both(): return lax.ppermute(array, ('dom', 'head'), pairs)]
    ppermute x10 -> x13, waiting for transfers between devices: 8.66 us -> 6.4 us  [swap(): return lax.ppermute(array, axis, [(i, i ^ mask) for i in range(devices)])]
    pallas_call x2, Pallas kernels: 2.82 us -> 4.64 us  [call(): pl.pallas_call(body, grid=grid, out_shape=tuple(out_parts) + tuple(out_wh...]
    pallas_call x6 -> x12, Pallas kernels: 6.85 us -> 5.45 us  [the longest x1 3.65 us: near(): pl.pallas_call(near_kernel, out_shape=(array(2 * rows, BF16),) + (array(c...]
    unnamed x22, local copies, waits for them, and re-layouts: 2.77 us -> 1.58 us
    ppermute x10 -> x13, starting transfers between devices: 8.95 us -> 9.06 us  [swap(): return lax.ppermute(array, axis, [(i, i ^ mask) for i in range(devices)])]
  transfers between devices with their start and end apart: 14 -> 17, of which waited for: 5 -> 8; matrix products, arithmetic and copies ran while one was open for 0% -> 0% of each run, Pallas kernels for 20% -> 27%
where the time goes in v4:
time: 38 us; the launch traced here: 37.7 us
  starting transfers between devices  18 us (47%)
  Pallas kernels  11.3 us (30%)
  waiting for transfers between devices  6.59 us (17%)
  local copies, waits for them, and re-layouts  1.58 us (4%)
    ppermute x13, starting transfers between devices, swap(): return lax.ppermute(array, axis, [(i, i ^ mask) for i in range(devices)])  9.06 us
    ppermute x13, waiting for transfers between devices, swap(): return lax.ppermute(array, axis, [(i, i ^ mask) for i in range(devices)])  6.4 us
    ppermute x2, starting transfers between devices, swap_by_core(): return lax.ppermute(array, ('dom', 'head'), pairs)  5.03 us
    pallas_call x2, Pallas kernels, call(): pl.pallas_call(body, grid=grid, out_shape=tuple(out_parts) + tuple(out_wh...  4.64 us
    pallas_call x1, Pallas kernels, near(): pl.pallas_call(near_kernel, out_shape=(array(2 * rows, BF16),) + (array(c...  3.65 us
    ppermute x1, starting transfers between devices, shards(): halo = lax.ppermute(lineup((side, across), ()), 'dom', pairs)  2.38 us
    unnamed x22, local copies, waits for them, and re-layouts  1.58 us
    ppermute x1, starting transfers between devices, swap_both(): return lax.ppermute(array, ('dom', 'head'), pairs)  1.49 us
  transfers between devices with their start and end apart: 17, of which 8 were waited for; matrix products, arithmetic and copies ran while one was open for 0% of the time, Pallas kernels for 27%

profile of v4, /device:TPU:0, one launch (start us, length us, event | category | flops | bytes accessed | tf_op | source)
XLA Modules:
  0.0 37.7 jit_solution(1644991299165793757)
XLA Ops:
  0.0 0.5 %collective-permute-start.4 = (bf16[128,512]{1,0:T(8,128)(2,1)}, bf16[128,512]{1,0:T(8,128)(2,1)S(1)}, u32[]{:S(2)}, u32[]{:S(2)}) collective-permute-start(bf16[128,512]{1,0:T(8,128)(2,1)} %refs_0_.1), channel_id=1, source_target_pairs={{0,1},{1,0},{2,3},{3,2},{4,5},{5,4},{6,7},{7,6},{8,9},{9,8},{10,11... | collective-permute-start | bytes 393224 | tf_op jit(solution)/shard_map/ppermute | solution.py:35
  0.5 0.9 %copy-done.7 = bf16[128,512]{1,0:T(8,128)(2,1)S(1)} copy-done((bf16[128,512]{1,0:T(8,128)(2,1)S(1)}, bf16[128,512]{1,0:T(8,128)(2,1)}, u32[]{:S(2)}) %copy-start.7) | copy-done | bytes 131096
  1.4 0.3 collective-permute-done.4.refs_1_
  1.7 2.9 %collective-permute-start.7 = (bf16[256,512]{1,0:T(8,128)(2,1)S(1)}, bf16[256,512]{1,0:T(8,128)(2,1)S(1)}, u32[]{:S(2)}, u32[]{:S(2)}) collective-permute-start(bf16[256,512]{1,0:T(8,128)(2,1)S(1)} %lineup.8.both_ref.refs_0_), channel_id=1, source_target_pairs={{0,4},{1,3},{2,6},{3,1},{4,0},{5,7},{6,2},{7,5},{8,12},{9,11},{10,... | collective-permute-start | bytes 786440 | tf_op jit(solution)/shard_map/ppermute | solution.py:55
  4.6 1.6 %collective-permute-start.5 = (bf16[128,512]{1,0:T(8,128)(2,1)S(1)}, bf16[128,512]{1,0:T(8,128)(2,1)S(1)}, u32[]{:S(2)}, u32[]{:S(2)}) collective-permute-start(bf16[128,512]{1,0:T(8,128)(2,1)S(1)} %copy-done.7), channel_id=1, source_target_pairs={{0,8},{4,12},{8,0},{12,4},{16,24},{20,28},{24,16},{28,20},{1,9},{5... | collective-permute-start | bytes 393224 | tf_op jit(solution)/shard_map/ppermute | solution.py:35
  6.2 2.6 %collective-permute-start = (bf16[128,512]{1,0:T(8,128)(2,1)S(1)}, bf16[128,512]{1,0:T(8,128)(2,1)S(1)}, u32[]{:S(2)}, u32[]{:S(2)}) collective-permute-start(bf16[128,512]{1,0:T(8,128)(2,1)S(1)} %copy-done.7), channel_id=1, source_target_pairs={{0,16},{4,20},{8,24},{12,28},{16,0},{20,4},{24,8},{28,12},{1,17},{... | collective-permute-start | bytes 393224 | tf_op jit(solution)/shard_map/ppermute | solution.py:35
  8.8 0.2 collective-permute-done.7.refs_0_.refs_1_
  9.0 2.1 %collective-permute-start.8 = (bf16[128,512]{1,0:T(8,128)(2,1)S(1)}, bf16[128,512]{1,0:T(8,128)(2,1)S(1)}, u32[]{:S(2)}, u32[]{:S(2)}) collective-permute-start(bf16[128,512]{1,0:T(8,128)(2,1)S(1)} %lineup.10), channel_id=1, source_target_pairs={{0,2},{1,5},{2,0},{3,7},{4,6},{5,1},{6,4},{7,3},{8,10},{9,13},{10,... | collective-permute-start | bytes 393224 | tf_op jit(solution)/shard_map/ppermute | solution.py:55
  11.1 0.9 %collective-permute-done.5.refs_0_ = bf16[128,512]{1,0:T(8,128)(2,1)S(1)} collective-permute-done((bf16[128,512]{1,0:T(8,128)(2,1)S(1)}, bf16[128,512]{1,0:T(8,128)(2,1)S(1)}, u32[]{:S(2)}, u32[]{:S(2)}) %collective-permute-start.5) | collective-permute-done | bytes 131104 | tf_op jit(solution)/shard_map/ppermute | solution.py:35
  12.0 0.0 collective-permute-start.6
  12.0 3.0 %collective-permute-done.refs_0_ = bf16[128,512]{1,0:T(8,128)(2,1)S(1)} collective-permute-done((bf16[128,512]{1,0:T(8,128)(2,1)S(1)}, bf16[128,512]{1,0:T(8,128)(2,1)S(1)}, u32[]{:S(2)}, u32[]{:S(2)}) %collective-permute-start) | collective-permute-done | bytes 131104 | tf_op jit(solution)/shard_map/ppermute | solution.py:35
  15.0 0.0 copy-start
  15.0 0.0 copy-start.1
  15.0 0.6 %collective-permute-start.1 = (bf16[128,512]{1,0:T(8,128)(2,1)S(1)}, bf16[128,512]{1,0:T(8,128)(2,1)S(1)}, u32[]{:S(2)}, u32[]{:S(2)}) collective-permute-start(bf16[128,512]{1,0:T(8,128)(2,1)S(1)} %lineup.6.refs_2_), channel_id=1, source_target_pairs={{0,2},{1,3},{2,0},{3,1},{4,6},{5,7},{6,4},{7,5},{8,10},{9,11},{10,... | collective-permute-start | bytes 393224 | tf_op jit(solution)/shard_map/ppermute | solution.py:35
  15.5 1.5 %collective-permute-start.2 = (bf16[128,512]{1,0:T(8,128)(2,1)S(1)}, bf16[128,512]{1,0:T(8,128)(2,1)S(1)}, u32[]{:S(2)}, u32[]{:S(2)}) collective-permute-start(bf16[128,512]{1,0:T(8,128)(2,1)S(1)} %lineup.6.refs_2_), channel_id=1, source_target_pairs={{0,4},{4,0},{8,12},{12,8},{16,20},{20,16},{24,28},{28,24},{1,5},{5... | collective-permute-start | bytes 393224 | tf_op jit(solution)/shard_map/ppermute | solution.py:35
  17.0 1.5 %collective-permute-start.3 = (bf16[128,512]{1,0:T(8,128)(2,1)S(1)}, bf16[128,512]{1,0:T(8,128)(2,1)S(1)}, u32[]{:S(2)}, u32[]{:S(2)}) collective-permute-start(bf16[128,512]{1,0:T(8,128)(2,1)S(1)} %lineup.6.refs_2_), channel_id=1, source_target_pairs={{0,6},{1,7},{2,4},{3,5},{4,2},{5,3},{6,0},{7,1},{8,14},{9,15},{10,... | collective-permute-start | bytes 393224 | tf_op jit(solution)/shard_map/ppermute | solution.py:45
  18.5 0.0 collective-permute-done.8.refs_1_.refs_2_
  18.6 2.4 %collective-permute-start.12 = (bf16[384,512]{1,0:T(8,128)(2,1)S(1)}, bf16[384,512]{1,0:T(8,128)(2,1)S(1)}, u32[]{:S(2)}, u32[]{:S(2)}) collective-permute-start(bf16[384,512]{1,0:T(8,128)(2,1)S(1)} %lineup.11), channel_id=1, source_target_pairs={{0,8},{8,16},{16,24},{12,4},{20,12},{28,20},{1,9},{9,17},{17,25},{... | collective-permute-start | bytes 1179656 | tf_op jit(solution)/shard_map/ppermute | solution.py:495
  20.9 0.0 collective-permute-done.6.refs_1_
  21.0 0.1 collective-permute-start.13
  21.1 0.0 copy-done.10
  21.1 0.0 copy-done.6
  21.1 3.6 %near.1 = (bf16[512,512]{1,0:T(8,128)(2,1)S(1)}, bf16[640,512]{1,0:T(8,128)(2,1)S(1)}, bf16[640,512]{1,0:T(8,128)(2,1)S(1)}, f32[256,512]{1,0:T(8,128)S(1)}, f32[256,512]{1,0:T(8,128)S(1)}) custom-call(f32[8]{0:T(128)S(1)} %copy-done.10, bf16[256,512]{1,0:T(8,128)(2,1)S(1)} %lineup.8.both_ref.refs_0_, bf16[256,512]{1,0:T(8,128)(2,1)S(1)} %lineup.9.others_ref, ...), custom_call_target="tpu_custom_call" | custom-call | flops 31457280 | bytes 262144 | tf_op jit(solution)/shard_map/near/pallas_call | solution.py:178
  24.8 0.0 collective-permute-done.1.refs_0_
  24.8 0.0 collective-permute-done.2.refs_1_
  24.8 0.0 collective-permute-done.3.refs_2_
  24.8 1.7 %far.1 = (bf16[384,512]{1,0:T(8,128)(2,1)S(1)}, bf16[384,512]{1,0:T(8,128)(2,1)S(1)}, bf16[256,640]{1,0:T(8,128)(2,1)S(1)}, f32[128,512]{1,0:T(8,128)S(1)}, f32[128,512]{1,0:T(8,128)S(1)}) custom-call(bf16[128,512]{1,0:T(8,128)(2,1)S(1)} %collective-permute-done.1.refs_0_, bf16[128,512]{1,0:T(8,128)(2,1)S(1)} %collective-permute-done.2.refs_1_, ...), custom_call_target="tpu_custom_call" | custom-call | flops 18874368 | bytes 262144 | tf_op jit(solution)/shard_map/far/pallas_call | solution.py:241
  26.5 0.6 %collective-permute-start.9 = (bf16[256,640]{1,0:T(8,128)(2,1)S(1)}, bf16[256,640]{1,0:T(8,128)(2,1)S(1)}, u32[]{:S(2)}, u32[]{:S(2)}) collective-permute-start(bf16[256,640]{1,0:T(8,128)(2,1)S(1)} %get-tuple-element.29), channel_id=1, source_target_pairs={{0,1},{1,0},{2,3},{3,2},{4,5},{5,4},{6,7},{7,6},{8,9},{9,8},{10,11... | collective-permute-start | bytes 983048 | tf_op jit(solution)/shard_map/ppermute | solution.py:35
  27.1 1.3 %collective-permute-done.9.packed_ref = bf16[256,640]{1,0:T(8,128)(2,1)S(1)} collective-permute-done((bf16[256,640]{1,0:T(8,128)(2,1)S(1)}, bf16[256,640]{1,0:T(8,128)(2,1)S(1)}, u32[]{:S(2)}, u32[]{:S(2)}) %collective-permute-start.9) | collective-permute-done | bytes 327712 | tf_op jit(solution)/shard_map/ppermute | solution.py:35
  28.3 0.2 combine.1.refs_5_
  28.6 0.5 %collective-permute-start.11 = (bf16[128,640]{1,0:T(8,128)(2,1)S(1)}, bf16[128,640]{1,0:T(8,128)(2,1)S(1)}, u32[]{:S(2)}, u32[]{:S(2)}) collective-permute-start(bf16[128,640]{1,0:T(8,128)(2,1)S(1)} %combine.1.refs_5_), channel_id=1, source_target_pairs={{0,8},{4,12},{8,0},{12,4},{16,24},{20,28},{24,16},{28,20},{1,9},{5... | collective-permute-start | bytes 491528 | tf_op jit(solution)/shard_map/ppermute | solution.py:35
  29.1 2.9 %own.1 = (bf16[144,512]{1,0:T(8,128)(2,1)S(1)}, f32[128,512]{1,0:T(8,128)S(1)}, f32[128,512]{1,0:T(8,128)S(1)}) custom-call(bf16[384,512]{1,0:T(8,128)(2,1)S(1)} %get-tuple-element.23.refs_0_, bf16[384,512]{1,0:T(8,128)(2,1)S(1)} %get-tuple-element.24.refs_1_, bf16[512,512]{1,0:T(8,128)(2,1)S(1)} %get-tuple-element.20.refs_5_.refs_2_, ...), custom_call_target="tpu_custom_call" | custom-call | flops 20971520 | bytes 262144 | tf_op jit(solution)/shard_map/own/pallas_call | solution.py:241
  32.0 0.1 collective-permute-start.10
  32.1 0.0 collective-permute-done.12.block_ref.refs_3_
  32.1 0.5 %collective-permute-start.16 = (bf16[128,512]{1,0:T(8,128)(2,1)S(1)}, bf16[128,512]{1,0:T(8,128)(2,1)S(1)}, u32[]{:S(2)}, u32[]{:S(2)}) collective-permute-start(bf16[128,512]{1,0:T(8,128)(2,1)S(1)} %rows.5), channel_id=1, source_target_pairs={{0,1},{1,0},{2,3},{3,2},{4,5},{5,4},{6,7},{7,6},{8,9},{9,8},{10,11... | collective-permute-start | bytes 393224 | tf_op jit(solution)/shard_map/ppermute | solution.py:35
  32.6 0.2 collective-permute-start.15
  32.8 0.0 copy-start.8
  32.8 0.0 collective-permute-done.13.refs_4_
  32.8 0.5 %collective-permute-start.14 = (bf16[128,512]{1,0:T(8,128)(2,1)S(1)}, bf16[128,512]{1,0:T(8,128)(2,1)S(1)}, u32[]{:S(2)}, u32[]{:S(2)}) collective-permute-start(bf16[128,512]{1,0:T(8,128)(2,1)S(1)} %rows.3), channel_id=1, source_target_pairs={{0,1},{1,0},{2,3},{3,2},{4,5},{5,4},{6,7},{7,6},{8,9},{9,8},{10,11... | collective-permute-start | bytes 393224 | tf_op jit(solution)/shard_map/ppermute | solution.py:35
  33.3 0.3 collective-permute-done.16.refs_7_
  33.6 0.4 %collective-permute-done.15.refs_6_ = bf16[128,512]{1,0:T(8,128)(2,1)S(1)} collective-permute-done((bf16[128,512]{1,0:T(8,128)(2,1)S(1)}, bf16[128,512]{1,0:T(8,128)(2,1)S(1)}, u32[]{:S(2)}, u32[]{:S(2)}) %collective-permute-start.15) | collective-permute-done | bytes 131104 | tf_op jit(solution)/shard_map/ppermute | solution.py:35
  34.0 0.2 collective-permute-done.14.refs_5_
  34.3 0.0 copy-done.4
  34.3 0.6 %copy-done.9 = s32[1,1,12]{2,1,0:T(1,128)S(1)} copy-done((s32[1,1,12]{2,1,0:T(1,128)S(1)}, s32[1,1,12]{2,1,0:T(1,128)}, u32[]{:S(2)}) %copy-start.9) | copy-done | bytes 72
  35.0 1.5 %message.1 = (f32[128,512]{1,0:T(8,128)S(1)}, f32[1,512]{1,0:T(1,128)S(1)}) custom-call(s32[12]{0:T(128)S(1)} %bitcast.3, bf16[16,128,128]{2,1,0:T(8,128)(2,1)S(1)} %copy-done.4, bf16[256,512]{1,0:T(8,128)(2,1)S(1)} %lineup.8.both_ref.refs_0_, bf16[256,512]{1,0:T(8,128)(2,1)S(1)} %collective-permute-done.7.refs_0_.refs_1_, ...), custom_call_target="tpu_custom_call" | custom-call | flops 29360128 | bytes 262144 | tf_op jit(solution)/shard_map/message/pallas_call | solution.py:398
  36.4 0.0 collective-permute-done.10.crossed_ref
  36.4 0.0 collective-permute-done.11.packed_ref
  36.4 1.2 %finish.1 = bf16[128,512]{1,0:T(8,128)(2,1)} custom-call(f32[128,512]{1,0:T(8,128)S(1)} %get-tuple-element.30.refs_0_.numer_ref, f32[128,512]{1,0:T(8,128)S(1)} %get-tuple-element.31.denom_ref, bf16[144,512]{1,0:T(8,128)(2,1)S(1)} %collective-permute-done.10.crossed_ref, bf16[128,640]{1,0:T(8,128)(2,1)S(1)} %collective-permute-done.11.packed_ref, ...), custom_call_target="tpu_custom_call" | custom-call | flops 4194304 | bytes 131072 | tf_op jit(solution)/shard_map/finish/pallas_call | solution.py:429
  (23 shorter events, 0.1 us)
Async XLA Ops:
  0.0 1.6 %collective-permute-start.4 = (bf16[128,512]{1,0:T(8,128)(2,1)}, bf16[128,512]{1,0:T(8,128)(2,1)S(1)}, u32[]{:S(2)}, u32[]{:S(2)}) collective-permute-start(bf16[128,512]{1,0:T(8,128)(2,1)} %refs_0_.1), channel_id=1, source_target_pairs={{0,1},{1,0},{2,3},{3,2},{4,5},{5,4},{6,7},{7,6},{8,9},{9,8},{10,11... | collective-permute-start | bytes 393224 | tf_op jit(solution)/shard_map/ppermute | solution.py:35
  0.5 0.9 %copy-start.7 = (bf16[128,512]{1,0:T(8,128)(2,1)S(1)}, bf16[128,512]{1,0:T(8,128)(2,1)}, u32[]{:S(2)}) copy-start(bf16[128,512]{1,0:T(8,128)(2,1)} %refs_0_.1) | copy-start | bytes 393220
  1.7 7.3 %collective-permute-start.7 = (bf16[256,512]{1,0:T(8,128)(2,1)S(1)}, bf16[256,512]{1,0:T(8,128)(2,1)S(1)}, u32[]{:S(2)}, u32[]{:S(2)}) collective-permute-start(bf16[256,512]{1,0:T(8,128)(2,1)S(1)} %lineup.8.both_ref.refs_0_), channel_id=1, source_target_pairs={{0,4},{1,3},{2,6},{3,1},{4,0},{5,7},{6,2},{7,5},{8,12},{9,11},{10,... | collective-permute-start | bytes 786440 | tf_op jit(solution)/shard_map/ppermute | solution.py:55
  4.6 7.4 %collective-permute-start.5 = (bf16[128,512]{1,0:T(8,128)(2,1)S(1)}, bf16[128,512]{1,0:T(8,128)(2,1)S(1)}, u32[]{:S(2)}, u32[]{:S(2)}) collective-permute-start(bf16[128,512]{1,0:T(8,128)(2,1)S(1)} %copy-done.7), channel_id=1, source_target_pairs={{0,8},{4,12},{8,0},{12,4},{16,24},{20,28},{24,16},{28,20},{1,9},{5... | collective-permute-start | bytes 393224 | tf_op jit(solution)/shard_map/ppermute | solution.py:35
  6.2 8.8 %collective-permute-start = (bf16[128,512]{1,0:T(8,128)(2,1)S(1)}, bf16[128,512]{1,0:T(8,128)(2,1)S(1)}, u32[]{:S(2)}, u32[]{:S(2)}) collective-permute-start(bf16[128,512]{1,0:T(8,128)(2,1)S(1)} %copy-done.7), channel_id=1, source_target_pairs={{0,16},{4,20},{8,24},{12,28},{16,0},{20,4},{24,8},{28,12},{1,17},{... | collective-permute-start | bytes 393224 | tf_op jit(solution)/shard_map/ppermute | solution.py:35
  8.9 12.1 %copy-start.10 = (f32[8]{0:T(128)S(1)}, f32[8]{0:T(128)}, u32[]{:S(2)}) copy-start(f32[8]{0:T(128)} %softness_ref.1) | copy-start | bytes 100
  9.0 9.6 %collective-permute-start.8 = (bf16[128,512]{1,0:T(8,128)(2,1)S(1)}, bf16[128,512]{1,0:T(8,128)(2,1)S(1)}, u32[]{:S(2)}, u32[]{:S(2)}) collective-permute-start(bf16[128,512]{1,0:T(8,128)(2,1)S(1)} %lineup.10), channel_id=1, source_target_pairs={{0,2},{1,5},{2,0},{3,7},{4,6},{5,1},{6,4},{7,3},{8,10},{9,13},{10,... | collective-permute-start | bytes 393224 | tf_op jit(solution)/shard_map/ppermute | solution.py:55
  12.0 9.0 %collective-permute-start.6 = (bf16[128,512]{1,0:T(8,128)(2,1)S(1)}, bf16[128,512]{1,0:T(8,128)(2,1)S(1)}, u32[]{:S(2)}, u32[]{:S(2)}) collective-permute-start(bf16[128,512]{1,0:T(8,128)(2,1)S(1)} %collective-permute-done.5.refs_0_), channel_id=1, source_target_pairs={{0,1},{1,0},{2,3},{3,2},{4,5},{5,4},{6,7},{7,6},{8,9},{9,8},{10,11... | collective-permute-start | bytes 393224 | tf_op jit(solution)/shard_map/ppermute | solution.py:35
  14.9 6.1 %copy-start.6 = (bf16[512,512]{1,0:T(8,128)(2,1)S(1)}, bf16[512,512]{1,0:T(8,128)(2,1)}, u32[]{:S(2)}) copy-start(bf16[512,512]{1,0:T(8,128)(2,1)} %refs_3_.2) | copy-start | bytes 1572868
  15.0 6.1 %copy-start = (bf16[512,512]{1,0:T(8,128)(2,1)S(1)}, bf16[512,512]{1,0:T(8,128)(2,1)}, u32[]{:S(2)}) copy-start(bf16[512,512]{1,0:T(8,128)(2,1)} %refs_3_.3) | copy-start | bytes 1572868
  15.0 6.1 %copy-start.1 = (bf16[512,512]{1,0:T(8,128)(2,1)S(1)}, bf16[512,512]{1,0:T(8,128)(2,1)}, u32[]{:S(2)}) copy-start(bf16[512,512]{1,0:T(8,128)(2,1)} %refs_4_.3) | copy-start | bytes 1572868
  15.0 9.8 %collective-permute-start.1 = (bf16[128,512]{1,0:T(8,128)(2,1)S(1)}, bf16[128,512]{1,0:T(8,128)(2,1)S(1)}, u32[]{:S(2)}, u32[]{:S(2)}) collective-permute-start(bf16[128,512]{1,0:T(8,128)(2,1)S(1)} %lineup.6.refs_2_), channel_id=1, source_target_pairs={{0,2},{1,3},{2,0},{3,1},{4,6},{5,7},{6,4},{7,5},{8,10},{9,11},{10,... | collective-permute-start | bytes 393224 | tf_op jit(solution)/shard_map/ppermute | solution.py:35
  15.5 9.2 %collective-permute-start.2 = (bf16[128,512]{1,0:T(8,128)(2,1)S(1)}, bf16[128,512]{1,0:T(8,128)(2,1)S(1)}, u32[]{:S(2)}, u32[]{:S(2)}) collective-permute-start(bf16[128,512]{1,0:T(8,128)(2,1)S(1)} %lineup.6.refs_2_), channel_id=1, source_target_pairs={{0,4},{4,0},{8,12},{12,8},{16,20},{20,16},{24,28},{28,24},{1,5},{5... | collective-permute-start | bytes 393224 | tf_op jit(solution)/shard_map/ppermute | solution.py:35
  17.0 7.7 %collective-permute-start.3 = (bf16[128,512]{1,0:T(8,128)(2,1)S(1)}, bf16[128,512]{1,0:T(8,128)(2,1)S(1)}, u32[]{:S(2)}, u32[]{:S(2)}) collective-permute-start(bf16[128,512]{1,0:T(8,128)(2,1)S(1)} %lineup.6.refs_2_), channel_id=1, source_target_pairs={{0,6},{1,7},{2,4},{3,5},{4,2},{5,3},{6,0},{7,1},{8,14},{9,15},{10,... | collective-permute-start | bytes 393224 | tf_op jit(solution)/shard_map/ppermute | solution.py:45
  18.6 13.6 %collective-permute-start.12 = (bf16[384,512]{1,0:T(8,128)(2,1)S(1)}, bf16[384,512]{1,0:T(8,128)(2,1)S(1)}, u32[]{:S(2)}, u32[]{:S(2)}) collective-permute-start(bf16[384,512]{1,0:T(8,128)(2,1)S(1)} %lineup.11), channel_id=1, source_target_pairs={{0,8},{8,16},{16,24},{12,4},{20,12},{28,20},{1,9},{9,17},{17,25},{... | collective-permute-start | bytes 1179656 | tf_op jit(solution)/shard_map/ppermute | solution.py:495
  21.0 11.9 %collective-permute-start.13 = (bf16[384,512]{1,0:T(8,128)(2,1)S(1)}, bf16[384,512]{1,0:T(8,128)(2,1)S(1)}, u32[]{:S(2)}, u32[]{:S(2)}) collective-permute-start(bf16[384,512]{1,0:T(8,128)(2,1)S(1)} %lineup.11), channel_id=1, source_target_pairs={{0,1},{1,0},{2,3},{3,2},{4,5},{5,4},{6,7},{7,6},{8,9},{9,8},{10,11... | collective-permute-start | bytes 1179656 | tf_op jit(solution)/shard_map/ppermute | solution.py:35
  26.5 1.8 %collective-permute-start.9 = (bf16[256,640]{1,0:T(8,128)(2,1)S(1)}, bf16[256,640]{1,0:T(8,128)(2,1)S(1)}, u32[]{:S(2)}, u32[]{:S(2)}) collective-permute-start(bf16[256,640]{1,0:T(8,128)(2,1)S(1)} %get-tuple-element.29), channel_id=1, source_target_pairs={{0,1},{1,0},{2,3},{3,2},{4,5},{5,4},{6,7},{7,6},{8,9},{9,8},{10,11... | collective-permute-start | bytes 983048 | tf_op jit(solution)/shard_map/ppermute | solution.py:35
  28.6 7.9 %collective-permute-start.11 = (bf16[128,640]{1,0:T(8,128)(2,1)S(1)}, bf16[128,640]{1,0:T(8,128)(2,1)S(1)}, u32[]{:S(2)}, u32[]{:S(2)}) collective-permute-start(bf16[128,640]{1,0:T(8,128)(2,1)S(1)} %combine.1.refs_5_), channel_id=1, source_target_pairs={{0,8},{4,12},{8,0},{12,4},{16,24},{20,28},{24,16},{28,20},{1,9},{5... | collective-permute-start | bytes 491528 | tf_op jit(solution)/shard_map/ppermute | solution.py:35
  29.1 5.2 %copy-start.4 = (bf16[16,128,128]{2,1,0:T(8,128)(2,1)S(1)}, bf16[16,128,128]{2,1,0:T(8,128)(2,1)}, u32[]{:S(2)}) copy-start(bf16[16,128,128]{2,1,0:T(8,128)(2,1)} %tiles_ref.1) | copy-start | bytes 1572868
  32.0 4.4 %collective-permute-start.10 = (bf16[144,512]{1,0:T(8,128)(2,1)S(1)}, bf16[144,512]{1,0:T(8,128)(2,1)S(1)}, u32[]{:S(2)}, u32[]{:S(2)}) collective-permute-start(bf16[144,512]{1,0:T(8,128)(2,1)S(1)} %get-tuple-element.32), channel_id=1, source_target_pairs={{0,1},{1,0},{2,3},{3,2},{4,5},{5,4},{6,7},{7,6},{8,9},{9,8},{10,11... | collective-permute-start | bytes 442376 | tf_op jit(solution)/shard_map/ppermute | solution.py:35
  32.1 2.2 %copy-start.2 = (bf16[512,1024]{1,0:T(8,128)(2,1)S(1)}, bf16[512,1024]{1,0:T(8,128)(2,1)}, u32[]{:S(2)}) copy-start(bf16[512,1024]{1,0:T(8,128)(2,1)} %refs_8_.1) | copy-start | bytes 3145732
  32.1 2.2 %copy-start.3 = (bf16[1024,512]{1,0:T(8,128)(2,1)S(1)}, bf16[1024,512]{1,0:T(8,128)(2,1)}, u32[]{:S(2)}) copy-start(bf16[1024,512]{1,0:T(8,128)(2,1)} %refs_9_.1) | copy-start | bytes 3145732
  32.1 1.5 %collective-permute-start.16 = (bf16[128,512]{1,0:T(8,128)(2,1)S(1)}, bf16[128,512]{1,0:T(8,128)(2,1)S(1)}, u32[]{:S(2)}, u32[]{:S(2)}) collective-permute-start(bf16[128,512]{1,0:T(8,128)(2,1)S(1)} %rows.5), channel_id=1, source_target_pairs={{0,1},{1,0},{2,3},{3,2},{4,5},{5,4},{6,7},{7,6},{8,9},{9,8},{10,11... | collective-permute-start | bytes 393224 | tf_op jit(solution)/shard_map/ppermute | solution.py:35
  32.6 1.4 %collective-permute-start.15 = (bf16[128,512]{1,0:T(8,128)(2,1)S(1)}, bf16[128,512]{1,0:T(8,128)(2,1)S(1)}, u32[]{:S(2)}, u32[]{:S(2)}) collective-permute-start(bf16[128,512]{1,0:T(8,128)(2,1)S(1)} %rows.4), channel_id=1, source_target_pairs={{0,1},{1,0},{2,3},{3,2},{4,5},{5,4},{6,7},{7,6},{8,9},{9,8},{10,11... | collective-permute-start | bytes 393224 | tf_op jit(solution)/shard_map/ppermute | solution.py:35
  32.8 1.5 %copy-start.8 = (f32[512]{0:T(512)S(1)}, f32[512]{0:T(512)}, u32[]{:S(2)}) copy-start(f32[512]{0:T(512)} %param.21) | copy-start | bytes 6148
  32.8 1.5 %collective-permute-start.14 = (bf16[128,512]{1,0:T(8,128)(2,1)S(1)}, bf16[128,512]{1,0:T(8,128)(2,1)S(1)}, u32[]{:S(2)}, u32[]{:S(2)}) collective-permute-start(bf16[128,512]{1,0:T(8,128)(2,1)S(1)} %rows.3), channel_id=1, source_target_pairs={{0,1},{1,0},{2,3},{3,2},{4,5},{5,4},{6,7},{7,6},{8,9},{9,8},{10,11... | collective-permute-start | bytes 393224 | tf_op jit(solution)/shard_map/ppermute | solution.py:35
  34.3 0.7 %copy-start.9 = (s32[1,1,12]{2,1,0:T(1,128)S(1)}, s32[1,1,12]{2,1,0:T(1,128)}, u32[]{:S(2)}) copy-start(s32[1,1,12]{2,1,0:T(1,128)} %param.12) | copy-start | bytes 148
  35.0 1.5 %copy-start.5 = (bf16[512,512]{1,0:T(8,128)(2,1)S(1)}, bf16[512,512]{1,0:T(8,128)(2,1)}, u32[]{:S(2)}) copy-start(bf16[512,512]{1,0:T(8,128)(2,1)} %final_ref.1) | copy-start | bytes 1572868

commit v5 on v4

--- a/solution.py
+++ b/solution.py
@@ -146,45 +146,76 @@
     )(block, *after)
 
 
-def near_kernel(softness_ref, both_ref, others_ref, *refs):
-    blocks, (asking_ref, lookup_ref, content_ref) = refs[:-10], refs[-10:-7]
-    queries_ref, keys_ref, values_ref, numer_ref, denom_ref, temper, sem = refs[-7:]
+def early_kernel(softness_ref, slots_ref, both_ref, side_ref, asking_ref, lookup_ref, content_ref, *refs):
+    queries_ref, scale_ref, keys_ref, values_ref, slots_out, temper, sems = refs
     half = both_ref.shape[0] // 2
-    mine, theirs = slice(0, half), slice(half, 2 * half)
-    copy = pltpu.make_async_copy(softness_ref, temper, sem)
-    copy.start()
-    nodes = [both_ref[mine, :]] + [block[...] for block in blocks]
+    copies = [
+        pltpu.make_async_copy(softness_ref, temper, sems.at[0]),
+        pltpu.make_async_copy(slots_ref, slots_out, sems.at[1]),
+    ]
+    for copy in copies:
+        copy.start()
+    nodes = [both_ref[:half, :], side_ref[...]]
     keys_values(nodes, lookup_ref, content_ref, keys_ref, values_ref)
-    rows = jnp.concatenate(
-        [others_ref[theirs, :], others_ref[mine, :], both_ref[theirs, :], both_ref[mine, :]], axis=0
-    )
-    projected = head_normed(dot(rows, asking_ref[...]))
-    copy.wait()
+    projected = head_normed(dot(both_ref[...], asking_ref[...]))
+    for copy in copies:
+        copy.wait()
     width = asking_ref.shape[1]
     head = lax.broadcasted_iota(jnp.int32, (1, width), 1) // SUBSPACE_WIDTH
     scale = jnp.zeros((1, width), F32)
     for h in range(NUM_SUBSPACES):
         scale = jnp.where(head == h, temper[h], scale)
     scale = scale * (math.log2(math.e) / math.sqrt(SUBSPACE_WIDTH))
+    scale_ref[...] = scale
     queries = (projected * scale).astype(BF16)
+    queries_ref[:half, :] = queries[half:]
+    queries_ref[half:, :] = queries[:half]
+
+
+def early(softness, slots, both, side, asking, lookup, content):
+    rows, width = both.shape
+    count = rows // 2 + side.shape[0]
+    array = lambda n, dtype: jax.ShapeDtypeStruct((n, width), dtype)
+    return pl.pallas_call(
+        early_kernel,
+        out_shape=(array(rows, BF16), array(1, F32), array(count, BF16), array(count, BF16))
+        + (jax.ShapeDtypeStruct(slots.shape, jnp.int32),),
+        in_specs=[ANY] * 2 + [VMEM] * 5,
+        out_specs=(VMEM,) * 5,
+        scratch_shapes=[pltpu.SMEM(softness.shape, F32), pltpu.SemaphoreType.DMA((2,))],
+        compiler_params=params(16),
+        cost_estimate=cost(2 * (rows + 2 * count) * width * width, rows, 4 << 20),
+        name="early",
+    )(softness, slots, both, side, asking, lookup, content)
+
+
+def near_kernel(scale_ref, held_keys, held_values, others_ref, *refs):
+    blocks, (asking_ref, lookup_ref, content_ref) = refs[:-8], refs[-8:-5]
+    queries_ref, keys_ref, values_ref, numer_ref, denom_ref = refs[-5:]
+    half, held = others_ref.shape[0] // 2, held_keys.shape[0]
+    keys_ref[:held, :] = held_keys[...]
+    values_ref[:held, :] = held_values[...]
+    nodes = [block[...] for block in blocks]
+    keys_values(nodes, lookup_ref, content_ref, keys_ref.at[held:], values_ref.at[held:])
+    rows = jnp.concatenate([others_ref[half:, :], others_ref[:half, :]], axis=0)
+    queries = (head_normed(dot(rows, asking_ref[...])) * scale_ref[...]).astype(BF16)
     queries_ref[...] = queries
-    numer_ref[...], denom_ref[...] = attend(queries[: 2 * half], keys_ref, values_ref)
-
-
-def near(softness, both, others, blocks, asking, lookup, content):
-    rows, width = both.shape
-    count = rows // 2 + sum(block.shape[0] for block in blocks)
+    numer_ref[...], denom_ref[...] = attend(queries, keys_ref, values_ref)
+
+
+def near(scale, keys, values, others, blocks, asking, lookup, content):
+    rows, width = others.shape
+    count = keys.shape[0] + sum(block.shape[0] for block in blocks)
     array = lambda n, dtype: jax.ShapeDtypeStruct((n, width), dtype)
     return pl.pallas_call(
         near_kernel,
-        out_shape=(array(2 * rows, BF16),) + (array(count, BF16),) * 2 + (array(rows, F32),) * 2,
-        in_specs=[ANY] + [VMEM] * (5 + len(blocks)),
+        out_shape=(array(rows, BF16),) + (array(count, BF16),) * 2 + (array(rows, F32),) * 2,
+        in_specs=[VMEM] * (7 + len(blocks)),
         out_specs=(VMEM,) * 5,
-        scratch_shapes=[pltpu.SMEM(softness.shape, F32), pltpu.SemaphoreType.DMA],
         compiler_params=params(16),
         cost_estimate=cost(6 * rows * count * width, rows * count * NUM_SUBSPACES, 4 << 20),
         name="near",
-    )(softness, both, others, *blocks, asking, lookup, content)
+    )(scale, keys, values, others, *blocks, asking, lookup, content)
 
 
 def pack(numer, denom):
@@ -301,13 +332,36 @@
     )
 
 
+def own_first_kernel(queries_ref, keys_ref, values_ref, *refs):
+    numer_ref, denom_ref = refs[-2:]
+    count = 2 * queries_ref.shape[0]
+    numer_ref[...], denom_ref[...] = attend(
+        queries_ref[...], keys_ref.at[:count], values_ref.at[:count]
+    )
+
+
+def own_first(queries, keys, values, after):
+    rows, width = queries.shape
+    return pl.pallas_call(
+        own_first_kernel,
+        out_shape=(jax.ShapeDtypeStruct((rows, width), F32),) * 2,
+        in_specs=[VMEM] * 3 + [ANY] * len(after),
+        out_specs=(VMEM,) * 2,
+        compiler_params=params(16),
+        cost_estimate=cost(8 * rows * rows * width, 2 * rows * rows * NUM_SUBSPACES, 2 << 20),
+        name="own_first",
+    )(queries, keys, values, *after)
+
+
 def own_kernel(steps, far_keys, far_values, queries_ref, near_keys, near_values, *refs):
-    sent_ref, numer_out, denom_out, numer_sum, denom_sum = refs
+    numer_ref, denom_ref, sent_ref, numer_out, denom_out = refs[:5]
+    numer_sum, denom_sum, keys_ref, values_ref = refs[5:]
     rows, width = numer_sum.shape
-    half = rows // 2
+    half, done, left = rows // 2, 2 * rows, near_keys.shape[0] - 2 * rows
 
     def start():
-        numer_sum[...], denom_sum[...] = attend(queries_ref[rows:, :], near_keys, near_values)
+        numer_sum[...] = numer_ref[...]
+        denom_sum[...] = denom_ref[...]
 
     def end():
         sent_ref[:half, :] = numer_sum[:half, :].astype(BF16)
@@ -317,47 +371,55 @@
         denom_out[...] = denom_sum[half:, :]
 
     at_step(steps, 0, start)
-    numer, denom = attend(queries_ref[rows:, :], far_keys, far_values)
+    if left:
+        keys_ref[:left, :] = near_keys[done:, :]
+        values_ref[:left, :] = near_values[done:, :]
+        keys_ref[left:, :] = far_keys[...]
+        values_ref[left:, :] = far_values[...]
+        numer, denom = attend(queries_ref[...], keys_ref, values_ref)
+    else:
+        numer, denom = attend(queries_ref[...], far_keys, far_values)
     numer_sum[...] += numer
     denom_sum[...] += denom
     at_step(steps, steps - 1, end)
 
 
-def own(far_keys, far_values, steps, queries, near_keys, near_values, after):
-    rows, width = queries.shape[0] // 2, queries.shape[1]
+def own(far_keys, far_values, steps, queries, near_keys, near_values, numer, denom, after):
+    rows, width = queries.shape
     half = rows // 2
+    count = near_keys.shape[0] - 2 * rows + far_keys.shape[0] // steps
     return call(
         own_kernel,
         steps,
         (far_keys, far_values),
-        (queries, near_keys, near_values),
+        (queries, near_keys, near_values, numer, denom),
         (),
         (jax.ShapeDtypeStruct((half + PARTS, width), BF16),)
         + (jax.ShapeDtypeStruct((half, width), F32),) * 2,
-        [pltpu.VMEM((rows, width), F32)] * 2,
-        cost(4 * rows * near_keys.shape[0] * width, 1 << 20, 4 << 20),
+        [pltpu.VMEM((rows, width), F32)] * 2 + [pltpu.VMEM((count, width), BF16)] * 2,
+        cost(4 * rows * count * width, rows * count * NUM_SUBSPACES, 4 << 20),
         "own",
         after,
     )
 
 
-def combine_kernel(numer_ref, denom_ref, packed_ref, packed_out):
+def combine_kernel(numer_ref, denom_ref, packed_ref, after_ref, packed_out):
     rows, width = numer_ref.shape
     numer = numer_ref[...] + packed_ref[:rows, :width].astype(F32)
     denom = denom_ref[...] + unpack_denom(packed_ref[:rows, width:], width)
     packed_out[...] = pack(numer, denom)
 
 
-def combine(numer, denom, packed):
+def combine(numer, denom, packed, after):
     return pl.pallas_call(
         combine_kernel,
         out_shape=jax.ShapeDtypeStruct((numer.shape[0], packed.shape[1]), BF16),
-        in_specs=[VMEM] * 3,
+        in_specs=[VMEM] * 3 + [ANY],
         out_specs=VMEM,
         compiler_params=params(8),
         cost_estimate=cost(4 * packed.shape[0] * packed.shape[1] * LANES, 0, 1 << 20),
         name="combine",
-    )(numer, denom, packed)
+    )(numer, denom, packed, *after)
 
 
 def message_kernel(slots_ref, tiles_ref, *refs):
@@ -366,7 +428,7 @@
     gain_out[...] = gain_ref[...]
     copy = pltpu.make_async_copy(slots_ref, slots, sem)
     copy.start()
-    group = slots_ref.shape[0] // 3
+    group = slots_ref.shape[1] // 3
     me, core, odd = lax.axis_index("head"), lax.axis_index("head") % 2, lax.axis_index("dom") % 2
     beside, beyond = 2 - 2 * odd, 2 * odd
     part, parts = lax.axis_index("dom"), lax.axis_size("dom")
@@ -384,7 +446,7 @@
     copy.wait()
     tiles = []
     for side, offset in order:
-        tile_id = slots[side * group + (me ^ offset)]
+        tile_id = slots[0, side * group + (me ^ offset)]
         tile_id = jnp.where(outside & (side == beyond), -1, tile_id)
         tile = tiles_ref[jnp.maximum(tile_id, 0)]
         tiles.append(jnp.where(tile_id >= 0, tile, jnp.zeros_like(tile)))
@@ -398,7 +460,7 @@
     return pl.pallas_call(
         message_kernel,
         out_shape=(jax.ShapeDtypeStruct((rows, width), F32), jax.ShapeDtypeStruct(gain.shape, F32)),
-        in_specs=[ANY] + [VMEM] * (4 + len(blocks)),
+        in_specs=[VMEM] + [VMEM] * (4 + len(blocks)),
         out_specs=(VMEM,) * 2,
         scratch_shapes=[pltpu.SMEM(slots.shape, jnp.int32), pltpu.SemaphoreType.DMA],
         compiler_params=params(16),
@@ -468,24 +530,34 @@
         return below, side, across
 
     held = lineup((nodes,))
-    if distant.shape[0] == block_len:
-        distant = lineup((distant,), work=20 << 20)
     both = lineup((held, swap(nodes, "head", 1)))
     side = swap_by_core(both, (1, 0), (0, 2))
     across = swap_by_core(lineup((side,), (), block_len), (0, 2), (1, 0))
     other = swap(nodes, "dom", 2)
     others = lineup((other, swap(other, "head", 1)))
+    queries, scale, keys, values, slots = early(
+        softness_per_subspace,
+        adjacent_group_bank_ids.reshape(1, -1),
+        both,
+        side,
+        asking_projector,
+        lookup_projector,
+        content_projector,
+    )
+    distant = lineup((distant,), (queries,))
     far_blocks = plane(distant)
     steps = distant.shape[0] // block_len
     if steps == 1:
-        early = (side, across, distant)
+        near_blocks = (across, distant, far_blocks[1])
+        far_blocks = (far_blocks[0], far_blocks[2])
     else:
-        early, far_blocks = (side, across), (distant,) + far_blocks
-    queries, keys, values, numer, denom = near(
-        softness_per_subspace,
-        both,
+        near_blocks, far_blocks = (across,), (distant,) + far_blocks
+    pair_queries, keys, values, numer, denom = near(
+        scale,
+        keys,
+        values,
         others,
-        early,
+        near_blocks,
         asking_projector,
         lookup_projector,
         content_projector,
@@ -494,10 +566,13 @@
     pairs = [(p, p + 2) for p in range(0, doms - 2, 2)] + [(p, p - 2) for p in range(3, doms, 2)]
     halo = lax.ppermute(lineup((side, across), ()), "dom", pairs)
     far_keys, far_values, packed, numer, denom = far(
-        far_blocks, block_len, lookup_projector, content_projector, queries, numer, denom
-    )
-    packed = packed_here = combine(numer, denom, swap(packed, "head", 1))
-    crossed, numer, denom = own(far_keys, far_values, steps, queries, keys, values, (packed,))
+        far_blocks, block_len, lookup_projector, content_projector, pair_queries, numer, denom
+    )
+    own_numer, own_denom = own_first(queries, keys, values, (packed,))
+    packed = combine(numer, denom, swap(packed, "head", 1), (own_numer,))
+    crossed, numer, denom = own(
+        far_keys, far_values, steps, queries, keys, values, own_numer, own_denom, (packed,)
+    )
     crossed = swap(crossed, "head", 1)
     packed = swap(packed, "dom", 2)
     got = swap(lineup((side, across)), "head", 1)
@@ -505,7 +580,7 @@
         swap(rows_of(halo, at * block_len, block_len, (numer,)), "head", 1) for at in range(3)
     ]
     local, gain = message(
-        adjacent_group_bank_ids.reshape(-1),
+        slots,
         coupling_strength_panels,
         (both, side, across, halo, got, *got_halo),
         passing_inner_coefficients,

time: 38 us -> 35.5 us (0.934)
  waiting for transfers between devices: 6.59 us -> 3.46 us
  Pallas kernels: 11.3 us -> 12.2 us
  local copies, waits for them, and re-layouts: 1.58 us -> 1.12 us
    ppermute x13, waiting for transfers between devices: 6.4 us -> 3.27 us  [swap(): return lax.ppermute(array, axis, [(i, i ^ mask) for i in range(devices)])]
    pallas_call x2, Pallas kernels: 4.64 us -> 2.91 us  [call(): pl.pallas_call(body, grid=grid, out_shape=tuple(out_parts) + tuple(out_wh...]
    pallas_call x1 -> x3, Pallas kernels: 3.65 us -> 5.32 us  [the longest x1 2.87 us: near(): pl.pallas_call(near_kernel, out_shape=(array(rows, BF16),) + (array(count...]
    pallas_call x6, Pallas kernels: 0.09 us -> 1.05 us  [lineup(): pl.pallas_call(functools.partial(lineup_kernel, len(blocks), rows), out_s...]
    unnamed x22, local copies, waits for them, and re-layouts: 1.58 us -> 1.12 us
  transfers between devices with their start and end apart: 17 -> 17, of which waited for: 8 -> 9; matrix products, arithmetic and copies ran while one was open for 0% -> 0% of each run, Pallas kernels for 27% -> 31%
where the time goes in v5:
time: 35.5 us; the launch traced here: 35.3 us
  starting transfers between devices  18.3 us (52%)
  Pallas kernels  12.2 us (34%)
  waiting for transfers between devices  3.46 us (10%)
  local copies, waits for them, and re-layouts  1.12 us (3%)
    ppermute x13, starting transfers between devices, swap(): return lax.ppermute(array, axis, [(i, i ^ mask) for i in range(devices)])  9.39 us
    ppermute x2, starting transfers between devices, swap_by_core(): return lax.ppermute(array, ('dom', 'head'), pairs)  5.03 us
    ppermute x13, waiting for transfers between devices, swap(): return lax.ppermute(array, axis, [(i, i ^ mask) for i in range(devices)])  3.27 us
    pallas_call x2, Pallas kernels, call(): pl.pallas_call(body, grid=grid, out_shape=tuple(out_parts) + tuple(out_wh...  2.91 us
    pallas_call x1, Pallas kernels, near(): pl.pallas_call(near_kernel, out_shape=(array(rows, BF16),) + (array(count...  2.87 us
    ppermute x1, starting transfers between devices, shards(): halo = lax.ppermute(lineup((side, across), ()), 'dom', pairs)  2.36 us
    ppermute x1, starting transfers between devices, swap_both(): return lax.ppermute(array, ('dom', 'head'), pairs)  1.49 us
    pallas_call x1, Pallas kernels, message(): pl.pallas_call(message_kernel, out_shape=(jax.ShapeDtypeStruct((rows, wid...  1.45 us
  transfers between devices with their start and end apart: 17, of which 9 were waited for; matrix products, arithmetic and copies ran while one was open for 0% of the time, Pallas kernels for 31%

profile of v5, /device:TPU:0, one launch (start us, length us, event | category | flops | bytes accessed | tf_op | source)
XLA Modules:
  0.0 35.3 jit_solution(12353362757410253020)
XLA Ops:
  0.0 0.5 %collective-permute-start.1 = (bf16[128,512]{1,0:T(8,128)(2,1)}, bf16[128,512]{1,0:T(8,128)(2,1)S(1)}, u32[]{:S(2)}, u32[]{:S(2)}) collective-permute-start(bf16[128,512]{1,0:T(8,128)(2,1)} %refs_0_.1), channel_id=1, source_target_pairs={{0,1},{1,0},{2,3},{3,2},{4,5},{5,4},{6,7},{7,6},{8,9},{9,8},{10,11... | collective-permute-start | bytes 393224 | tf_op jit(solution)/shard_map/ppermute | solution.py:35
  0.5 1.0 %lineup.6.refs_0_.nodes_ref = bf16[128,512]{1,0:T(8,128)(2,1)S(1)} custom-call(bf16[128,512]{1,0:T(8,128)(2,1)} %refs_0_.1), custom_call_target="tpu_custom_call" | custom-call | bytes 32768 | tf_op jit(solution)/shard_map/lineup/pallas_call | solution.py:122
  1.4 0.0 copy-start
  1.4 0.2 collective-permute-done.1.refs_1_
  1.7 2.9 %collective-permute-start.2 = (bf16[256,512]{1,0:T(8,128)(2,1)S(1)}, bf16[256,512]{1,0:T(8,128)(2,1)S(1)}, u32[]{:S(2)}, u32[]{:S(2)}) collective-permute-start(bf16[256,512]{1,0:T(8,128)(2,1)S(1)} %lineup.7.both_ref.refs_0_), channel_id=1, source_target_pairs={{0,4},{1,3},{2,6},{3,1},{4,0},{5,7},{6,2},{7,5},{8,12},{9,11},{10,... | collective-permute-start | bytes 786440 | tf_op jit(solution)/shard_map/ppermute | solution.py:55
  4.6 1.6 %collective-permute-start.5 = (bf16[128,512]{1,0:T(8,128)(2,1)}, bf16[128,512]{1,0:T(8,128)(2,1)S(1)}, u32[]{:S(2)}, u32[]{:S(2)}) collective-permute-start(bf16[128,512]{1,0:T(8,128)(2,1)} %refs_0_.1), channel_id=1, source_target_pairs={{0,8},{4,12},{8,0},{12,4},{16,24},{20,28},{24,16},{28,20},{1,9},{5... | collective-permute-start | bytes 393224 | tf_op jit(solution)/shard_map/ppermute | solution.py:35
  6.2 2.6 %collective-permute-start = (bf16[128,512]{1,0:T(8,128)(2,1)}, bf16[128,512]{1,0:T(8,128)(2,1)S(1)}, u32[]{:S(2)}, u32[]{:S(2)}) collective-permute-start(bf16[128,512]{1,0:T(8,128)(2,1)} %refs_0_.1), channel_id=1, source_target_pairs={{0,16},{4,20},{8,24},{12,28},{16,0},{20,4},{24,8},{28,12},{1,17},{... | collective-permute-start | bytes 393224 | tf_op jit(solution)/shard_map/ppermute | solution.py:35
  8.8 0.2 collective-permute-done.2.side_ref.refs_0_.refs_1_
  9.0 0.0 copy-start.9
  9.0 0.0 copy-start.10
  9.0 2.1 %collective-permute-start.7 = (bf16[128,512]{1,0:T(8,128)(2,1)S(1)}, bf16[128,512]{1,0:T(8,128)(2,1)S(1)}, u32[]{:S(2)}, u32[]{:S(2)}) collective-permute-start(bf16[128,512]{1,0:T(8,128)(2,1)S(1)} %lineup.10), channel_id=1, source_target_pairs={{0,2},{1,5},{2,0},{3,7},{4,6},{5,1},{6,4},{7,3},{8,10},{9,13},{10,... | collective-permute-start | bytes 393224 | tf_op jit(solution)/shard_map/ppermute | solution.py:55
  11.1 1.1 %collective-permute-done.5.refs_0_ = bf16[128,512]{1,0:T(8,128)(2,1)S(1)} collective-permute-done((bf16[128,512]{1,0:T(8,128)(2,1)}, bf16[128,512]{1,0:T(8,128)(2,1)S(1)}, u32[]{:S(2)}, u32[]{:S(2)}) %collective-permute-start.5) | collective-permute-done | bytes 131104 | tf_op jit(solution)/shard_map/ppermute | solution.py:35
  12.2 0.0 copy-start.2
  12.2 1.0 %copy-done.2 = bf16[512,512]{1,0:T(8,128)(2,1)S(1)} copy-done((bf16[512,512]{1,0:T(8,128)(2,1)S(1)}, bf16[512,512]{1,0:T(8,128)(2,1)}, u32[]{:S(2)}) %copy-start.2) | copy-done | bytes 524312
  13.2 1.1 %early.1 = (bf16[256,512]{1,0:T(8,128)(2,1)S(1)}, f32[1,512]{1,0:T(1,128)S(1)}, bf16[384,512]{1,0:T(8,128)(2,1)S(1)}, bf16[384,512]{1,0:T(8,128)(2,1)S(1)}, s32[1,12]{1,0:T(1,128)S(1)}) custom-call(f32[8]{0:T(128)S(1)} %copy-done.9, s32[1,12]{1,0:T(1,128)S(1)} %bitcast.3, bf16[256,512]{1,0:T(8,128)(2,1)S(1)} %lineup.7.both_ref.refs_0_, ...), custom_call_target="tpu_custom_call" | custom-call | flops 33554432 | bytes 262144 | tf_op jit(solution)/shard_map/early/pallas_call | solution.py:179
  14.3 0.8 %collective-permute-done.refs_0_ = bf16[128,512]{1,0:T(8,128)(2,1)S(1)} collective-permute-done((bf16[128,512]{1,0:T(8,128)(2,1)}, bf16[128,512]{1,0:T(8,128)(2,1)S(1)}, u32[]{:S(2)}, u32[]{:S(2)}) %collective-permute-start) | collective-permute-done | bytes 131104 | tf_op jit(solution)/shard_map/ppermute | solution.py:35
  15.2 0.0 copy-start.3
  15.2 1.6 %collective-permute-start.8 = (bf16[128,512]{1,0:T(8,128)(2,1)S(1)}, bf16[128,512]{1,0:T(8,128)(2,1)S(1)}, u32[]{:S(2)}, u32[]{:S(2)}) collective-permute-start(bf16[128,512]{1,0:T(8,128)(2,1)S(1)} %lineup.8.refs_1_), channel_id=1, source_target_pairs={{0,4},{4,0},{8,12},{12,8},{16,20},{20,16},{24,28},{28,24},{1,5},{5... | collective-permute-start | bytes 393224 | tf_op jit(solution)/shard_map/ppermute | solution.py:35
  16.7 0.5 %collective-permute-start.3 = (bf16[128,512]{1,0:T(8,128)(2,1)S(1)}, bf16[128,512]{1,0:T(8,128)(2,1)S(1)}, u32[]{:S(2)}, u32[]{:S(2)}) collective-permute-start(bf16[128,512]{1,0:T(8,128)(2,1)S(1)} %lineup.8.refs_1_), channel_id=1, source_target_pairs={{0,2},{1,3},{2,0},{3,1},{4,6},{5,7},{6,4},{7,5},{8,10},{9,11},{10,... | collective-permute-start | bytes 393224 | tf_op jit(solution)/shard_map/ppermute | solution.py:35
  17.3 1.5 %collective-permute-start.4 = (bf16[128,512]{1,0:T(8,128)(2,1)S(1)}, bf16[128,512]{1,0:T(8,128)(2,1)S(1)}, u32[]{:S(2)}, u32[]{:S(2)}) collective-permute-start(bf16[128,512]{1,0:T(8,128)(2,1)S(1)} %lineup.8.refs_1_), channel_id=1, source_target_pairs={{0,6},{1,7},{2,4},{3,5},{4,2},{5,3},{6,0},{7,1},{8,14},{9,15},{10,... | collective-permute-start | bytes 393224 | tf_op jit(solution)/shard_map/ppermute | solution.py:45
  18.7 0.0 collective-permute-done.7.refs_0_.refs_1_.refs_2_
  18.8 2.4 %collective-permute-start.12 = (bf16[384,512]{1,0:T(8,128)(2,1)S(1)}, bf16[384,512]{1,0:T(8,128)(2,1)S(1)}, u32[]{:S(2)}, u32[]{:S(2)}) collective-permute-start(bf16[384,512]{1,0:T(8,128)(2,1)S(1)} %lineup.11), channel_id=1, source_target_pairs={{0,8},{8,16},{16,24},{12,4},{20,12},{28,20},{1,9},{9,17},{17,25},{... | collective-permute-start | bytes 1179656 | tf_op jit(solution)/shard_map/ppermute | solution.py:567
  21.1 0.0 collective-permute-done.6.refs_1_
  21.2 0.1 collective-permute-start.13
  21.3 0.0 collective-permute-done.8.refs_2_
  21.3 2.9 %near.1 = (bf16[256,512]{1,0:T(8,128)(2,1)S(1)}, bf16[768,512]{1,0:T(8,128)(2,1)S(1)}, bf16[768,512]{1,0:T(8,128)(2,1)S(1)}, f32[256,512]{1,0:T(8,128)S(1)}, f32[256,512]{1,0:T(8,128)S(1)}) custom-call(f32[1,512]{1,0:T(1,128)S(1)} %get-tuple-element.28.scale_ref, bf16[384,512]{1,0:T(8,128)(2,1)S(1)} %get-tuple-element.29.held_keys, ...), custom_call_target="tpu_custom_call" | custom-call | flops 37748736 | bytes 262144 | tf_op jit(solution)/shard_map/near/pallas_call | solution.py:210
  24.2 0.1 collective-permute-done.3.refs_0_
  24.3 1.3 %far.1 = (bf16[256,512]{1,0:T(8,128)(2,1)S(1)}, bf16[256,512]{1,0:T(8,128)(2,1)S(1)}, bf16[256,640]{1,0:T(8,128)(2,1)S(1)}, f32[128,512]{1,0:T(8,128)S(1)}, f32[128,512]{1,0:T(8,128)S(1)}) custom-call(bf16[128,512]{1,0:T(8,128)(2,1)S(1)} %collective-permute-done.3.refs_0_, bf16[128,512]{1,0:T(8,128)(2,1)S(1)} %collective-permute-done.4.refs_1_, ...), custom_call_target="tpu_custom_call" | custom-call | flops 12582912 | bytes 262144 | tf_op jit(solution)/shard_map/far/pallas_call | solution.py:272
  25.6 0.5 %collective-permute-start.9 = (bf16[256,640]{1,0:T(8,128)(2,1)S(1)}, bf16[256,640]{1,0:T(8,128)(2,1)S(1)}, u32[]{:S(2)}, u32[]{:S(2)}) collective-permute-start(bf16[256,640]{1,0:T(8,128)(2,1)S(1)} %get-tuple-element.38.refs_0_), channel_id=1, source_target_pairs={{0,1},{1,0},{2,3},{3,2},{4,5},{5,4},{6,7},{7,6},{8,9},{9,8},{10,11... | collective-permute-start | bytes 983048 | tf_op jit(solution)/shard_map/ppermute | solution.py:35
  26.1 1.4 %own_first.1 = (f32[256,512]{1,0:T(8,128)S(1)}, f32[256,512]{1,0:T(8,128)S(1)}) custom-call(bf16[256,512]{1,0:T(8,128)(2,1)S(1)} %get-tuple-element.27.refs_1_.queries_ref.refs_2_, bf16[768,512]{1,0:T(8,128)(2,1)S(1)} %get-tuple-element.36.keys_ref.refs_3_, bf16[768,512]{1,0:T(8,128)(2,1)S(1)} %get-tuple-element.37.values_ref.refs_4_, ...), custom_call_target="tpu_custom_call" | custom-call | flops 16777216 | bytes 131072 | tf_op jit(solution)/shard_map/own_first/pallas_call | solution.py:345
  27.4 0.0 collective-permute-done.9.packed_ref
  27.4 0.2 combine.1.refs_7_
  27.7 1.0 %collective-permute-start.11 = (bf16[128,640]{1,0:T(8,128)(2,1)S(1)}, bf16[128,640]{1,0:T(8,128)(2,1)S(1)}, u32[]{:S(2)}, u32[]{:S(2)}) collective-permute-start(bf16[128,640]{1,0:T(8,128)(2,1)S(1)} %combine.1.refs_7_), channel_id=1, source_target_pairs={{0,8},{4,12},{8,0},{12,4},{16,24},{20,28},{24,16},{28,20},{1,9},{5... | collective-permute-start | bytes 491528 | tf_op jit(solution)/shard_map/ppermute | solution.py:35
  28.6 1.6 %own.1 = (bf16[144,512]{1,0:T(8,128)(2,1)S(1)}, f32[128,512]{1,0:T(8,128)S(1)}, f32[128,512]{1,0:T(8,128)S(1)}) custom-call(bf16[256,512]{1,0:T(8,128)(2,1)S(1)} %get-tuple-element.34.refs_0_, bf16[256,512]{1,0:T(8,128)(2,1)S(1)} %get-tuple-element.35.refs_1_, bf16[256,512]{1,0:T(8,128)(2,1)S(1)} %get-tuple-element.27.refs_1_.queries_ref.refs_2_, ...), custom_call_target="tpu_custom_call" | custom-call | flops 16777216 | bytes 262144 | tf_op jit(solution)/shard_map/own/pallas_call | solution.py:272
  30.2 0.0 collective-permute-start.10
  30.2 0.0 copy-start.4
  30.3 0.0 copy-start.5
  30.3 0.6 %collective-permute-start.16 = (bf16[128,512]{1,0:T(8,128)(2,1)S(1)}, bf16[128,512]{1,0:T(8,128)(2,1)S(1)}, u32[]{:S(2)}, u32[]{:S(2)}) collective-permute-start(bf16[128,512]{1,0:T(8,128)(2,1)S(1)} %rows.5), channel_id=1, source_target_pairs={{0,1},{1,0},{2,3},{3,2},{4,5},{5,4},{6,7},{7,6},{8,9},{9,8},{10,11... | collective-permute-start | bytes 393224 | tf_op jit(solution)/shard_map/ppermute | solution.py:35
  30.9 0.1 collective-permute-start.15
  31.0 0.0 copy-start.8
  31.0 0.6 %collective-permute-start.14 = (bf16[128,512]{1,0:T(8,128)(2,1)S(1)}, bf16[128,512]{1,0:T(8,128)(2,1)S(1)}, u32[]{:S(2)}, u32[]{:S(2)}) collective-permute-start(bf16[128,512]{1,0:T(8,128)(2,1)S(1)} %rows.3), channel_id=1, source_target_pairs={{0,1},{1,0},{2,3},{3,2},{4,5},{5,4},{6,7},{7,6},{8,9},{9,8},{10,11... | collective-permute-start | bytes 393224 | tf_op jit(solution)/shard_map/ppermute | solution.py:35
  31.6 0.3 collective-permute-done.16.refs_7_
  31.9 0.4 %collective-permute-done.15.refs_6_ = bf16[128,512]{1,0:T(8,128)(2,1)S(1)} collective-permute-done((bf16[128,512]{1,0:T(8,128)(2,1)S(1)}, bf16[128,512]{1,0:T(8,128)(2,1)S(1)}, u32[]{:S(2)}, u32[]{:S(2)}) %collective-permute-start.15) | collective-permute-done | bytes 131104 | tf_op jit(solution)/shard_map/ppermute | solution.py:35
  32.3 0.2 collective-permute-done.14.refs_5_
  32.6 0.0 copy-start.7
  32.6 1.5 %message.1 = (f32[128,512]{1,0:T(8,128)S(1)}, f32[1,512]{1,0:T(1,128)S(1)}) custom-call(s32[1,12]{1,0:T(1,128)S(1)} %get-tuple-element.46.slots_ref, bf16[16,128,128]{2,1,0:T(8,128)(2,1)S(1)} %copy-done.6, bf16[256,512]{1,0:T(8,128)(2,1)S(1)} %lineup.7.both_ref.refs_0_, bf16[256,512]{1,0:T(8,128)(2,1)S(1)} %collective-permute-done.2.side_ref.refs_0_.refs_1_, ...), custom_call_target="tpu_custom_call" | custom-call | flops 29360128 | bytes 262144 | tf_op jit(solution)/shard_map/message/pallas_call | solution.py:460
  34.0 0.1 collective-permute-done.11.packed_ref
  34.1 1.2 %finish.1 = bf16[128,512]{1,0:T(8,128)(2,1)} custom-call(f32[128,512]{1,0:T(8,128)S(1)} %get-tuple-element.43.refs_0_.numer_ref, f32[128,512]{1,0:T(8,128)S(1)} %get-tuple-element.44.denom_ref, bf16[144,512]{1,0:T(8,128)(2,1)S(1)} %collective-permute-done.10.crossed_ref, bf16[128,640]{1,0:T(8,128)(2,1)S(1)} %collective-permute-done.11.packed_ref, ...), custom_call_target="tpu_custom_call" | custom-call | flops 4194304 | bytes 131072 | tf_op jit(solution)/shard_map/finish/pallas_call | solution.py:491
  (25 shorter events, 0.2 us)
Async XLA Ops:
  0.0 1.6 %collective-permute-start.1 = (bf16[128,512]{1,0:T(8,128)(2,1)}, bf16[128,512]{1,0:T(8,128)(2,1)S(1)}, u32[]{:S(2)}, u32[]{:S(2)}) collective-permute-start(bf16[128,512]{1,0:T(8,128)(2,1)} %refs_0_.1), channel_id=1, source_target_pairs={{0,1},{1,0},{2,3},{3,2},{4,5},{5,4},{6,7},{7,6},{8,9},{9,8},{10,11... | collective-permute-start | bytes 393224 | tf_op jit(solution)/shard_map/ppermute | solution.py:35
  0.5 11.7 %copy-start.1 = (bf16[512,512]{1,0:T(8,128)(2,1)S(1)}, bf16[512,512]{1,0:T(8,128)(2,1)}, u32[]{:S(2)}) copy-start(bf16[512,512]{1,0:T(8,128)(2,1)} %refs_3_.3) | copy-start | bytes 1572868
  1.4 10.7 %copy-start = (bf16[512,512]{1,0:T(8,128)(2,1)S(1)}, bf16[512,512]{1,0:T(8,128)(2,1)}, u32[]{:S(2)}) copy-start(bf16[512,512]{1,0:T(8,128)(2,1)} %refs_2_.1) | copy-start | bytes 1572868
  1.7 7.3 %collective-permute-start.2 = (bf16[256,512]{1,0:T(8,128)(2,1)S(1)}, bf16[256,512]{1,0:T(8,128)(2,1)S(1)}, u32[]{:S(2)}, u32[]{:S(2)}) collective-permute-start(bf16[256,512]{1,0:T(8,128)(2,1)S(1)} %lineup.7.both_ref.refs_0_), channel_id=1, source_target_pairs={{0,4},{1,3},{2,6},{3,1},{4,0},{5,7},{6,2},{7,5},{8,12},{9,11},{10,... | collective-permute-start | bytes 786440 | tf_op jit(solution)/shard_map/ppermute | solution.py:55
  4.6 7.6 %collective-permute-start.5 = (bf16[128,512]{1,0:T(8,128)(2,1)}, bf16[128,512]{1,0:T(8,128)(2,1)S(1)}, u32[]{:S(2)}, u32[]{:S(2)}) collective-permute-start(bf16[128,512]{1,0:T(8,128)(2,1)} %refs_0_.1), channel_id=1, source_target_pairs={{0,8},{4,12},{8,0},{12,4},{16,24},{20,28},{24,16},{28,20},{1,9},{5... | collective-permute-start | bytes 393224 | tf_op jit(solution)/shard_map/ppermute | solution.py:35
  6.2 9.0 %collective-permute-start = (bf16[128,512]{1,0:T(8,128)(2,1)}, bf16[128,512]{1,0:T(8,128)(2,1)S(1)}, u32[]{:S(2)}, u32[]{:S(2)}) collective-permute-start(bf16[128,512]{1,0:T(8,128)(2,1)} %refs_0_.1), channel_id=1, source_target_pairs={{0,16},{4,20},{8,24},{12,28},{16,0},{20,4},{24,8},{28,12},{1,17},{... | collective-permute-start | bytes 393224 | tf_op jit(solution)/shard_map/ppermute | solution.py:35
  9.0 3.2 %copy-start.9 = (f32[8]{0:T(128)S(1)}, f32[8]{0:T(128)}, u32[]{:S(2)}) copy-start(f32[8]{0:T(128)} %softness_ref.1) | copy-start | bytes 100
  9.0 3.2 %copy-start.10 = (s32[1,1,12]{2,1,0:T(1,128)S(1)}, s32[1,1,12]{2,1,0:T(1,128)}, u32[]{:S(2)}) copy-start(s32[1,1,12]{2,1,0:T(1,128)} %param.12) | copy-start | bytes 148
  9.0 9.8 %collective-permute-start.7 = (bf16[128,512]{1,0:T(8,128)(2,1)S(1)}, bf16[128,512]{1,0:T(8,128)(2,1)S(1)}, u32[]{:S(2)}, u32[]{:S(2)}) collective-permute-start(bf16[128,512]{1,0:T(8,128)(2,1)S(1)} %lineup.10), channel_id=1, source_target_pairs={{0,2},{1,5},{2,0},{3,7},{4,6},{5,1},{6,4},{7,3},{8,10},{9,13},{10,... | collective-permute-start | bytes 393224 | tf_op jit(solution)/shard_map/ppermute | solution.py:55
  12.1 9.0 %collective-permute-start.6 = (bf16[128,512]{1,0:T(8,128)(2,1)S(1)}, bf16[128,512]{1,0:T(8,128)(2,1)S(1)}, u32[]{:S(2)}, u32[]{:S(2)}) collective-permute-start(bf16[128,512]{1,0:T(8,128)(2,1)S(1)} %collective-permute-done.5.refs_0_), channel_id=1, source_target_pairs={{0,1},{1,0},{2,3},{3,2},{4,5},{5,4},{6,7},{7,6},{8,9},{9,8},{10,11... | collective-permute-start | bytes 393224 | tf_op jit(solution)/shard_map/ppermute | solution.py:35
  12.2 1.0 %copy-start.2 = (bf16[512,512]{1,0:T(8,128)(2,1)S(1)}, bf16[512,512]{1,0:T(8,128)(2,1)}, u32[]{:S(2)}) copy-start(bf16[512,512]{1,0:T(8,128)(2,1)} %refs_3_.2) | copy-start | bytes 1572868
  15.2 6.1 %copy-start.3 = (bf16[512,512]{1,0:T(8,128)(2,1)S(1)}, bf16[512,512]{1,0:T(8,128)(2,1)}, u32[]{:S(2)}) copy-start(bf16[512,512]{1,0:T(8,128)(2,1)} %refs_3_.2) | copy-start | bytes 1572868
  15.2 6.1 %collective-permute-start.8 = (bf16[128,512]{1,0:T(8,128)(2,1)S(1)}, bf16[128,512]{1,0:T(8,128)(2,1)S(1)}, u32[]{:S(2)}, u32[]{:S(2)}) collective-permute-start(bf16[128,512]{1,0:T(8,128)(2,1)S(1)} %lineup.8.refs_1_), channel_id=1, source_target_pairs={{0,4},{4,0},{8,12},{12,8},{16,20},{20,16},{24,28},{28,24},{1,5},{5... | collective-permute-start | bytes 393224 | tf_op jit(solution)/shard_map/ppermute | solution.py:35
  16.7 7.5 %collective-permute-start.3 = (bf16[128,512]{1,0:T(8,128)(2,1)S(1)}, bf16[128,512]{1,0:T(8,128)(2,1)S(1)}, u32[]{:S(2)}, u32[]{:S(2)}) collective-permute-start(bf16[128,512]{1,0:T(8,128)(2,1)S(1)} %lineup.8.refs_1_), channel_id=1, source_target_pairs={{0,2},{1,3},{2,0},{3,1},{4,6},{5,7},{6,4},{7,5},{8,10},{9,11},{10,... | collective-permute-start | bytes 393224 | tf_op jit(solution)/shard_map/ppermute | solution.py:35
  17.3 7.0 %collective-permute-start.4 = (bf16[128,512]{1,0:T(8,128)(2,1)S(1)}, bf16[128,512]{1,0:T(8,128)(2,1)S(1)}, u32[]{:S(2)}, u32[]{:S(2)}) collective-permute-start(bf16[128,512]{1,0:T(8,128)(2,1)S(1)} %lineup.8.refs_1_), channel_id=1, source_target_pairs={{0,6},{1,7},{2,4},{3,5},{4,2},{5,3},{6,0},{7,1},{8,14},{9,15},{10,... | collective-permute-start | bytes 393224 | tf_op jit(solution)/shard_map/ppermute | solution.py:45
  18.8 11.5 %collective-permute-start.12 = (bf16[384,512]{1,0:T(8,128)(2,1)S(1)}, bf16[384,512]{1,0:T(8,128)(2,1)S(1)}, u32[]{:S(2)}, u32[]{:S(2)}) collective-permute-start(bf16[384,512]{1,0:T(8,128)(2,1)S(1)} %lineup.11), channel_id=1, source_target_pairs={{0,8},{8,16},{16,24},{12,4},{20,12},{28,20},{1,9},{9,17},{17,25},{... | collective-permute-start | bytes 1179656 | tf_op jit(solution)/shard_map/ppermute | solution.py:567
  21.2 9.8 %collective-permute-start.13 = (bf16[384,512]{1,0:T(8,128)(2,1)S(1)}, bf16[384,512]{1,0:T(8,128)(2,1)S(1)}, u32[]{:S(2)}, u32[]{:S(2)}) collective-permute-start(bf16[384,512]{1,0:T(8,128)(2,1)S(1)} %lineup.11), channel_id=1, source_target_pairs={{0,1},{1,0},{2,3},{3,2},{4,5},{5,4},{6,7},{7,6},{8,9},{9,8},{10,11... | collective-permute-start | bytes 1179656 | tf_op jit(solution)/shard_map/ppermute | solution.py:35
  25.6 1.9 %collective-permute-start.9 = (bf16[256,640]{1,0:T(8,128)(2,1)S(1)}, bf16[256,640]{1,0:T(8,128)(2,1)S(1)}, u32[]{:S(2)}, u32[]{:S(2)}) collective-permute-start(bf16[256,640]{1,0:T(8,128)(2,1)S(1)} %get-tuple-element.38.refs_0_), channel_id=1, source_target_pairs={{0,1},{1,0},{2,3},{3,2},{4,5},{5,4},{6,7},{7,6},{8,9},{9,8},{10,11... | collective-permute-start | bytes 983048 | tf_op jit(solution)/shard_map/ppermute | solution.py:35
  27.7 6.4 %collective-permute-start.11 = (bf16[128,640]{1,0:T(8,128)(2,1)S(1)}, bf16[128,640]{1,0:T(8,128)(2,1)S(1)}, u32[]{:S(2)}, u32[]{:S(2)}) collective-permute-start(bf16[128,640]{1,0:T(8,128)(2,1)S(1)} %combine.1.refs_7_), channel_id=1, source_target_pairs={{0,8},{4,12},{8,0},{12,4},{16,24},{20,28},{24,16},{28,20},{1,9},{5... | collective-permute-start | bytes 491528 | tf_op jit(solution)/shard_map/ppermute | solution.py:35
  28.6 3.9 %copy-start.6 = (bf16[16,128,128]{2,1,0:T(8,128)(2,1)S(1)}, bf16[16,128,128]{2,1,0:T(8,128)(2,1)}, u32[]{:S(2)}) copy-start(bf16[16,128,128]{2,1,0:T(8,128)(2,1)} %tiles_ref.1) | copy-start | bytes 1572868
  30.2 3.8 %collective-permute-start.10 = (bf16[144,512]{1,0:T(8,128)(2,1)S(1)}, bf16[144,512]{1,0:T(8,128)(2,1)S(1)}, u32[]{:S(2)}, u32[]{:S(2)}) collective-permute-start(bf16[144,512]{1,0:T(8,128)(2,1)S(1)} %get-tuple-element.45), channel_id=1, source_target_pairs={{0,1},{1,0},{2,3},{3,2},{4,5},{5,4},{6,7},{7,6},{8,9},{9,8},{10,11... | collective-permute-start | bytes 442376 | tf_op jit(solution)/shard_map/ppermute | solution.py:35
  30.2 2.3 %copy-start.4 = (bf16[512,1024]{1,0:T(8,128)(2,1)S(1)}, bf16[512,1024]{1,0:T(8,128)(2,1)}, u32[]{:S(2)}) copy-start(bf16[512,1024]{1,0:T(8,128)(2,1)} %refs_8_.1) | copy-start | bytes 3145732
  30.3 2.3 %copy-start.5 = (bf16[1024,512]{1,0:T(8,128)(2,1)S(1)}, bf16[1024,512]{1,0:T(8,128)(2,1)}, u32[]{:S(2)}) copy-start(bf16[1024,512]{1,0:T(8,128)(2,1)} %refs_9_.1) | copy-start | bytes 3145732
  30.3 1.5 %collective-permute-start.16 = (bf16[128,512]{1,0:T(8,128)(2,1)S(1)}, bf16[128,512]{1,0:T(8,128)(2,1)S(1)}, u32[]{:S(2)}, u32[]{:S(2)}) collective-permute-start(bf16[128,512]{1,0:T(8,128)(2,1)S(1)} %rows.5), channel_id=1, source_target_pairs={{0,1},{1,0},{2,3},{3,2},{4,5},{5,4},{6,7},{7,6},{8,9},{9,8},{10,11... | collective-permute-start | bytes 393224 | tf_op jit(solution)/shard_map/ppermute | solution.py:35
  30.9 1.4 %collective-permute-start.15 = (bf16[128,512]{1,0:T(8,128)(2,1)S(1)}, bf16[128,512]{1,0:T(8,128)(2,1)S(1)}, u32[]{:S(2)}, u32[]{:S(2)}) collective-permute-start(bf16[128,512]{1,0:T(8,128)(2,1)S(1)} %rows.4), channel_id=1, source_target_pairs={{0,1},{1,0},{2,3},{3,2},{4,5},{5,4},{6,7},{7,6},{8,9},{9,8},{10,11... | collective-permute-start | bytes 393224 | tf_op jit(solution)/shard_map/ppermute | solution.py:35
  31.0 1.6 %copy-start.8 = (f32[512]{0:T(512)S(1)}, f32[512]{0:T(512)}, u32[]{:S(2)}) copy-start(f32[512]{0:T(512)} %param.21) | copy-start | bytes 6148
  31.0 1.5 %collective-permute-start.14 = (bf16[128,512]{1,0:T(8,128)(2,1)S(1)}, bf16[128,512]{1,0:T(8,128)(2,1)S(1)}, u32[]{:S(2)}, u32[]{:S(2)}) collective-permute-start(bf16[128,512]{1,0:T(8,128)(2,1)S(1)} %rows.3), channel_id=1, source_target_pairs={{0,1},{1,0},{2,3},{3,2},{4,5},{5,4},{6,7},{7,6},{8,9},{9,8},{10,11... | collective-permute-start | bytes 393224 | tf_op jit(solution)/shard_map/ppermute | solution.py:35
  32.6 1.5 %copy-start.7 = (bf16[512,512]{1,0:T(8,128)(2,1)S(1)}, bf16[512,512]{1,0:T(8,128)(2,1)}, u32[]{:S(2)}) copy-start(bf16[512,512]{1,0:T(8,128)(2,1)} %final_ref.1) | copy-start | bytes 1572868

commit v6 on v5

--- a/solution.py
+++ b/solution.py
@@ -189,33 +189,33 @@
     )(softness, slots, both, side, asking, lookup, content)
 
 
-def near_kernel(scale_ref, held_keys, held_values, others_ref, *refs):
+def near_kernel(scale_ref, held_keys, held_values, other_ref, first_ref, second_ref, *refs):
     blocks, (asking_ref, lookup_ref, content_ref) = refs[:-8], refs[-8:-5]
     queries_ref, keys_ref, values_ref, numer_ref, denom_ref = refs[-5:]
-    half, held = others_ref.shape[0] // 2, held_keys.shape[0]
+    held = held_keys.shape[0]
     keys_ref[:held, :] = held_keys[...]
     values_ref[:held, :] = held_values[...]
     nodes = [block[...] for block in blocks]
     keys_values(nodes, lookup_ref, content_ref, keys_ref.at[held:], values_ref.at[held:])
-    rows = jnp.concatenate([others_ref[half:, :], others_ref[:half, :]], axis=0)
+    rows = jnp.concatenate([first_ref[...], second_ref[...], other_ref[...]], axis=0)
     queries = (head_normed(dot(rows, asking_ref[...])) * scale_ref[...]).astype(BF16)
     queries_ref[...] = queries
     numer_ref[...], denom_ref[...] = attend(queries, keys_ref, values_ref)
 
 
 def near(scale, keys, values, others, blocks, asking, lookup, content):
-    rows, width = others.shape
+    rows, width = 2 * others[0].shape[0], others[0].shape[1]
     count = keys.shape[0] + sum(block.shape[0] for block in blocks)
     array = lambda n, dtype: jax.ShapeDtypeStruct((n, width), dtype)
     return pl.pallas_call(
         near_kernel,
         out_shape=(array(rows, BF16),) + (array(count, BF16),) * 2 + (array(rows, F32),) * 2,
-        in_specs=[VMEM] * (7 + len(blocks)),
+        in_specs=[VMEM] * (6 + len(others) + len(blocks)),
         out_specs=(VMEM,) * 5,
         compiler_params=params(16),
         cost_estimate=cost(6 * rows * count * width, rows * count * NUM_SUBSPACES, 4 << 20),
         name="near",
-    )(scale, keys, values, others, *blocks, asking, lookup, content)
+    )(scale, keys, values, *others, *blocks, asking, lookup, content)
 
 
 def pack(numer, denom):
@@ -422,53 +422,86 @@
     )(numer, denom, packed, *after)
 
 
-def message_kernel(slots_ref, tiles_ref, *refs):
-    both_ref, side_ref, across_ref, halo_ref, got_ref, *got_halo = refs[:8]
-    inner_ref, outer_ref, gain_ref, local_ref, gain_out, slots, sem = refs[8:]
+def around_kernel(slots_ref, twin_ref, tiles_ref, both_ref, side_ref, across_ref, halo_ref, *refs):
+    mine_ref, theirs_ref, slots, sems = refs
+    copies = [
+        pltpu.make_async_copy(source, slots.at[i], sems.at[i])
+        for i, source in enumerate((slots_ref, twin_ref))
+    ]
+    for copy in copies:
+        copy.start()
+    group = slots_ref.shape[1] // 3
+    me, core = lax.axis_index("head"), lax.axis_index("head") % 2
+    part, parts = lax.axis_index("dom"), lax.axis_size("dom")
+    beside, beyond = 2 - 2 * (part % 2), 2 * (part % 2)
+    inside = (part != 0) & (part != parts - 1)
+    pick = lambda first, second: first + core * (second - first)
+    order = [(1, 0, True), (pick(beside, 1), pick(0, 2), True), (pick(beside, 1), pick(1, 3), True)]
+    order += [(beside, 2, True), (beyond, 0, inside & (core == 0)), (beyond, 1, inside & (core == 0))]
+    order += [(beyond, 2, inside)]
+    rows = across_ref.shape[0]
+    nodes = [both_ref[:rows, :], side_ref[...], across_ref[...], halo_ref[...]]
+    for copy in copies:
+        copy.wait()
+    wide = []
+    for receiver in range(2):
+        tiles = []
+        for side, offset, held in order:
+            tile_id = slots[receiver, 0, side * group + (me ^ offset)]
+            tile = tiles_ref[jnp.maximum(tile_id, 0)]
+            tiles.append(jnp.where((tile_id >= 0) & held, tile, jnp.zeros_like(tile)))
+        wide.append(jnp.concatenate(tiles, axis=1))
+    sums = dot(jnp.concatenate(wide, axis=0), jnp.concatenate(nodes, axis=0))
+    mine_ref[...] = sums[:rows]
+    theirs_ref[...] = sums[rows:].astype(BF16)
+
+
+def around(slots, twin_slots, tiles, blocks, kept, after):
+    rows, width = tiles.shape[1], blocks[0].shape[1]
+
+    def body(*refs):
+        around_kernel(*refs[:7], *refs[8 + len(after) :])
+
+    return pl.pallas_call(
+        body,
+        out_shape=(
+            jax.ShapeDtypeStruct((rows, width), F32),
+            jax.ShapeDtypeStruct((rows, width), BF16),
+        ),
+        in_specs=[VMEM] * 8 + [ANY] * len(after),
+        out_specs=(VMEM,) * 2,
+        scratch_shapes=[
+            pltpu.SMEM((2,) + slots.shape, jnp.int32),
+            pltpu.SemaphoreType.DMA((2,)),
+        ],
+        compiler_params=params(8),
+        cost_estimate=cost(28 * rows * rows * width, 0, 1 << 20),
+        name="around",
+    )(slots, twin_slots, tiles, *blocks, kept, *after)
+
+
+def message_kernel(mine_ref, got_ref, inner_ref, outer_ref, gain_ref, local_ref, gain_out):
     gain_out[...] = gain_ref[...]
-    copy = pltpu.make_async_copy(slots_ref, slots, sem)
-    copy.start()
-    group = slots_ref.shape[1] // 3
-    me, core, odd = lax.axis_index("head"), lax.axis_index("head") % 2, lax.axis_index("dom") % 2
-    beside, beyond = 2 - 2 * odd, 2 * odd
-    part, parts = lax.axis_index("dom"), lax.axis_size("dom")
-    outside = (part == 0) | (part == parts - 1)
-    pick = lambda first, second: first + core * (second - first)
-    order = [(1, 0), (1, 1)]
-    order += [(pick(beside, 1), pick(0, 2)), (pick(beside, 1), pick(1, 3)), (beside, 2)]
-    order += [(pick(1, beside), pick(3, 1)), (pick(1, beside), pick(2, 0)), (beside, 3)]
-    order += [(beyond, core), (beyond, 1 - core), (beyond, 2), (beyond, 3)]
-    rows = across_ref.shape[0]
-    kept = halo_ref[: 2 * rows, :]
-    sent = jnp.concatenate([got_halo[0][...], got_halo[1][...]], axis=0)
-    nodes = [both_ref[...], side_ref[...], across_ref[...], got_ref[...]]
-    nodes += [jnp.where(core == 0, kept, sent), halo_ref[2 * rows :, :], got_halo[2][...]]
-    copy.wait()
-    tiles = []
-    for side, offset in order:
-        tile_id = slots[0, side * group + (me ^ offset)]
-        tile_id = jnp.where(outside & (side == beyond), -1, tile_id)
-        tile = tiles_ref[jnp.maximum(tile_id, 0)]
-        tiles.append(jnp.where(tile_id >= 0, tile, jnp.zeros_like(tile)))
-    aggregate = dot(jnp.concatenate(tiles, axis=1), jnp.concatenate(nodes, axis=0)).astype(BF16)
+    aggregate = (mine_ref[...] + got_ref[...].astype(F32)).astype(BF16)
     hidden = jax.nn.gelu(dot(aggregate, inner_ref[...])).astype(BF16)
     local_ref[...] = dot(hidden, outer_ref[...])
 
 
-def message(slots, tiles, blocks, inner, outer, gain):
-    rows, width, hidden = tiles.shape[1], inner.shape[0], inner.shape[1]
+def message(mine, got, inner, outer, gain):
+    rows, width = mine.shape
+    hidden = inner.shape[1]
     return pl.pallas_call(
         message_kernel,
-        out_shape=(jax.ShapeDtypeStruct((rows, width), F32), jax.ShapeDtypeStruct(gain.shape, F32)),
-        in_specs=[VMEM] + [VMEM] * (4 + len(blocks)),
+        out_shape=(
+            jax.ShapeDtypeStruct((rows, width), F32),
+            jax.ShapeDtypeStruct(gain.shape, F32),
+        ),
+        in_specs=[VMEM] * 5,
         out_specs=(VMEM,) * 2,
-        scratch_shapes=[pltpu.SMEM(slots.shape, jnp.int32), pltpu.SemaphoreType.DMA],
         compiler_params=params(16),
-        cost_estimate=cost(
-            2 * rows * width * (12 * rows + 2 * hidden), rows * hidden, 4 << 20
-        ),
+        cost_estimate=cost(4 * rows * width * hidden, rows * hidden, 4 << 20),
         name="message",
-    )(slots, tiles, *blocks, inner, outer, gain)
+    )(mine, got, inner, outer, gain)
 
 
 def finish_kernel(
@@ -530,11 +563,13 @@
         return below, side, across
 
     held = lineup((nodes,))
+    twin_slots = swap(adjacent_group_bank_ids.reshape(1, -1), "head", 1)
     both = lineup((held, swap(nodes, "head", 1)))
     side = swap_by_core(both, (1, 0), (0, 2))
     across = swap_by_core(lineup((side,), (), block_len), (0, 2), (1, 0))
     other = swap(nodes, "dom", 2)
-    others = lineup((other, swap(other, "head", 1)))
+    halves = [rows_of(other, at, block_len // 2) for at in (0, block_len // 2)]
+    others = (other,) + tuple(swap(part, "head", 1) for part in halves)
     queries, scale, keys, values, slots = early(
         softness_per_subspace,
         adjacent_group_bank_ids.reshape(1, -1),
@@ -563,7 +598,8 @@
         content_projector,
     )
 
-    pairs = [(p, p + 2) for p in range(0, doms - 2, 2)] + [(p, p - 2) for p in range(3, doms, 2)]
+    pairs = [(p, p + 2) for p in range(0, doms - 2, 2)] + [(doms - 2, doms - 1)]
+    pairs += [(p, p - 2) for p in range(3, doms, 2)] + [(1, 0)]
     halo = lax.ppermute(lineup((side, across), ()), "dom", pairs)
     far_keys, far_values, packed, numer, denom = far(
         far_blocks, block_len, lookup_projector, content_projector, pair_queries, numer, denom
@@ -575,14 +611,17 @@
     )
     crossed = swap(crossed, "head", 1)
     packed = swap(packed, "dom", 2)
-    got = swap(lineup((side, across)), "head", 1)
-    got_halo = [
-        swap(rows_of(halo, at * block_len, block_len, (numer,)), "head", 1) for at in range(3)
-    ]
+    mine, theirs = around(
+        slots,
+        twin_slots,
+        coupling_strength_panels,
+        (both, side, across, halo),
+        final_projector,
+        (numer,),
+    )
     local, gain = message(
-        slots,
-        coupling_strength_panels,
-        (both, side, across, halo, got, *got_halo),
+        mine,
+        swap(theirs, "head", 1),
         passing_inner_coefficients,
         passing_outer_coefficients,
         mixing_layer_gain.reshape(1, -1),

time: 35.5 us -> 35 us (0.986)
  starting transfers between devices: 18.3 us -> 17.4 us
  Pallas kernels: 12.2 us -> 11.3 us
  local copies, waits for them, and re-layouts: 1.12 us -> 2 us
  waiting for transfers between devices: 3.46 us -> 3.9 us
    ppermute x1, starting transfers between devices: 2.36 us -> 1.15 us  [shards(): halo = lax.ppermute(lineup((side, across), ()), 'dom', pairs)]
    pallas_call x0 -> x1, Pallas kernels: none -> 1.01 us  [around(): pl.pallas_call(body, out_shape=(jax.ShapeDtypeStruct((rows, width), F32),...]
    pallas_call x6 -> x5, Pallas kernels: 1.05 us -> 0.07 us  [lineup(): pl.pallas_call(functools.partial(lineup_kernel, len(blocks), rows), out_s...]
    pallas_call x1, Pallas kernels: 1.45 us -> 0.55 us  [message(): pl.pallas_call(message_kernel, out_shape=(jax.ShapeDtypeStruct((rows, wid...]
    unnamed x22 -> x26, local copies, waits for them, and re-layouts: 1.12 us -> 2 us
    ppermute x13 -> x12, starting transfers between devices: 9.39 us -> 10 us  [swap(): return lax.ppermute(array, axis, [(i, i ^ mask) for i in range(devices)])]
    ppermute x13 -> x12, waiting for transfers between devices: 3.27 us -> 3.71 us  [swap(): return lax.ppermute(array, axis, [(i, i ^ mask) for i in range(devices)])]
  transfers between devices with their start and end apart: 17 -> 16, of which waited for: 9 -> 8; matrix products, arithmetic and copies ran while one was open for 0% -> 0% of each run, Pallas kernels for 31% -> 29%
where the time goes in v6:
time: 35 us; the launch traced here: 34.8 us
  starting transfers between devices  17.4 us (50%)
  Pallas kernels  11.3 us (32%)
  waiting for transfers between devices  3.9 us (11%)
  local copies, waits for them, and re-layouts  2 us (6%)
    ppermute x12, starting transfers between devices, swap(): return lax.ppermute(array, axis, [(i, i ^ mask) for i in range(devices)])  10 us
    ppermute x2, starting transfers between devices, swap_by_core(): return lax.ppermute(array, ('dom', 'head'), pairs)  5.03 us
    ppermute x12, waiting for transfers between devices, swap(): return lax.ppermute(array, axis, [(i, i ^ mask) for i in range(devices)])  3.71 us
    pallas_call x2, Pallas kernels, call(): pl.pallas_call(body, grid=grid, out_shape=tuple(out_parts) + tuple(out_wh...  2.89 us
    pallas_call x1, Pallas kernels, near(): pl.pallas_call(near_kernel, out_shape=(array(rows, BF16),) + (array(count...  2.88 us
    unnamed x26, local copies, waits for them, and re-layouts  2 us
    pallas_call x1, Pallas kernels, own_first(): pl.pallas_call(own_first_kernel, out_shape=(jax.ShapeDtypeStruct((rows, w...  1.36 us
    pallas_call x1, Pallas kernels, finish(): pl.pallas_call(finish_kernel, out_shape=jax.ShapeDtypeStruct((rows, width...  1.22 us
  transfers between devices with their start and end apart: 16, of which 8 were waited for; matrix products, arithmetic and copies ran while one was open for 0% of the time, Pallas kernels for 29%

profile of v6, /device:TPU:0, one launch (start us, length us, event | category | flops | bytes accessed | tf_op | source)
XLA Modules:
  0.0 34.8 jit_solution(12679208717424234184)
XLA Ops:
  0.0 0.5 %collective-permute-start.1 = (bf16[128,512]{1,0:T(8,128)(2,1)}, bf16[128,512]{1,0:T(8,128)(2,1)S(1)}, u32[]{:S(2)}, u32[]{:S(2)}) collective-permute-start(bf16[128,512]{1,0:T(8,128)(2,1)} %refs_0_.1), channel_id=1, source_target_pairs={{0,1},{1,0},{2,3},{3,2},{4,5},{5,4},{6,7},{7,6},{8,9},{9,8},{10,11... | collective-permute-start | bytes 393224 | tf_op jit(solution)/shard_map/ppermute | solution.py:35
  0.5 0.9 %copy-done.8 = bf16[128,512]{1,0:T(8,128)(2,1)S(1)} copy-done((bf16[128,512]{1,0:T(8,128)(2,1)S(1)}, bf16[128,512]{1,0:T(8,128)(2,1)}, u32[]{:S(2)}) %copy-start.8) | copy-done | bytes 131096
  1.4 0.0 copy-start
  1.4 0.3 collective-permute-done.1.refs_1_
  1.7 2.9 %collective-permute-start.2 = (bf16[256,512]{1,0:T(8,128)(2,1)S(1)}, bf16[256,512]{1,0:T(8,128)(2,1)S(1)}, u32[]{:S(2)}, u32[]{:S(2)}) collective-permute-start(bf16[256,512]{1,0:T(8,128)(2,1)S(1)} %lineup.6.both_ref.refs_3_), channel_id=1, source_target_pairs={{0,4},{1,3},{2,6},{3,1},{4,0},{5,7},{6,2},{7,5},{8,12},{9,11},{10,... | collective-permute-start | bytes 786440 | tf_op jit(solution)/shard_map/ppermute | solution.py:55
  4.6 2.6 %collective-permute-start = (bf16[128,512]{1,0:T(8,128)(2,1)S(1)}, bf16[128,512]{1,0:T(8,128)(2,1)S(1)}, u32[]{:S(2)}, u32[]{:S(2)}) collective-permute-start(bf16[128,512]{1,0:T(8,128)(2,1)S(1)} %copy-done.9), channel_id=1, source_target_pairs={{0,16},{4,20},{8,24},{12,28},{16,0},{20,4},{24,8},{28,12},{1,17},{... | collective-permute-start | bytes 393224 | tf_op jit(solution)/shard_map/ppermute | solution.py:35
  7.2 1.6 %collective-permute-start.5 = (bf16[128,512]{1,0:T(8,128)(2,1)S(1)}, bf16[128,512]{1,0:T(8,128)(2,1)S(1)}, u32[]{:S(2)}, u32[]{:S(2)}) collective-permute-start(bf16[128,512]{1,0:T(8,128)(2,1)S(1)} %copy-done.9), channel_id=1, source_target_pairs={{0,8},{4,12},{8,0},{12,4},{16,24},{20,28},{24,16},{28,20},{1,9},{5... | collective-permute-start | bytes 393224 | tf_op jit(solution)/shard_map/ppermute | solution.py:35
  8.8 0.2 collective-permute-done.2.side_ref.refs_0_.refs_4_
  9.0 0.0 copy-start.11
  9.0 0.0 copy-start.12
  9.0 2.1 %collective-permute-start.8 = (bf16[128,512]{1,0:T(8,128)(2,1)S(1)}, bf16[128,512]{1,0:T(8,128)(2,1)S(1)}, u32[]{:S(2)}, u32[]{:S(2)}) collective-permute-start(bf16[128,512]{1,0:T(8,128)(2,1)S(1)} %lineup.8), channel_id=1, source_target_pairs={{0,2},{1,5},{2,0},{3,7},{4,6},{5,1},{6,4},{7,3},{8,10},{9,13},{10,... | collective-permute-start | bytes 393224 | tf_op jit(solution)/shard_map/ppermute | solution.py:55
  11.1 0.0 copy-start.2
  11.1 1.0 %copy-done.2 = bf16[512,512]{1,0:T(8,128)(2,1)S(1)} copy-done((bf16[512,512]{1,0:T(8,128)(2,1)S(1)}, bf16[512,512]{1,0:T(8,128)(2,1)}, u32[]{:S(2)}) %copy-start.2) | copy-done | bytes 524312
  12.1 1.1 %early.1 = (bf16[256,512]{1,0:T(8,128)(2,1)S(1)}, f32[1,512]{1,0:T(1,128)S(1)}, bf16[384,512]{1,0:T(8,128)(2,1)S(1)}, bf16[384,512]{1,0:T(8,128)(2,1)S(1)}, s32[1,12]{1,0:T(1,128)S(1)}) custom-call(f32[8]{0:T(128)S(1)} %copy-done.11, s32[1,12]{1,0:T(1,128)S(1)} %bitcast.3, bf16[256,512]{1,0:T(8,128)(2,1)S(1)} %lineup.6.both_ref.refs_3_, ...), custom_call_target="tpu_custom_call" | custom-call | flops 33554432 | bytes 262144 | tf_op jit(solution)/shard_map/early/pallas_call | solution.py:179
  13.3 0.4 %collective-permute-done.refs_0_ = bf16[128,512]{1,0:T(8,128)(2,1)S(1)} collective-permute-done((bf16[128,512]{1,0:T(8,128)(2,1)S(1)}, bf16[128,512]{1,0:T(8,128)(2,1)S(1)}, u32[]{:S(2)}, u32[]{:S(2)}) %collective-permute-start) | collective-permute-done | bytes 131104 | tf_op jit(solution)/shard_map/ppermute | solution.py:35
  13.7 1.1 %collective-permute-start.9 = (bf16[128,512]{1,0:T(8,128)(2,1)S(1)}, bf16[128,512]{1,0:T(8,128)(2,1)S(1)}, u32[]{:S(2)}, u32[]{:S(2)}) collective-permute-start(bf16[128,512]{1,0:T(8,128)(2,1)S(1)} %lineup.7.refs_1_), channel_id=1, source_target_pairs={{0,4},{4,0},{8,12},{12,8},{16,20},{20,16},{24,28},{28,24},{1,5},{5... | collective-permute-start | bytes 393224 | tf_op jit(solution)/shard_map/ppermute | solution.py:35
  14.8 1.2 %collective-permute-start.3 = (bf16[128,512]{1,0:T(8,128)(2,1)S(1)}, bf16[128,512]{1,0:T(8,128)(2,1)S(1)}, u32[]{:S(2)}, u32[]{:S(2)}) collective-permute-start(bf16[128,512]{1,0:T(8,128)(2,1)S(1)} %lineup.7.refs_1_), channel_id=1, source_target_pairs={{0,2},{1,3},{2,0},{3,1},{4,6},{5,7},{6,4},{7,5},{8,10},{9,11},{10,... | collective-permute-start | bytes 393224 | tf_op jit(solution)/shard_map/ppermute | solution.py:35
  16.1 1.2 %collective-permute-start.4 = (bf16[128,512]{1,0:T(8,128)(2,1)S(1)}, bf16[128,512]{1,0:T(8,128)(2,1)S(1)}, u32[]{:S(2)}, u32[]{:S(2)}) collective-permute-start(bf16[128,512]{1,0:T(8,128)(2,1)S(1)} %lineup.7.refs_1_), channel_id=1, source_target_pairs={{0,6},{1,7},{2,4},{3,5},{4,2},{5,3},{6,0},{7,1},{8,14},{9,15},{10,... | collective-permute-start | bytes 393224 | tf_op jit(solution)/shard_map/ppermute | solution.py:45
  17.3 0.0 copy-start.3
  17.3 0.1 collective-permute-start.6
  17.4 0.5 %collective-permute-start.7 = (bf16[64,512]{1,0:T(8,128)(2,1)S(1)}, bf16[64,512]{1,0:T(8,128)(2,1)S(1)}, u32[]{:S(2)}, u32[]{:S(2)}) collective-permute-start(bf16[64,512]{1,0:T(8,128)(2,1)S(1)} %rows.3), channel_id=1, source_target_pairs={{0,1},{1,0},{2,3},{3,2},{4,5},{5,4},{6,7},{7,6},{8,9},{9,8},{10,11... | collective-permute-start | bytes 196616 | tf_op jit(solution)/shard_map/ppermute | solution.py:35
  18.0 0.6 %collective-permute-done.6.first_ref = bf16[64,512]{1,0:T(8,128)(2,1)S(1)} collective-permute-done((bf16[64,512]{1,0:T(8,128)(2,1)S(1)}, bf16[64,512]{1,0:T(8,128)(2,1)S(1)}, u32[]{:S(2)}, u32[]{:S(2)}) %collective-permute-start.6) | collective-permute-done | bytes 65568 | tf_op jit(solution)/shard_map/ppermute | solution.py:35
  18.6 1.2 %collective-permute-start.14 = (bf16[384,512]{1,0:T(8,128)(2,1)S(1)}, bf16[384,512]{1,0:T(8,128)(2,1)S(1)}, u32[]{:S(2)}, u32[]{:S(2)}) collective-permute-start(bf16[384,512]{1,0:T(8,128)(2,1)S(1)} %lineup.9), channel_id=1, source_target_pairs={{0,8},{8,16},{16,24},{24,28},{12,4},{20,12},{28,20},{4,0},{1,9},{9... | collective-permute-start | bytes 1179656 | tf_op jit(solution)/shard_map/ppermute | solution.py:603
  19.8 0.0 collective-permute-done.7.second_ref
  19.8 0.0 collective-permute-done.9.refs_2_
  19.8 2.9 %near.1 = (bf16[256,512]{1,0:T(8,128)(2,1)S(1)}, bf16[768,512]{1,0:T(8,128)(2,1)S(1)}, bf16[768,512]{1,0:T(8,128)(2,1)S(1)}, f32[256,512]{1,0:T(8,128)S(1)}, f32[256,512]{1,0:T(8,128)S(1)}) custom-call(f32[1,512]{1,0:T(1,128)S(1)} %get-tuple-element.30.scale_ref, bf16[384,512]{1,0:T(8,128)(2,1)S(1)} %get-tuple-element.31.held_keys, ...), custom_call_target="tpu_custom_call" | custom-call | flops 37748736 | bytes 262144 | tf_op jit(solution)/shard_map/near/pallas_call | solution.py:210
  22.7 0.2 collective-permute-done.3.refs_0_
  22.8 0.0 collective-permute-done.4.refs_1_
  22.8 1.3 %far.1 = (bf16[256,512]{1,0:T(8,128)(2,1)S(1)}, bf16[256,512]{1,0:T(8,128)(2,1)S(1)}, bf16[256,640]{1,0:T(8,128)(2,1)S(1)}, f32[128,512]{1,0:T(8,128)S(1)}, f32[128,512]{1,0:T(8,128)S(1)}) custom-call(bf16[128,512]{1,0:T(8,128)(2,1)S(1)} %collective-permute-done.3.refs_0_, bf16[128,512]{1,0:T(8,128)(2,1)S(1)} %collective-permute-done.4.refs_1_, ...), custom_call_target="tpu_custom_call" | custom-call | flops 12582912 | bytes 262144 | tf_op jit(solution)/shard_map/far/pallas_call | solution.py:272
  24.1 0.1 collective-permute-start.10
  24.2 1.4 %own_first.1 = (f32[256,512]{1,0:T(8,128)S(1)}, f32[256,512]{1,0:T(8,128)S(1)}) custom-call(bf16[256,512]{1,0:T(8,128)(2,1)S(1)} %get-tuple-element.29.refs_1_.queries_ref.refs_2_, bf16[768,512]{1,0:T(8,128)(2,1)S(1)} %get-tuple-element.38.keys_ref.refs_3_, bf16[768,512]{1,0:T(8,128)(2,1)S(1)} %get-tuple-element.39.values_ref.refs_4_, ...), custom_call_target="tpu_custom_call" | custom-call | flops 16777216 | bytes 131072 | tf_op jit(solution)/shard_map/own_first/pallas_call | solution.py:345
  25.6 0.2 collective-permute-done.10.packed_ref
  25.8 0.2 combine.1.refs_7_
  26.1 1.5 %collective-permute-start.12 = (bf16[128,640]{1,0:T(8,128)(2,1)S(1)}, bf16[128,640]{1,0:T(8,128)(2,1)S(1)}, u32[]{:S(2)}, u32[]{:S(2)}) collective-permute-start(bf16[128,640]{1,0:T(8,128)(2,1)S(1)} %combine.1.refs_7_), channel_id=1, source_target_pairs={{0,8},{4,12},{8,0},{12,4},{16,24},{20,28},{24,16},{28,20},{1,9},{5... | collective-permute-start | bytes 491528 | tf_op jit(solution)/shard_map/ppermute | solution.py:35
  27.6 1.6 %own.1 = (bf16[144,512]{1,0:T(8,128)(2,1)S(1)}, f32[128,512]{1,0:T(8,128)S(1)}, f32[128,512]{1,0:T(8,128)S(1)}) custom-call(bf16[256,512]{1,0:T(8,128)(2,1)S(1)} %get-tuple-element.36.refs_0_, bf16[256,512]{1,0:T(8,128)(2,1)S(1)} %get-tuple-element.37.refs_1_, bf16[256,512]{1,0:T(8,128)(2,1)S(1)} %get-tuple-element.29.refs_1_.queries_ref.refs_2_, ...), custom_call_target="tpu_custom_call" | custom-call | flops 16777216 | bytes 262144 | tf_op jit(solution)/shard_map/own/pallas_call | solution.py:272
  29.2 0.0 collective-permute-start.11
  29.2 0.5 %collective-permute-start.13 = (s32[1,12]{1,0:T(1,128)S(1)}, s32[1,12]{1,0:T(1,128)S(1)}, u32[]{:S(2)}, u32[]{:S(2)}) collective-permute-start(s32[1,12]{1,0:T(1,128)S(1)} %bitcast.4), channel_id=1, source_target_pairs={{0,1},{1,0},{2,3},{3,2},{4,5},{5,4},{6,7},{7,6},{8,9},{9,8},{10,11... | collective-permute-start | bytes 152 | tf_op jit(solution)/shard_map/ppermute | solution.py:35
  29.7 0.9 %collective-permute-done.13.refs_1_ = s32[1,12]{1,0:T(1,128)S(1)} collective-permute-done((s32[1,12]{1,0:T(1,128)S(1)}, s32[1,12]{1,0:T(1,128)S(1)}, u32[]{:S(2)}, u32[]{:S(2)}) %collective-permute-start.13) | collective-permute-done | bytes 80 | tf_op jit(solution)/shard_map/ppermute | solution.py:35
  30.6 0.0 collective-permute-done.14.refs_6_
  30.6 0.0 copy-start.5
  30.6 0.0 copy-start.6
  30.6 1.0 %around.1 = (f32[128,512]{1,0:T(8,128)S(1)}, bf16[128,512]{1,0:T(8,128)(2,1)S(1)}) custom-call(s32[1,12]{1,0:T(1,128)S(1)} %get-tuple-element.48.refs_0_, s32[1,12]{1,0:T(1,128)S(1)} %collective-permute-done.13.refs_1_, bf16[16,128,128]{2,1,0:T(8,128)(2,1)S(1)} %copy-done.7, bf16[256,512]{1,0:T(8,128)(2,1)S(1)} %lineup.6.both_ref.refs_3_, ...), custom_call_target="tpu_custom_call" | custom-call | flops 14680064 | bytes 65536 | tf_op jit(solution)/shard_map/around/pallas_call | solution.py:465
  31.6 0.0 copy-start.10
  31.6 0.3 collective-permute-start.15
  31.9 1.1 %collective-permute-done.15.got_ref = bf16[128,512]{1,0:T(8,128)(2,1)S(1)} collective-permute-done((bf16[128,512]{1,0:T(8,128)(2,1)S(1)}, bf16[128,512]{1,0:T(8,128)(2,1)S(1)}, u32[]{:S(2)}, u32[]{:S(2)}) %collective-permute-start.15) | collective-permute-done | bytes 131104 | tf_op jit(solution)/shard_map/ppermute | solution.py:35
  33.0 0.6 %message.1 = (f32[128,512]{1,0:T(8,128)S(1)}, f32[1,512]{1,0:T(1,128)S(1)}) custom-call(f32[128,512]{1,0:T(8,128)S(1)} %get-tuple-element.49.mine_ref, bf16[128,512]{1,0:T(8,128)(2,1)S(1)} %collective-permute-done.15.got_ref, bf16[512,1024]{1,0:T(8,128)(2,1)S(1)} %copy-done.5, bf16[1024,512]{1,0:T(8,128)(2,1)S(1)} %copy-done.6, f32[1,512]{1,0:T(1,128)S(1)} %bitcast.2), custom_call_target="tpu_custom_call" | custom-call | flops 16777216 | bytes 262144 | tf_op jit(solution)/shard_map/message/pallas_call | solution.py:493
  33.6 0.0 collective-permute-done.11.crossed_ref
  33.6 1.2 %finish.1 = bf16[128,512]{1,0:T(8,128)(2,1)} custom-call(f32[128,512]{1,0:T(8,128)S(1)} %get-tuple-element.45.refs_8_.numer_ref, f32[128,512]{1,0:T(8,128)S(1)} %get-tuple-element.46.denom_ref, bf16[144,512]{1,0:T(8,128)(2,1)S(1)} %collective-permute-done.11.crossed_ref, bf16[128,640]{1,0:T(8,128)(2,1)S(1)} %collective-permute-done.12.packed_ref, ...), custom_call_target="tpu_custom_call" | custom-call | flops 4194304 | bytes 131072 | tf_op jit(solution)/shard_map/finish/pallas_call | solution.py:524
  (26 shorter events, 0.1 us)
Async XLA Ops:
  0.0 1.6 %collective-permute-start.1 = (bf16[128,512]{1,0:T(8,128)(2,1)}, bf16[128,512]{1,0:T(8,128)(2,1)S(1)}, u32[]{:S(2)}, u32[]{:S(2)}) collective-permute-start(bf16[128,512]{1,0:T(8,128)(2,1)} %refs_0_.1), channel_id=1, source_target_pairs={{0,1},{1,0},{2,3},{3,2},{4,5},{5,4},{6,7},{7,6},{8,9},{9,8},{10,11... | collective-permute-start | bytes 393224 | tf_op jit(solution)/shard_map/ppermute | solution.py:35
  0.5 0.9 %copy-start.8 = (bf16[128,512]{1,0:T(8,128)(2,1)S(1)}, bf16[128,512]{1,0:T(8,128)(2,1)}, u32[]{:S(2)}) copy-start(bf16[128,512]{1,0:T(8,128)(2,1)} %refs_0_.1) | copy-start | bytes 393220
  1.4 3.2 %copy-start.9 = (bf16[128,512]{1,0:T(8,128)(2,1)S(1)}, bf16[128,512]{1,0:T(8,128)(2,1)}, u32[]{:S(2)}) copy-start(bf16[128,512]{1,0:T(8,128)(2,1)} %refs_0_.1) | copy-start | bytes 393220
  1.4 9.7 %copy-start.1 = (bf16[512,512]{1,0:T(8,128)(2,1)S(1)}, bf16[512,512]{1,0:T(8,128)(2,1)}, u32[]{:S(2)}) copy-start(bf16[512,512]{1,0:T(8,128)(2,1)} %refs_3_.3) | copy-start | bytes 1572868
  1.4 9.7 %copy-start = (bf16[512,512]{1,0:T(8,128)(2,1)S(1)}, bf16[512,512]{1,0:T(8,128)(2,1)}, u32[]{:S(2)}) copy-start(bf16[512,512]{1,0:T(8,128)(2,1)} %refs_2_.2) | copy-start | bytes 1572868
  1.7 7.3 %collective-permute-start.2 = (bf16[256,512]{1,0:T(8,128)(2,1)S(1)}, bf16[256,512]{1,0:T(8,128)(2,1)S(1)}, u32[]{:S(2)}, u32[]{:S(2)}) collective-permute-start(bf16[256,512]{1,0:T(8,128)(2,1)S(1)} %lineup.6.both_ref.refs_3_), channel_id=1, source_target_pairs={{0,4},{1,3},{2,6},{3,1},{4,0},{5,7},{6,2},{7,5},{8,12},{9,11},{10,... | collective-permute-start | bytes 786440 | tf_op jit(solution)/shard_map/ppermute | solution.py:55
  4.6 9.1 %collective-permute-start = (bf16[128,512]{1,0:T(8,128)(2,1)S(1)}, bf16[128,512]{1,0:T(8,128)(2,1)S(1)}, u32[]{:S(2)}, u32[]{:S(2)}) collective-permute-start(bf16[128,512]{1,0:T(8,128)(2,1)S(1)} %copy-done.9), channel_id=1, source_target_pairs={{0,16},{4,20},{8,24},{12,28},{16,0},{20,4},{24,8},{28,12},{1,17},{... | collective-permute-start | bytes 393224 | tf_op jit(solution)/shard_map/ppermute | solution.py:35
  7.2 10.1 %collective-permute-start.5 = (bf16[128,512]{1,0:T(8,128)(2,1)S(1)}, bf16[128,512]{1,0:T(8,128)(2,1)S(1)}, u32[]{:S(2)}, u32[]{:S(2)}) collective-permute-start(bf16[128,512]{1,0:T(8,128)(2,1)S(1)} %copy-done.9), channel_id=1, source_target_pairs={{0,8},{4,12},{8,0},{12,4},{16,24},{20,28},{24,16},{28,20},{1,9},{5... | collective-permute-start | bytes 393224 | tf_op jit(solution)/shard_map/ppermute | solution.py:35
  9.0 2.1 %copy-start.11 = (f32[8]{0:T(128)S(1)}, f32[8]{0:T(128)}, u32[]{:S(2)}) copy-start(f32[8]{0:T(128)} %softness_ref.1) | copy-start | bytes 100
  9.0 2.1 %copy-start.12 = (s32[1,1,12]{2,1,0:T(1,128)S(1)}, s32[1,1,12]{2,1,0:T(1,128)}, u32[]{:S(2)}) copy-start(s32[1,1,12]{2,1,0:T(1,128)} %param.12) | copy-start | bytes 148
  9.0 8.4 %collective-permute-start.8 = (bf16[128,512]{1,0:T(8,128)(2,1)S(1)}, bf16[128,512]{1,0:T(8,128)(2,1)S(1)}, u32[]{:S(2)}, u32[]{:S(2)}) collective-permute-start(bf16[128,512]{1,0:T(8,128)(2,1)S(1)} %lineup.8), channel_id=1, source_target_pairs={{0,2},{1,5},{2,0},{3,7},{4,6},{5,1},{6,4},{7,3},{8,10},{9,13},{10,... | collective-permute-start | bytes 393224 | tf_op jit(solution)/shard_map/ppermute | solution.py:55
  11.1 1.0 %copy-start.2 = (bf16[512,512]{1,0:T(8,128)(2,1)S(1)}, bf16[512,512]{1,0:T(8,128)(2,1)}, u32[]{:S(2)}) copy-start(bf16[512,512]{1,0:T(8,128)(2,1)} %refs_3_.2) | copy-start | bytes 1572868
  13.7 6.1 %collective-permute-start.9 = (bf16[128,512]{1,0:T(8,128)(2,1)S(1)}, bf16[128,512]{1,0:T(8,128)(2,1)S(1)}, u32[]{:S(2)}, u32[]{:S(2)}) collective-permute-start(bf16[128,512]{1,0:T(8,128)(2,1)S(1)} %lineup.7.refs_1_), channel_id=1, source_target_pairs={{0,4},{4,0},{8,12},{12,8},{16,20},{20,16},{24,28},{28,24},{1,5},{5... | collective-permute-start | bytes 393224 | tf_op jit(solution)/shard_map/ppermute | solution.py:35
  14.8 8.0 %collective-permute-start.3 = (bf16[128,512]{1,0:T(8,128)(2,1)S(1)}, bf16[128,512]{1,0:T(8,128)(2,1)S(1)}, u32[]{:S(2)}, u32[]{:S(2)}) collective-permute-start(bf16[128,512]{1,0:T(8,128)(2,1)S(1)} %lineup.7.refs_1_), channel_id=1, source_target_pairs={{0,2},{1,3},{2,0},{3,1},{4,6},{5,7},{6,4},{7,5},{8,10},{9,11},{10,... | collective-permute-start | bytes 393224 | tf_op jit(solution)/shard_map/ppermute | solution.py:35
  16.1 6.8 %collective-permute-start.4 = (bf16[128,512]{1,0:T(8,128)(2,1)S(1)}, bf16[128,512]{1,0:T(8,128)(2,1)S(1)}, u32[]{:S(2)}, u32[]{:S(2)}) collective-permute-start(bf16[128,512]{1,0:T(8,128)(2,1)S(1)} %lineup.7.refs_1_), channel_id=1, source_target_pairs={{0,6},{1,7},{2,4},{3,5},{4,2},{5,3},{6,0},{7,1},{8,14},{9,15},{10,... | collective-permute-start | bytes 393224 | tf_op jit(solution)/shard_map/ppermute | solution.py:45
  17.3 2.5 %copy-start.3 = (bf16[512,512]{1,0:T(8,128)(2,1)S(1)}, bf16[512,512]{1,0:T(8,128)(2,1)}, u32[]{:S(2)}) copy-start(bf16[512,512]{1,0:T(8,128)(2,1)} %refs_3_.2) | copy-start | bytes 1572868
  17.3 1.3 %collective-permute-start.6 = (bf16[64,512]{1,0:T(8,128)(2,1)S(1)}, bf16[64,512]{1,0:T(8,128)(2,1)S(1)}, u32[]{:S(2)}, u32[]{:S(2)}) collective-permute-start(bf16[64,512]{1,0:T(8,128)(2,1)S(1)} %rows.2), channel_id=1, source_target_pairs={{0,1},{1,0},{2,3},{3,2},{4,5},{5,4},{6,7},{7,6},{8,9},{9,8},{10,11... | collective-permute-start | bytes 196616 | tf_op jit(solution)/shard_map/ppermute | solution.py:35
  17.4 2.4 %collective-permute-start.7 = (bf16[64,512]{1,0:T(8,128)(2,1)S(1)}, bf16[64,512]{1,0:T(8,128)(2,1)S(1)}, u32[]{:S(2)}, u32[]{:S(2)}) collective-permute-start(bf16[64,512]{1,0:T(8,128)(2,1)S(1)} %rows.3), channel_id=1, source_target_pairs={{0,1},{1,0},{2,3},{3,2},{4,5},{5,4},{6,7},{7,6},{8,9},{9,8},{10,11... | collective-permute-start | bytes 196616 | tf_op jit(solution)/shard_map/ppermute | solution.py:35
  18.6 11.9 %collective-permute-start.14 = (bf16[384,512]{1,0:T(8,128)(2,1)S(1)}, bf16[384,512]{1,0:T(8,128)(2,1)S(1)}, u32[]{:S(2)}, u32[]{:S(2)}) collective-permute-start(bf16[384,512]{1,0:T(8,128)(2,1)S(1)} %lineup.9), channel_id=1, source_target_pairs={{0,8},{8,16},{16,24},{24,28},{12,4},{20,12},{28,20},{4,0},{1,9},{9... | collective-permute-start | bytes 1179656 | tf_op jit(solution)/shard_map/ppermute | solution.py:603
  24.1 1.7 %collective-permute-start.10 = (bf16[256,640]{1,0:T(8,128)(2,1)S(1)}, bf16[256,640]{1,0:T(8,128)(2,1)S(1)}, u32[]{:S(2)}, u32[]{:S(2)}) collective-permute-start(bf16[256,640]{1,0:T(8,128)(2,1)S(1)} %get-tuple-element.40.refs_0_), channel_id=1, source_target_pairs={{0,1},{1,0},{2,3},{3,2},{4,5},{5,4},{6,7},{7,6},{8,9},{9,8},{10,11... | collective-permute-start | bytes 983048 | tf_op jit(solution)/shard_map/ppermute | solution.py:35
  26.1 7.5 %collective-permute-start.12 = (bf16[128,640]{1,0:T(8,128)(2,1)S(1)}, bf16[128,640]{1,0:T(8,128)(2,1)S(1)}, u32[]{:S(2)}, u32[]{:S(2)}) collective-permute-start(bf16[128,640]{1,0:T(8,128)(2,1)S(1)} %combine.1.refs_7_), channel_id=1, source_target_pairs={{0,8},{4,12},{8,0},{12,4},{16,24},{20,28},{24,16},{28,20},{1,9},{5... | collective-permute-start | bytes 491528 | tf_op jit(solution)/shard_map/ppermute | solution.py:35
  27.6 3.0 %copy-start.4 = (bf16[512,512]{1,0:T(8,128)(2,1)S(1)}, bf16[512,512]{1,0:T(8,128)(2,1)}, u32[]{:S(2)}) copy-start(bf16[512,512]{1,0:T(8,128)(2,1)} %final_ref.1) | copy-start | bytes 1572868
  27.6 3.0 %copy-start.7 = (bf16[16,128,128]{2,1,0:T(8,128)(2,1)S(1)}, bf16[16,128,128]{2,1,0:T(8,128)(2,1)}, u32[]{:S(2)}) copy-start(bf16[16,128,128]{2,1,0:T(8,128)(2,1)} %refs_2_.3) | copy-start | bytes 1572868
  29.2 4.5 %collective-permute-start.11 = (bf16[144,512]{1,0:T(8,128)(2,1)S(1)}, bf16[144,512]{1,0:T(8,128)(2,1)S(1)}, u32[]{:S(2)}, u32[]{:S(2)}) collective-permute-start(bf16[144,512]{1,0:T(8,128)(2,1)S(1)} %get-tuple-element.47), channel_id=1, source_target_pairs={{0,1},{1,0},{2,3},{3,2},{4,5},{5,4},{6,7},{7,6},{8,9},{9,8},{10,11... | collective-permute-start | bytes 442376 | tf_op jit(solution)/shard_map/ppermute | solution.py:35
  29.2 1.4 %collective-permute-start.13 = (s32[1,12]{1,0:T(1,128)S(1)}, s32[1,12]{1,0:T(1,128)S(1)}, u32[]{:S(2)}, u32[]{:S(2)}) collective-permute-start(s32[1,12]{1,0:T(1,128)S(1)} %bitcast.4), channel_id=1, source_target_pairs={{0,1},{1,0},{2,3},{3,2},{4,5},{5,4},{6,7},{7,6},{8,9},{9,8},{10,11... | collective-permute-start | bytes 152 | tf_op jit(solution)/shard_map/ppermute | solution.py:35
  30.6 2.5 %copy-start.5 = (bf16[512,1024]{1,0:T(8,128)(2,1)S(1)}, bf16[512,1024]{1,0:T(8,128)(2,1)}, u32[]{:S(2)}) copy-start(bf16[512,1024]{1,0:T(8,128)(2,1)} %inner_ref.1) | copy-start | bytes 3145732
  30.6 2.5 %copy-start.6 = (bf16[1024,512]{1,0:T(8,128)(2,1)S(1)}, bf16[1024,512]{1,0:T(8,128)(2,1)}, u32[]{:S(2)}) copy-start(bf16[1024,512]{1,0:T(8,128)(2,1)} %outer_ref.1) | copy-start | bytes 3145732
  31.6 1.4 %copy-start.10 = (f32[512]{0:T(512)S(1)}, f32[512]{0:T(512)}, u32[]{:S(2)}) copy-start(f32[512]{0:T(512)} %param.21) | copy-start | bytes 6148
  31.6 1.4 %collective-permute-start.15 = (bf16[128,512]{1,0:T(8,128)(2,1)S(1)}, bf16[128,512]{1,0:T(8,128)(2,1)S(1)}, u32[]{:S(2)}, u32[]{:S(2)}) collective-permute-start(bf16[128,512]{1,0:T(8,128)(2,1)S(1)} %get-tuple-element.50), channel_id=1, source_target_pairs={{0,1},{1,0},{2,3},{3,2},{4,5},{5,4},{6,7},{7,6},{8,9},{9,8},{10,11... | collective-permute-start | bytes 393224 | tf_op jit(solution)/shard_map/ppermute | solution.py:35

commit v7 on v6

--- a/solution.py
+++ b/solution.py
@@ -436,22 +436,30 @@
     beside, beyond = 2 - 2 * (part % 2), 2 * (part % 2)
     inside = (part != 0) & (part != parts - 1)
     pick = lambda first, second: first + core * (second - first)
-    order = [(1, 0, True), (pick(beside, 1), pick(0, 2), True), (pick(beside, 1), pick(1, 3), True)]
-    order += [(beside, 2, True), (beyond, 0, inside & (core == 0)), (beyond, 1, inside & (core == 0))]
+    order = [(1, 0, True), (beside, 2, True)]
+    order += [(pick(beside, 1), pick(0, 2), True), (pick(beside, 1), pick(1, 3), True)]
+    order += [(beyond, 0, inside & (core == 0)), (beyond, 1, inside & (core == 0))]
     order += [(beyond, 2, inside)]
     rows = across_ref.shape[0]
-    nodes = [both_ref[:rows, :], side_ref[...], across_ref[...], halo_ref[...]]
+    nodes = [
+        jnp.concatenate([both_ref[:rows, :], across_ref[...]], axis=0),
+        side_ref[...],
+        halo_ref[: 2 * rows, :],
+        halo_ref[2 * rows :, :],
+    ]
     for copy in copies:
         copy.wait()
-    wide = []
-    for receiver in range(2):
+    columns = []
+    for side, offset, held in order:
         tiles = []
-        for side, offset, held in order:
+        for receiver in range(2):
             tile_id = slots[receiver, 0, side * group + (me ^ offset)]
             tile = tiles_ref[jnp.maximum(tile_id, 0)]
             tiles.append(jnp.where((tile_id >= 0) & held, tile, jnp.zeros_like(tile)))
-        wide.append(jnp.concatenate(tiles, axis=1))
-    sums = dot(jnp.concatenate(wide, axis=0), jnp.concatenate(nodes, axis=0))
+        columns.append(jnp.concatenate(tiles, axis=0))
+    sums = dot(columns[6], nodes[3])
+    for i in range(3):
+        sums += dot(jnp.concatenate(columns[2 * i : 2 * i + 2], axis=1), nodes[i])
     mine_ref[...] = sums[:rows]
     theirs_ref[...] = sums[rows:].astype(BF16)
 

time: 35 us -> 35 us (level)
  no operation moved by 1% of the time
where the time goes in v7:
time: 35 us; the launch traced here: 34.8 us
  starting transfers between devices  17.4 us (50%)
  Pallas kernels  11.3 us (32%)
  waiting for transfers between devices  3.9 us (11%)
  local copies, waits for them, and re-layouts  2 us (6%)
    ppermute x12, starting transfers between devices, swap(): return lax.ppermute(array, axis, [(i, i ^ mask) for i in range(devices)])  10 us
    ppermute x2, starting transfers between devices, swap_by_core(): return lax.ppermute(array, ('dom', 'head'), pairs)  5.03 us
    ppermute x12, waiting for transfers between devices, swap(): return lax.ppermute(array, axis, [(i, i ^ mask) for i in range(devices)])  3.71 us
    pallas_call x2, Pallas kernels, call(): pl.pallas_call(body, grid=grid, out_shape=tuple(out_parts) + tuple(out_wh...  2.89 us
    pallas_call x1, Pallas kernels, near(): pl.pallas_call(near_kernel, out_shape=(array(rows, BF16),) + (array(count...  2.88 us
    unnamed x26, local copies, waits for them, and re-layouts  2 us
    pallas_call x1, Pallas kernels, own_first(): pl.pallas_call(own_first_kernel, out_shape=(jax.ShapeDtypeStruct((rows, w...  1.36 us
    pallas_call x1, Pallas kernels, finish(): pl.pallas_call(finish_kernel, out_shape=jax.ShapeDtypeStruct((rows, width...  1.21 us
  transfers between devices with their start and end apart: 16, of which 8 were waited for; matrix products, arithmetic and copies ran while one was open for 0% of the time, Pallas kernels for 29%

profile of v7, /device:TPU:0, one launch (start us, length us, event | category | flops | bytes accessed | tf_op | source)
XLA Modules:
  0.0 34.8 jit_solution(15360890184276038616)
XLA Ops:
  0.0 0.5 %collective-permute-start.1 = (bf16[128,512]{1,0:T(8,128)(2,1)}, bf16[128,512]{1,0:T(8,128)(2,1)S(1)}, u32[]{:S(2)}, u32[]{:S(2)}) collective-permute-start(bf16[128,512]{1,0:T(8,128)(2,1)} %refs_0_.1), channel_id=1, source_target_pairs={{0,1},{1,0},{2,3},{3,2},{4,5},{5,4},{6,7},{7,6},{8,9},{9,8},{10,11... | collective-permute-start | bytes 393224 | tf_op jit(solution)/shard_map/ppermute | solution.py:35
  0.5 0.9 %copy-done.8 = bf16[128,512]{1,0:T(8,128)(2,1)S(1)} copy-done((bf16[128,512]{1,0:T(8,128)(2,1)S(1)}, bf16[128,512]{1,0:T(8,128)(2,1)}, u32[]{:S(2)}) %copy-start.8) | copy-done | bytes 131096
  1.4 0.0 copy-start
  1.4 0.3 collective-permute-done.1.refs_1_
  1.7 2.9 %collective-permute-start.2 = (bf16[256,512]{1,0:T(8,128)(2,1)S(1)}, bf16[256,512]{1,0:T(8,128)(2,1)S(1)}, u32[]{:S(2)}, u32[]{:S(2)}) collective-permute-start(bf16[256,512]{1,0:T(8,128)(2,1)S(1)} %lineup.6.both_ref.refs_3_), channel_id=1, source_target_pairs={{0,4},{1,3},{2,6},{3,1},{4,0},{5,7},{6,2},{7,5},{8,12},{9,11},{10,... | collective-permute-start | bytes 786440 | tf_op jit(solution)/shard_map/ppermute | solution.py:55
  4.6 2.6 %collective-permute-start = (bf16[128,512]{1,0:T(8,128)(2,1)S(1)}, bf16[128,512]{1,0:T(8,128)(2,1)S(1)}, u32[]{:S(2)}, u32[]{:S(2)}) collective-permute-start(bf16[128,512]{1,0:T(8,128)(2,1)S(1)} %copy-done.9), channel_id=1, source_target_pairs={{0,16},{4,20},{8,24},{12,28},{16,0},{20,4},{24,8},{28,12},{1,17},{... | collective-permute-start | bytes 393224 | tf_op jit(solution)/shard_map/ppermute | solution.py:35
  7.2 1.6 %collective-permute-start.5 = (bf16[128,512]{1,0:T(8,128)(2,1)S(1)}, bf16[128,512]{1,0:T(8,128)(2,1)S(1)}, u32[]{:S(2)}, u32[]{:S(2)}) collective-permute-start(bf16[128,512]{1,0:T(8,128)(2,1)S(1)} %copy-done.9), channel_id=1, source_target_pairs={{0,8},{4,12},{8,0},{12,4},{16,24},{20,28},{24,16},{28,20},{1,9},{5... | collective-permute-start | bytes 393224 | tf_op jit(solution)/shard_map/ppermute | solution.py:35
  8.8 0.2 collective-permute-done.2.side_ref.refs_0_.refs_4_
  9.0 0.0 copy-start.11
  9.0 0.0 copy-start.12
  9.0 2.1 %collective-permute-start.8 = (bf16[128,512]{1,0:T(8,128)(2,1)S(1)}, bf16[128,512]{1,0:T(8,128)(2,1)S(1)}, u32[]{:S(2)}, u32[]{:S(2)}) collective-permute-start(bf16[128,512]{1,0:T(8,128)(2,1)S(1)} %lineup.8), channel_id=1, source_target_pairs={{0,2},{1,5},{2,0},{3,7},{4,6},{5,1},{6,4},{7,3},{8,10},{9,13},{10,... | collective-permute-start | bytes 393224 | tf_op jit(solution)/shard_map/ppermute | solution.py:55
  11.1 0.0 copy-start.2
  11.1 1.0 %copy-done.2 = bf16[512,512]{1,0:T(8,128)(2,1)S(1)} copy-done((bf16[512,512]{1,0:T(8,128)(2,1)S(1)}, bf16[512,512]{1,0:T(8,128)(2,1)}, u32[]{:S(2)}) %copy-start.2) | copy-done | bytes 524312
  12.1 1.1 %early.1 = (bf16[256,512]{1,0:T(8,128)(2,1)S(1)}, f32[1,512]{1,0:T(1,128)S(1)}, bf16[384,512]{1,0:T(8,128)(2,1)S(1)}, bf16[384,512]{1,0:T(8,128)(2,1)S(1)}, s32[1,12]{1,0:T(1,128)S(1)}) custom-call(f32[8]{0:T(128)S(1)} %copy-done.11, s32[1,12]{1,0:T(1,128)S(1)} %bitcast.3, bf16[256,512]{1,0:T(8,128)(2,1)S(1)} %lineup.6.both_ref.refs_3_, ...), custom_call_target="tpu_custom_call" | custom-call | flops 33554432 | bytes 262144 | tf_op jit(solution)/shard_map/early/pallas_call | solution.py:179
  13.3 0.4 %collective-permute-done.refs_0_ = bf16[128,512]{1,0:T(8,128)(2,1)S(1)} collective-permute-done((bf16[128,512]{1,0:T(8,128)(2,1)S(1)}, bf16[128,512]{1,0:T(8,128)(2,1)S(1)}, u32[]{:S(2)}, u32[]{:S(2)}) %collective-permute-start) | collective-permute-done | bytes 131104 | tf_op jit(solution)/shard_map/ppermute | solution.py:35
  13.7 1.1 %collective-permute-start.9 = (bf16[128,512]{1,0:T(8,128)(2,1)S(1)}, bf16[128,512]{1,0:T(8,128)(2,1)S(1)}, u32[]{:S(2)}, u32[]{:S(2)}) collective-permute-start(bf16[128,512]{1,0:T(8,128)(2,1)S(1)} %lineup.7.refs_1_), channel_id=1, source_target_pairs={{0,4},{4,0},{8,12},{12,8},{16,20},{20,16},{24,28},{28,24},{1,5},{5... | collective-permute-start | bytes 393224 | tf_op jit(solution)/shard_map/ppermute | solution.py:35
  14.8 1.2 %collective-permute-start.3 = (bf16[128,512]{1,0:T(8,128)(2,1)S(1)}, bf16[128,512]{1,0:T(8,128)(2,1)S(1)}, u32[]{:S(2)}, u32[]{:S(2)}) collective-permute-start(bf16[128,512]{1,0:T(8,128)(2,1)S(1)} %lineup.7.refs_1_), channel_id=1, source_target_pairs={{0,2},{1,3},{2,0},{3,1},{4,6},{5,7},{6,4},{7,5},{8,10},{9,11},{10,... | collective-permute-start | bytes 393224 | tf_op jit(solution)/shard_map/ppermute | solution.py:35
  16.1 1.2 %collective-permute-start.4 = (bf16[128,512]{1,0:T(8,128)(2,1)S(1)}, bf16[128,512]{1,0:T(8,128)(2,1)S(1)}, u32[]{:S(2)}, u32[]{:S(2)}) collective-permute-start(bf16[128,512]{1,0:T(8,128)(2,1)S(1)} %lineup.7.refs_1_), channel_id=1, source_target_pairs={{0,6},{1,7},{2,4},{3,5},{4,2},{5,3},{6,0},{7,1},{8,14},{9,15},{10,... | collective-permute-start | bytes 393224 | tf_op jit(solution)/shard_map/ppermute | solution.py:45
  17.3 0.0 copy-start.3
  17.3 0.1 collective-permute-start.6
  17.4 0.5 %collective-permute-start.7 = (bf16[64,512]{1,0:T(8,128)(2,1)S(1)}, bf16[64,512]{1,0:T(8,128)(2,1)S(1)}, u32[]{:S(2)}, u32[]{:S(2)}) collective-permute-start(bf16[64,512]{1,0:T(8,128)(2,1)S(1)} %rows.3), channel_id=1, source_target_pairs={{0,1},{1,0},{2,3},{3,2},{4,5},{5,4},{6,7},{7,6},{8,9},{9,8},{10,11... | collective-permute-start | bytes 196616 | tf_op jit(solution)/shard_map/ppermute | solution.py:35
  18.0 0.6 %collective-permute-done.6.first_ref = bf16[64,512]{1,0:T(8,128)(2,1)S(1)} collective-permute-done((bf16[64,512]{1,0:T(8,128)(2,1)S(1)}, bf16[64,512]{1,0:T(8,128)(2,1)S(1)}, u32[]{:S(2)}, u32[]{:S(2)}) %collective-permute-start.6) | collective-permute-done | bytes 65568 | tf_op jit(solution)/shard_map/ppermute | solution.py:35
  18.6 1.2 %collective-permute-start.14 = (bf16[384,512]{1,0:T(8,128)(2,1)S(1)}, bf16[384,512]{1,0:T(8,128)(2,1)S(1)}, u32[]{:S(2)}, u32[]{:S(2)}) collective-permute-start(bf16[384,512]{1,0:T(8,128)(2,1)S(1)} %lineup.9), channel_id=1, source_target_pairs={{0,8},{8,16},{16,24},{24,28},{12,4},{20,12},{28,20},{4,0},{1,9},{9... | collective-permute-start | bytes 1179656 | tf_op jit(solution)/shard_map/ppermute | solution.py:611
  19.8 0.0 collective-permute-done.7.second_ref
  19.8 0.0 collective-permute-done.9.refs_2_
  19.8 2.9 %near.1 = (bf16[256,512]{1,0:T(8,128)(2,1)S(1)}, bf16[768,512]{1,0:T(8,128)(2,1)S(1)}, bf16[768,512]{1,0:T(8,128)(2,1)S(1)}, f32[256,512]{1,0:T(8,128)S(1)}, f32[256,512]{1,0:T(8,128)S(1)}) custom-call(f32[1,512]{1,0:T(1,128)S(1)} %get-tuple-element.30.scale_ref, bf16[384,512]{1,0:T(8,128)(2,1)S(1)} %get-tuple-element.31.held_keys, ...), custom_call_target="tpu_custom_call" | custom-call | flops 37748736 | bytes 262144 | tf_op jit(solution)/shard_map/near/pallas_call | solution.py:210
  22.7 0.2 collective-permute-done.3.refs_0_
  22.8 0.0 collective-permute-done.4.refs_1_
  22.8 1.3 %far.1 = (bf16[256,512]{1,0:T(8,128)(2,1)S(1)}, bf16[256,512]{1,0:T(8,128)(2,1)S(1)}, bf16[256,640]{1,0:T(8,128)(2,1)S(1)}, f32[128,512]{1,0:T(8,128)S(1)}, f32[128,512]{1,0:T(8,128)S(1)}) custom-call(bf16[128,512]{1,0:T(8,128)(2,1)S(1)} %collective-permute-done.3.refs_0_, bf16[128,512]{1,0:T(8,128)(2,1)S(1)} %collective-permute-done.4.refs_1_, ...), custom_call_target="tpu_custom_call" | custom-call | flops 12582912 | bytes 262144 | tf_op jit(solution)/shard_map/far/pallas_call | solution.py:272
  24.1 0.1 collective-permute-start.10
  24.2 1.4 %own_first.1 = (f32[256,512]{1,0:T(8,128)S(1)}, f32[256,512]{1,0:T(8,128)S(1)}) custom-call(bf16[256,512]{1,0:T(8,128)(2,1)S(1)} %get-tuple-element.29.refs_1_.queries_ref.refs_2_, bf16[768,512]{1,0:T(8,128)(2,1)S(1)} %get-tuple-element.38.keys_ref.refs_3_, bf16[768,512]{1,0:T(8,128)(2,1)S(1)} %get-tuple-element.39.values_ref.refs_4_, ...), custom_call_target="tpu_custom_call" | custom-call | flops 16777216 | bytes 131072 | tf_op jit(solution)/shard_map/own_first/pallas_call | solution.py:345
  25.6 0.2 collective-permute-done.10.packed_ref
  25.8 0.2 combine.1.refs_7_
  26.1 1.5 %collective-permute-start.12 = (bf16[128,640]{1,0:T(8,128)(2,1)S(1)}, bf16[128,640]{1,0:T(8,128)(2,1)S(1)}, u32[]{:S(2)}, u32[]{:S(2)}) collective-permute-start(bf16[128,640]{1,0:T(8,128)(2,1)S(1)} %combine.1.refs_7_), channel_id=1, source_target_pairs={{0,8},{4,12},{8,0},{12,4},{16,24},{20,28},{24,16},{28,20},{1,9},{5... | collective-permute-start | bytes 491528 | tf_op jit(solution)/shard_map/ppermute | solution.py:35
  27.6 1.6 %own.1 = (bf16[144,512]{1,0:T(8,128)(2,1)S(1)}, f32[128,512]{1,0:T(8,128)S(1)}, f32[128,512]{1,0:T(8,128)S(1)}) custom-call(bf16[256,512]{1,0:T(8,128)(2,1)S(1)} %get-tuple-element.36.refs_0_, bf16[256,512]{1,0:T(8,128)(2,1)S(1)} %get-tuple-element.37.refs_1_, bf16[256,512]{1,0:T(8,128)(2,1)S(1)} %get-tuple-element.29.refs_1_.queries_ref.refs_2_, ...), custom_call_target="tpu_custom_call" | custom-call | flops 16777216 | bytes 262144 | tf_op jit(solution)/shard_map/own/pallas_call | solution.py:272
  29.2 0.0 collective-permute-start.11
  29.2 0.5 %collective-permute-start.13 = (s32[1,12]{1,0:T(1,128)S(1)}, s32[1,12]{1,0:T(1,128)S(1)}, u32[]{:S(2)}, u32[]{:S(2)}) collective-permute-start(s32[1,12]{1,0:T(1,128)S(1)} %bitcast.4), channel_id=1, source_target_pairs={{0,1},{1,0},{2,3},{3,2},{4,5},{5,4},{6,7},{7,6},{8,9},{9,8},{10,11... | collective-permute-start | bytes 152 | tf_op jit(solution)/shard_map/ppermute | solution.py:35
  29.7 0.9 %collective-permute-done.13.refs_1_ = s32[1,12]{1,0:T(1,128)S(1)} collective-permute-done((s32[1,12]{1,0:T(1,128)S(1)}, s32[1,12]{1,0:T(1,128)S(1)}, u32[]{:S(2)}, u32[]{:S(2)}) %collective-permute-start.13) | collective-permute-done | bytes 80 | tf_op jit(solution)/shard_map/ppermute | solution.py:35
  30.6 0.0 collective-permute-done.14.refs_6_
  30.6 0.0 copy-start.5
  30.6 0.0 copy-start.6
  30.6 1.0 %around.1 = (f32[128,512]{1,0:T(8,128)S(1)}, bf16[128,512]{1,0:T(8,128)(2,1)S(1)}) custom-call(s32[1,12]{1,0:T(1,128)S(1)} %get-tuple-element.48.refs_0_, s32[1,12]{1,0:T(1,128)S(1)} %collective-permute-done.13.refs_1_, bf16[16,128,128]{2,1,0:T(8,128)(2,1)S(1)} %copy-done.7, bf16[256,512]{1,0:T(8,128)(2,1)S(1)} %lineup.6.both_ref.refs_3_, ...), custom_call_target="tpu_custom_call" | custom-call | flops 14680064 | bytes 65536 | tf_op jit(solution)/shard_map/around/pallas_call | solution.py:473
  31.6 0.0 copy-start.10
  31.6 0.3 collective-permute-start.15
  31.9 1.1 %collective-permute-done.15.got_ref = bf16[128,512]{1,0:T(8,128)(2,1)S(1)} collective-permute-done((bf16[128,512]{1,0:T(8,128)(2,1)S(1)}, bf16[128,512]{1,0:T(8,128)(2,1)S(1)}, u32[]{:S(2)}, u32[]{:S(2)}) %collective-permute-start.15) | collective-permute-done | bytes 131104 | tf_op jit(solution)/shard_map/ppermute | solution.py:35
  33.0 0.6 %message.1 = (f32[128,512]{1,0:T(8,128)S(1)}, f32[1,512]{1,0:T(1,128)S(1)}) custom-call(f32[128,512]{1,0:T(8,128)S(1)} %get-tuple-element.49.mine_ref, bf16[128,512]{1,0:T(8,128)(2,1)S(1)} %collective-permute-done.15.got_ref, bf16[512,1024]{1,0:T(8,128)(2,1)S(1)} %copy-done.5, bf16[1024,512]{1,0:T(8,128)(2,1)S(1)} %copy-done.6, f32[1,512]{1,0:T(1,128)S(1)} %bitcast.2), custom_call_target="tpu_custom_call" | custom-call | flops 16777216 | bytes 262144 | tf_op jit(solution)/shard_map/message/pallas_call | solution.py:501
  33.6 0.0 collective-permute-done.12.packed_ref
  33.6 1.2 %finish.1 = bf16[128,512]{1,0:T(8,128)(2,1)} custom-call(f32[128,512]{1,0:T(8,128)S(1)} %get-tuple-element.45.refs_8_.numer_ref, f32[128,512]{1,0:T(8,128)S(1)} %get-tuple-element.46.denom_ref, bf16[144,512]{1,0:T(8,128)(2,1)S(1)} %collective-permute-done.11.crossed_ref, bf16[128,640]{1,0:T(8,128)(2,1)S(1)} %collective-permute-done.12.packed_ref, ...), custom_call_target="tpu_custom_call" | custom-call | flops 4194304 | bytes 131072 | tf_op jit(solution)/shard_map/finish/pallas_call | solution.py:532
  (26 shorter events, 0.1 us)
Async XLA Ops:
  0.0 1.6 %collective-permute-start.1 = (bf16[128,512]{1,0:T(8,128)(2,1)}, bf16[128,512]{1,0:T(8,128)(2,1)S(1)}, u32[]{:S(2)}, u32[]{:S(2)}) collective-permute-start(bf16[128,512]{1,0:T(8,128)(2,1)} %refs_0_.1), channel_id=1, source_target_pairs={{0,1},{1,0},{2,3},{3,2},{4,5},{5,4},{6,7},{7,6},{8,9},{9,8},{10,11... | collective-permute-start | bytes 393224 | tf_op jit(solution)/shard_map/ppermute | solution.py:35
  0.5 0.9 %copy-start.8 = (bf16[128,512]{1,0:T(8,128)(2,1)S(1)}, bf16[128,512]{1,0:T(8,128)(2,1)}, u32[]{:S(2)}) copy-start(bf16[128,512]{1,0:T(8,128)(2,1)} %refs_0_.1) | copy-start | bytes 393220
  1.4 3.2 %copy-start.9 = (bf16[128,512]{1,0:T(8,128)(2,1)S(1)}, bf16[128,512]{1,0:T(8,128)(2,1)}, u32[]{:S(2)}) copy-start(bf16[128,512]{1,0:T(8,128)(2,1)} %refs_0_.1) | copy-start | bytes 393220
  1.4 9.7 %copy-start.1 = (bf16[512,512]{1,0:T(8,128)(2,1)S(1)}, bf16[512,512]{1,0:T(8,128)(2,1)}, u32[]{:S(2)}) copy-start(bf16[512,512]{1,0:T(8,128)(2,1)} %refs_3_.3) | copy-start | bytes 1572868
  1.4 9.7 %copy-start = (bf16[512,512]{1,0:T(8,128)(2,1)S(1)}, bf16[512,512]{1,0:T(8,128)(2,1)}, u32[]{:S(2)}) copy-start(bf16[512,512]{1,0:T(8,128)(2,1)} %refs_2_.2) | copy-start | bytes 1572868
  1.7 7.3 %collective-permute-start.2 = (bf16[256,512]{1,0:T(8,128)(2,1)S(1)}, bf16[256,512]{1,0:T(8,128)(2,1)S(1)}, u32[]{:S(2)}, u32[]{:S(2)}) collective-permute-start(bf16[256,512]{1,0:T(8,128)(2,1)S(1)} %lineup.6.both_ref.refs_3_), channel_id=1, source_target_pairs={{0,4},{1,3},{2,6},{3,1},{4,0},{5,7},{6,2},{7,5},{8,12},{9,11},{10,... | collective-permute-start | bytes 786440 | tf_op jit(solution)/shard_map/ppermute | solution.py:55
  4.6 9.1 %collective-permute-start = (bf16[128,512]{1,0:T(8,128)(2,1)S(1)}, bf16[128,512]{1,0:T(8,128)(2,1)S(1)}, u32[]{:S(2)}, u32[]{:S(2)}) collective-permute-start(bf16[128,512]{1,0:T(8,128)(2,1)S(1)} %copy-done.9), channel_id=1, source_target_pairs={{0,16},{4,20},{8,24},{12,28},{16,0},{20,4},{24,8},{28,12},{1,17},{... | collective-permute-start | bytes 393224 | tf_op jit(solution)/shard_map/ppermute | solution.py:35
  7.2 10.1 %collective-permute-start.5 = (bf16[128,512]{1,0:T(8,128)(2,1)S(1)}, bf16[128,512]{1,0:T(8,128)(2,1)S(1)}, u32[]{:S(2)}, u32[]{:S(2)}) collective-permute-start(bf16[128,512]{1,0:T(8,128)(2,1)S(1)} %copy-done.9), channel_id=1, source_target_pairs={{0,8},{4,12},{8,0},{12,4},{16,24},{20,28},{24,16},{28,20},{1,9},{5... | collective-permute-start | bytes 393224 | tf_op jit(solution)/shard_map/ppermute | solution.py:35
  9.0 2.1 %copy-start.11 = (f32[8]{0:T(128)S(1)}, f32[8]{0:T(128)}, u32[]{:S(2)}) copy-start(f32[8]{0:T(128)} %softness_ref.1) | copy-start | bytes 100
  9.0 2.1 %copy-start.12 = (s32[1,1,12]{2,1,0:T(1,128)S(1)}, s32[1,1,12]{2,1,0:T(1,128)}, u32[]{:S(2)}) copy-start(s32[1,1,12]{2,1,0:T(1,128)} %param.12) | copy-start | bytes 148
  9.0 8.4 %collective-permute-start.8 = (bf16[128,512]{1,0:T(8,128)(2,1)S(1)}, bf16[128,512]{1,0:T(8,128)(2,1)S(1)}, u32[]{:S(2)}, u32[]{:S(2)}) collective-permute-start(bf16[128,512]{1,0:T(8,128)(2,1)S(1)} %lineup.8), channel_id=1, source_target_pairs={{0,2},{1,5},{2,0},{3,7},{4,6},{5,1},{6,4},{7,3},{8,10},{9,13},{10,... | collective-permute-start | bytes 393224 | tf_op jit(solution)/shard_map/ppermute | solution.py:55
  11.1 1.0 %copy-start.2 = (bf16[512,512]{1,0:T(8,128)(2,1)S(1)}, bf16[512,512]{1,0:T(8,128)(2,1)}, u32[]{:S(2)}) copy-start(bf16[512,512]{1,0:T(8,128)(2,1)} %refs_3_.2) | copy-start | bytes 1572868
  13.7 6.1 %collective-permute-start.9 = (bf16[128,512]{1,0:T(8,128)(2,1)S(1)}, bf16[128,512]{1,0:T(8,128)(2,1)S(1)}, u32[]{:S(2)}, u32[]{:S(2)}) collective-permute-start(bf16[128,512]{1,0:T(8,128)(2,1)S(1)} %lineup.7.refs_1_), channel_id=1, source_target_pairs={{0,4},{4,0},{8,12},{12,8},{16,20},{20,16},{24,28},{28,24},{1,5},{5... | collective-permute-start | bytes 393224 | tf_op jit(solution)/shard_map/ppermute | solution.py:35
  14.8 8.0 %collective-permute-start.3 = (bf16[128,512]{1,0:T(8,128)(2,1)S(1)}, bf16[128,512]{1,0:T(8,128)(2,1)S(1)}, u32[]{:S(2)}, u32[]{:S(2)}) collective-permute-start(bf16[128,512]{1,0:T(8,128)(2,1)S(1)} %lineup.7.refs_1_), channel_id=1, source_target_pairs={{0,2},{1,3},{2,0},{3,1},{4,6},{5,7},{6,4},{7,5},{8,10},{9,11},{10,... | collective-permute-start | bytes 393224 | tf_op jit(solution)/shard_map/ppermute | solution.py:35
  16.1 6.8 %collective-permute-start.4 = (bf16[128,512]{1,0:T(8,128)(2,1)S(1)}, bf16[128,512]{1,0:T(8,128)(2,1)S(1)}, u32[]{:S(2)}, u32[]{:S(2)}) collective-permute-start(bf16[128,512]{1,0:T(8,128)(2,1)S(1)} %lineup.7.refs_1_), channel_id=1, source_target_pairs={{0,6},{1,7},{2,4},{3,5},{4,2},{5,3},{6,0},{7,1},{8,14},{9,15},{10,... | collective-permute-start | bytes 393224 | tf_op jit(solution)/shard_map/ppermute | solution.py:45
  17.3 2.5 %copy-start.3 = (bf16[512,512]{1,0:T(8,128)(2,1)S(1)}, bf16[512,512]{1,0:T(8,128)(2,1)}, u32[]{:S(2)}) copy-start(bf16[512,512]{1,0:T(8,128)(2,1)} %refs_3_.2) | copy-start | bytes 1572868
  17.3 1.3 %collective-permute-start.6 = (bf16[64,512]{1,0:T(8,128)(2,1)S(1)}, bf16[64,512]{1,0:T(8,128)(2,1)S(1)}, u32[]{:S(2)}, u32[]{:S(2)}) collective-permute-start(bf16[64,512]{1,0:T(8,128)(2,1)S(1)} %rows.2), channel_id=1, source_target_pairs={{0,1},{1,0},{2,3},{3,2},{4,5},{5,4},{6,7},{7,6},{8,9},{9,8},{10,11... | collective-permute-start | bytes 196616 | tf_op jit(solution)/shard_map/ppermute | solution.py:35
  17.4 2.4 %collective-permute-start.7 = (bf16[64,512]{1,0:T(8,128)(2,1)S(1)}, bf16[64,512]{1,0:T(8,128)(2,1)S(1)}, u32[]{:S(2)}, u32[]{:S(2)}) collective-permute-start(bf16[64,512]{1,0:T(8,128)(2,1)S(1)} %rows.3), channel_id=1, source_target_pairs={{0,1},{1,0},{2,3},{3,2},{4,5},{5,4},{6,7},{7,6},{8,9},{9,8},{10,11... | collective-permute-start | bytes 196616 | tf_op jit(solution)/shard_map/ppermute | solution.py:35
  18.6 11.9 %collective-permute-start.14 = (bf16[384,512]{1,0:T(8,128)(2,1)S(1)}, bf16[384,512]{1,0:T(8,128)(2,1)S(1)}, u32[]{:S(2)}, u32[]{:S(2)}) collective-permute-start(bf16[384,512]{1,0:T(8,128)(2,1)S(1)} %lineup.9), channel_id=1, source_target_pairs={{0,8},{8,16},{16,24},{24,28},{12,4},{20,12},{28,20},{4,0},{1,9},{9... | collective-permute-start | bytes 1179656 | tf_op jit(solution)/shard_map/ppermute | solution.py:611
  24.1 1.7 %collective-permute-start.10 = (bf16[256,640]{1,0:T(8,128)(2,1)S(1)}, bf16[256,640]{1,0:T(8,128)(2,1)S(1)}, u32[]{:S(2)}, u32[]{:S(2)}) collective-permute-start(bf16[256,640]{1,0:T(8,128)(2,1)S(1)} %get-tuple-element.40.refs_0_), channel_id=1, source_target_pairs={{0,1},{1,0},{2,3},{3,2},{4,5},{5,4},{6,7},{7,6},{8,9},{9,8},{10,11... | collective-permute-start | bytes 983048 | tf_op jit(solution)/shard_map/ppermute | solution.py:35
  26.1 7.5 %collective-permute-start.12 = (bf16[128,640]{1,0:T(8,128)(2,1)S(1)}, bf16[128,640]{1,0:T(8,128)(2,1)S(1)}, u32[]{:S(2)}, u32[]{:S(2)}) collective-permute-start(bf16[128,640]{1,0:T(8,128)(2,1)S(1)} %combine.1.refs_7_), channel_id=1, source_target_pairs={{0,8},{4,12},{8,0},{12,4},{16,24},{20,28},{24,16},{28,20},{1,9},{5... | collective-permute-start | bytes 491528 | tf_op jit(solution)/shard_map/ppermute | solution.py:35
  27.6 3.0 %copy-start.4 = (bf16[512,512]{1,0:T(8,128)(2,1)S(1)}, bf16[512,512]{1,0:T(8,128)(2,1)}, u32[]{:S(2)}) copy-start(bf16[512,512]{1,0:T(8,128)(2,1)} %final_ref.1) | copy-start | bytes 1572868
  27.6 3.0 %copy-start.7 = (bf16[16,128,128]{2,1,0:T(8,128)(2,1)S(1)}, bf16[16,128,128]{2,1,0:T(8,128)(2,1)}, u32[]{:S(2)}) copy-start(bf16[16,128,128]{2,1,0:T(8,128)(2,1)} %refs_2_.3) | copy-start | bytes 1572868
  29.2 4.5 %collective-permute-start.11 = (bf16[144,512]{1,0:T(8,128)(2,1)S(1)}, bf16[144,512]{1,0:T(8,128)(2,1)S(1)}, u32[]{:S(2)}, u32[]{:S(2)}) collective-permute-start(bf16[144,512]{1,0:T(8,128)(2,1)S(1)} %get-tuple-element.47), channel_id=1, source_target_pairs={{0,1},{1,0},{2,3},{3,2},{4,5},{5,4},{6,7},{7,6},{8,9},{9,8},{10,11... | collective-permute-start | bytes 442376 | tf_op jit(solution)/shard_map/ppermute | solution.py:35
  29.2 1.4 %collective-permute-start.13 = (s32[1,12]{1,0:T(1,128)S(1)}, s32[1,12]{1,0:T(1,128)S(1)}, u32[]{:S(2)}, u32[]{:S(2)}) collective-permute-start(s32[1,12]{1,0:T(1,128)S(1)} %bitcast.4), channel_id=1, source_target_pairs={{0,1},{1,0},{2,3},{3,2},{4,5},{5,4},{6,7},{7,6},{8,9},{9,8},{10,11... | collective-permute-start | bytes 152 | tf_op jit(solution)/shard_map/ppermute | solution.py:35
  30.6 2.5 %copy-start.5 = (bf16[512,1024]{1,0:T(8,128)(2,1)S(1)}, bf16[512,1024]{1,0:T(8,128)(2,1)}, u32[]{:S(2)}) copy-start(bf16[512,1024]{1,0:T(8,128)(2,1)} %inner_ref.1) | copy-start | bytes 3145732
  30.6 2.5 %copy-start.6 = (bf16[1024,512]{1,0:T(8,128)(2,1)S(1)}, bf16[1024,512]{1,0:T(8,128)(2,1)}, u32[]{:S(2)}) copy-start(bf16[1024,512]{1,0:T(8,128)(2,1)} %outer_ref.1) | copy-start | bytes 3145732
  31.6 1.4 %copy-start.10 = (f32[512]{0:T(512)S(1)}, f32[512]{0:T(512)}, u32[]{:S(2)}) copy-start(f32[512]{0:T(512)} %param.21) | copy-start | bytes 6148
  31.6 1.4 %collective-permute-start.15 = (bf16[128,512]{1,0:T(8,128)(2,1)S(1)}, bf16[128,512]{1,0:T(8,128)(2,1)S(1)}, u32[]{:S(2)}, u32[]{:S(2)}) collective-permute-start(bf16[128,512]{1,0:T(8,128)(2,1)S(1)} %get-tuple-element.50), channel_id=1, source_target_pairs={{0,1},{1,0},{2,3},{3,2},{4,5},{5,4},{6,7},{7,6},{8,9},{9,8},{10,11... | collective-permute-start | bytes 393224 | tf_op jit(solution)/shard_map/ppermute | solution.py:35

commit v8 on v6

--- a/solution.py
+++ b/solution.py
@@ -505,7 +505,8 @@
 
 
 def finish_kernel(
-    numer_ref, denom_ref, crossed_ref, packed_ref, final_ref, gain_ref, local_ref, nodes_ref, out_ref
+    numer_ref, denom_ref, crossed_ref, packed_ref, final_ref, gain_ref, local_ref, nodes_ref, out_ref,
+    held, sems,
 ):
     width = numer_ref.shape[1]
     rows = numer_ref.shape[0]
@@ -514,9 +515,20 @@
     denom += unpack_denom(packed_ref[:, width:], width)
     mixed = (numer / denom).astype(BF16)
     attended = dot(mixed, final_ref[...])
-    mean = jnp.mean(attended * attended, axis=-1, keepdims=True)
-    normed = attended * lax.rsqrt(mean + norm_eps) * gain_ref[...]
-    out_ref[...] = (nodes_ref[...].astype(F32) + local_ref[...] + normed).astype(BF16)
+    half = rows // 2
+    copies = []
+    for at in range(2):
+        part = slice(at * half, (at + 1) * half)
+        here = attended[part]
+        mean = jnp.mean(here * here, axis=-1, keepdims=True)
+        normed = here * lax.rsqrt(mean + norm_eps) * gain_ref[...]
+        total = nodes_ref[part, :].astype(F32) + local_ref[part, :] + normed
+        held[at] = total.astype(BF16)
+        copy = pltpu.make_async_copy(held.at[at], out_ref.at[pl.ds(at * half, half)], sems.at[at])
+        copy.start()
+        copies.append(copy)
+    for copy in copies:
+        copy.wait()
 
 
 def finish(numer, denom, crossed, packed, final, gain, local, nodes):
@@ -525,7 +537,11 @@
         finish_kernel,
         out_shape=jax.ShapeDtypeStruct((rows, width), BF16),
         in_specs=[VMEM] * 8,
-        out_specs=VMEM,
+        out_specs=ANY,
+        scratch_shapes=[
+            pltpu.VMEM((2, rows // 2, width), BF16),
+            pltpu.SemaphoreType.DMA((2,)),
+        ],
         compiler_params=params(16),
         cost_estimate=cost(2 * rows * width * width, rows, 2 << 20),
         name="finish",

time: 35 us -> 35 us (level)
  no operation moved by 1% of the time
where the time goes in v8:
time: 35 us; the launch traced here: 34.8 us
  starting transfers between devices  17.4 us (50%)
  Pallas kernels  11.3 us (32%)
  waiting for transfers between devices  3.9 us (11%)
  local copies, waits for them, and re-layouts  2 us (6%)
    ppermute x12, starting transfers between devices, swap(): return lax.ppermute(array, axis, [(i, i ^ mask) for i in range(devices)])  10 us
    ppermute x2, starting transfers between devices, swap_by_core(): return lax.ppermute(array, ('dom', 'head'), pairs)  5.03 us
    ppermute x12, waiting for transfers between devices, swap(): return lax.ppermute(array, axis, [(i, i ^ mask) for i in range(devices)])  3.71 us
    pallas_call x2, Pallas kernels, call(): pl.pallas_call(body, grid=grid, out_shape=tuple(out_parts) + tuple(out_wh...  2.89 us
    pallas_call x1, Pallas kernels, near(): pl.pallas_call(near_kernel, out_shape=(array(rows, BF16),) + (array(count...  2.88 us
    unnamed x26, local copies, waits for them, and re-layouts  2 us
    pallas_call x1, Pallas kernels, own_first(): pl.pallas_call(own_first_kernel, out_shape=(jax.ShapeDtypeStruct((rows, w...  1.36 us
    pallas_call x1, Pallas kernels, finish(): pl.pallas_call(finish_kernel, out_shape=jax.ShapeDtypeStruct((rows, width...  1.2 us
  transfers between devices with their start and end apart: 16, of which 8 were waited for; matrix products, arithmetic and copies ran while one was open for 0% of the time, Pallas kernels for 29%

profile of v8, /device:TPU:0, one launch (start us, length us, event | category | flops | bytes accessed | tf_op | source)
XLA Modules:
  0.0 34.8 jit_solution(10686476584489304951)
XLA Ops:
  0.0 0.5 %collective-permute-start.1 = (bf16[128,512]{1,0:T(8,128)(2,1)}, bf16[128,512]{1,0:T(8,128)(2,1)S(1)}, u32[]{:S(2)}, u32[]{:S(2)}) collective-permute-start(bf16[128,512]{1,0:T(8,128)(2,1)} %refs_0_.1), channel_id=1, source_target_pairs={{0,1},{1,0},{2,3},{3,2},{4,5},{5,4},{6,7},{7,6},{8,9},{9,8},{10,11... | collective-permute-start | bytes 393224 | tf_op jit(solution)/shard_map/ppermute | solution.py:35
  0.5 0.9 %copy-done.8 = bf16[128,512]{1,0:T(8,128)(2,1)S(1)} copy-done((bf16[128,512]{1,0:T(8,128)(2,1)S(1)}, bf16[128,512]{1,0:T(8,128)(2,1)}, u32[]{:S(2)}) %copy-start.8) | copy-done | bytes 131096
  1.4 0.0 copy-start
  1.4 0.3 collective-permute-done.1.refs_1_
  1.7 2.9 %collective-permute-start.2 = (bf16[256,512]{1,0:T(8,128)(2,1)S(1)}, bf16[256,512]{1,0:T(8,128)(2,1)S(1)}, u32[]{:S(2)}, u32[]{:S(2)}) collective-permute-start(bf16[256,512]{1,0:T(8,128)(2,1)S(1)} %lineup.6.both_ref.refs_3_), channel_id=1, source_target_pairs={{0,4},{1,3},{2,6},{3,1},{4,0},{5,7},{6,2},{7,5},{8,12},{9,11},{10,... | collective-permute-start | bytes 786440 | tf_op jit(solution)/shard_map/ppermute | solution.py:55
  4.6 2.6 %collective-permute-start = (bf16[128,512]{1,0:T(8,128)(2,1)S(1)}, bf16[128,512]{1,0:T(8,128)(2,1)S(1)}, u32[]{:S(2)}, u32[]{:S(2)}) collective-permute-start(bf16[128,512]{1,0:T(8,128)(2,1)S(1)} %copy-done.9), channel_id=1, source_target_pairs={{0,16},{4,20},{8,24},{12,28},{16,0},{20,4},{24,8},{28,12},{1,17},{... | collective-permute-start | bytes 393224 | tf_op jit(solution)/shard_map/ppermute | solution.py:35
  7.2 1.6 %collective-permute-start.5 = (bf16[128,512]{1,0:T(8,128)(2,1)S(1)}, bf16[128,512]{1,0:T(8,128)(2,1)S(1)}, u32[]{:S(2)}, u32[]{:S(2)}) collective-permute-start(bf16[128,512]{1,0:T(8,128)(2,1)S(1)} %copy-done.9), channel_id=1, source_target_pairs={{0,8},{4,12},{8,0},{12,4},{16,24},{20,28},{24,16},{28,20},{1,9},{5... | collective-permute-start | bytes 393224 | tf_op jit(solution)/shard_map/ppermute | solution.py:35
  8.8 0.2 collective-permute-done.2.side_ref.refs_0_.refs_4_
  9.0 0.0 copy-start.11
  9.0 0.0 copy-start.12
  9.0 2.1 %collective-permute-start.8 = (bf16[128,512]{1,0:T(8,128)(2,1)S(1)}, bf16[128,512]{1,0:T(8,128)(2,1)S(1)}, u32[]{:S(2)}, u32[]{:S(2)}) collective-permute-start(bf16[128,512]{1,0:T(8,128)(2,1)S(1)} %lineup.8), channel_id=1, source_target_pairs={{0,2},{1,5},{2,0},{3,7},{4,6},{5,1},{6,4},{7,3},{8,10},{9,13},{10,... | collective-permute-start | bytes 393224 | tf_op jit(solution)/shard_map/ppermute | solution.py:55
  11.1 0.0 copy-start.2
  11.1 1.0 %copy-done.2 = bf16[512,512]{1,0:T(8,128)(2,1)S(1)} copy-done((bf16[512,512]{1,0:T(8,128)(2,1)S(1)}, bf16[512,512]{1,0:T(8,128)(2,1)}, u32[]{:S(2)}) %copy-start.2) | copy-done | bytes 524312
  12.1 1.1 %early.1 = (bf16[256,512]{1,0:T(8,128)(2,1)S(1)}, f32[1,512]{1,0:T(1,128)S(1)}, bf16[384,512]{1,0:T(8,128)(2,1)S(1)}, bf16[384,512]{1,0:T(8,128)(2,1)S(1)}, s32[1,12]{1,0:T(1,128)S(1)}) custom-call(f32[8]{0:T(128)S(1)} %copy-done.11, s32[1,12]{1,0:T(1,128)S(1)} %bitcast.3, bf16[256,512]{1,0:T(8,128)(2,1)S(1)} %lineup.6.both_ref.refs_3_, ...), custom_call_target="tpu_custom_call" | custom-call | flops 33554432 | bytes 262144 | tf_op jit(solution)/shard_map/early/pallas_call | solution.py:179
  13.3 0.4 %collective-permute-done.refs_0_ = bf16[128,512]{1,0:T(8,128)(2,1)S(1)} collective-permute-done((bf16[128,512]{1,0:T(8,128)(2,1)S(1)}, bf16[128,512]{1,0:T(8,128)(2,1)S(1)}, u32[]{:S(2)}, u32[]{:S(2)}) %collective-permute-start) | collective-permute-done | bytes 131104 | tf_op jit(solution)/shard_map/ppermute | solution.py:35
  13.7 1.1 %collective-permute-start.9 = (bf16[128,512]{1,0:T(8,128)(2,1)S(1)}, bf16[128,512]{1,0:T(8,128)(2,1)S(1)}, u32[]{:S(2)}, u32[]{:S(2)}) collective-permute-start(bf16[128,512]{1,0:T(8,128)(2,1)S(1)} %lineup.7.refs_1_), channel_id=1, source_target_pairs={{0,4},{4,0},{8,12},{12,8},{16,20},{20,16},{24,28},{28,24},{1,5},{5... | collective-permute-start | bytes 393224 | tf_op jit(solution)/shard_map/ppermute | solution.py:35
  14.8 1.2 %collective-permute-start.3 = (bf16[128,512]{1,0:T(8,128)(2,1)S(1)}, bf16[128,512]{1,0:T(8,128)(2,1)S(1)}, u32[]{:S(2)}, u32[]{:S(2)}) collective-permute-start(bf16[128,512]{1,0:T(8,128)(2,1)S(1)} %lineup.7.refs_1_), channel_id=1, source_target_pairs={{0,2},{1,3},{2,0},{3,1},{4,6},{5,7},{6,4},{7,5},{8,10},{9,11},{10,... | collective-permute-start | bytes 393224 | tf_op jit(solution)/shard_map/ppermute | solution.py:35
  16.1 1.2 %collective-permute-start.4 = (bf16[128,512]{1,0:T(8,128)(2,1)S(1)}, bf16[128,512]{1,0:T(8,128)(2,1)S(1)}, u32[]{:S(2)}, u32[]{:S(2)}) collective-permute-start(bf16[128,512]{1,0:T(8,128)(2,1)S(1)} %lineup.7.refs_1_), channel_id=1, source_target_pairs={{0,6},{1,7},{2,4},{3,5},{4,2},{5,3},{6,0},{7,1},{8,14},{9,15},{10,... | collective-permute-start | bytes 393224 | tf_op jit(solution)/shard_map/ppermute | solution.py:45
  17.3 0.0 collective-permute-done.5.block_ref.other_ref
  17.3 0.0 copy-start.3
  17.3 0.1 collective-permute-start.6
  17.4 0.5 %collective-permute-start.7 = (bf16[64,512]{1,0:T(8,128)(2,1)S(1)}, bf16[64,512]{1,0:T(8,128)(2,1)S(1)}, u32[]{:S(2)}, u32[]{:S(2)}) collective-permute-start(bf16[64,512]{1,0:T(8,128)(2,1)S(1)} %rows.3), channel_id=1, source_target_pairs={{0,1},{1,0},{2,3},{3,2},{4,5},{5,4},{6,7},{7,6},{8,9},{9,8},{10,11... | collective-permute-start | bytes 196616 | tf_op jit(solution)/shard_map/ppermute | solution.py:35
  18.0 0.6 %collective-permute-done.6.first_ref = bf16[64,512]{1,0:T(8,128)(2,1)S(1)} collective-permute-done((bf16[64,512]{1,0:T(8,128)(2,1)S(1)}, bf16[64,512]{1,0:T(8,128)(2,1)S(1)}, u32[]{:S(2)}, u32[]{:S(2)}) %collective-permute-start.6) | collective-permute-done | bytes 65568 | tf_op jit(solution)/shard_map/ppermute | solution.py:35
  18.6 1.2 %collective-permute-start.14 = (bf16[384,512]{1,0:T(8,128)(2,1)S(1)}, bf16[384,512]{1,0:T(8,128)(2,1)S(1)}, u32[]{:S(2)}, u32[]{:S(2)}) collective-permute-start(bf16[384,512]{1,0:T(8,128)(2,1)S(1)} %lineup.9), channel_id=1, source_target_pairs={{0,8},{8,16},{16,24},{24,28},{12,4},{20,12},{28,20},{4,0},{1,9},{9... | collective-permute-start | bytes 1179656 | tf_op jit(solution)/shard_map/ppermute | solution.py:619
  19.8 0.0 collective-permute-done.7.second_ref
  19.8 0.0 collective-permute-done.9.refs_2_
  19.8 2.9 %near.1 = (bf16[256,512]{1,0:T(8,128)(2,1)S(1)}, bf16[768,512]{1,0:T(8,128)(2,1)S(1)}, bf16[768,512]{1,0:T(8,128)(2,1)S(1)}, f32[256,512]{1,0:T(8,128)S(1)}, f32[256,512]{1,0:T(8,128)S(1)}) custom-call(f32[1,512]{1,0:T(1,128)S(1)} %get-tuple-element.30.scale_ref, bf16[384,512]{1,0:T(8,128)(2,1)S(1)} %get-tuple-element.31.held_keys, ...), custom_call_target="tpu_custom_call" | custom-call | flops 37748736 | bytes 262144 | tf_op jit(solution)/shard_map/near/pallas_call | solution.py:210
  22.7 0.2 collective-permute-done.3.refs_0_
  22.8 0.0 collective-permute-done.4.refs_1_
  22.8 1.3 %far.1 = (bf16[256,512]{1,0:T(8,128)(2,1)S(1)}, bf16[256,512]{1,0:T(8,128)(2,1)S(1)}, bf16[256,640]{1,0:T(8,128)(2,1)S(1)}, f32[128,512]{1,0:T(8,128)S(1)}, f32[128,512]{1,0:T(8,128)S(1)}) custom-call(bf16[128,512]{1,0:T(8,128)(2,1)S(1)} %collective-permute-done.3.refs_0_, bf16[128,512]{1,0:T(8,128)(2,1)S(1)} %collective-permute-done.4.refs_1_, ...), custom_call_target="tpu_custom_call" | custom-call | flops 12582912 | bytes 262144 | tf_op jit(solution)/shard_map/far/pallas_call | solution.py:272
  24.1 0.1 collective-permute-start.10
  24.2 1.4 %own_first.1 = (f32[256,512]{1,0:T(8,128)S(1)}, f32[256,512]{1,0:T(8,128)S(1)}) custom-call(bf16[256,512]{1,0:T(8,128)(2,1)S(1)} %get-tuple-element.29.refs_1_.queries_ref.refs_2_, bf16[768,512]{1,0:T(8,128)(2,1)S(1)} %get-tuple-element.38.keys_ref.refs_3_, bf16[768,512]{1,0:T(8,128)(2,1)S(1)} %get-tuple-element.39.values_ref.refs_4_, ...), custom_call_target="tpu_custom_call" | custom-call | flops 16777216 | bytes 131072 | tf_op jit(solution)/shard_map/own_first/pallas_call | solution.py:345
  25.6 0.2 collective-permute-done.10.packed_ref
  25.8 0.2 combine.1.refs_7_
  26.1 1.5 %collective-permute-start.12 = (bf16[128,640]{1,0:T(8,128)(2,1)S(1)}, bf16[128,640]{1,0:T(8,128)(2,1)S(1)}, u32[]{:S(2)}, u32[]{:S(2)}) collective-permute-start(bf16[128,640]{1,0:T(8,128)(2,1)S(1)} %combine.1.refs_7_), channel_id=1, source_target_pairs={{0,8},{4,12},{8,0},{12,4},{16,24},{20,28},{24,16},{28,20},{1,9},{5... | collective-permute-start | bytes 491528 | tf_op jit(solution)/shard_map/ppermute | solution.py:35
  27.6 1.6 %own.1 = (bf16[144,512]{1,0:T(8,128)(2,1)S(1)}, f32[128,512]{1,0:T(8,128)S(1)}, f32[128,512]{1,0:T(8,128)S(1)}) custom-call(bf16[256,512]{1,0:T(8,128)(2,1)S(1)} %get-tuple-element.36.refs_0_, bf16[256,512]{1,0:T(8,128)(2,1)S(1)} %get-tuple-element.37.refs_1_, bf16[256,512]{1,0:T(8,128)(2,1)S(1)} %get-tuple-element.29.refs_1_.queries_ref.refs_2_, ...), custom_call_target="tpu_custom_call" | custom-call | flops 16777216 | bytes 262144 | tf_op jit(solution)/shard_map/own/pallas_call | solution.py:272
  29.2 0.0 collective-permute-start.11
  29.2 0.5 %collective-permute-start.13 = (s32[1,12]{1,0:T(1,128)S(1)}, s32[1,12]{1,0:T(1,128)S(1)}, u32[]{:S(2)}, u32[]{:S(2)}) collective-permute-start(s32[1,12]{1,0:T(1,128)S(1)} %bitcast.4), channel_id=1, source_target_pairs={{0,1},{1,0},{2,3},{3,2},{4,5},{5,4},{6,7},{7,6},{8,9},{9,8},{10,11... | collective-permute-start | bytes 152 | tf_op jit(solution)/shard_map/ppermute | solution.py:35
  29.7 0.9 %collective-permute-done.13.refs_1_ = s32[1,12]{1,0:T(1,128)S(1)} collective-permute-done((s32[1,12]{1,0:T(1,128)S(1)}, s32[1,12]{1,0:T(1,128)S(1)}, u32[]{:S(2)}, u32[]{:S(2)}) %collective-permute-start.13) | collective-permute-done | bytes 80 | tf_op jit(solution)/shard_map/ppermute | solution.py:35
  30.6 0.0 copy-start.5
  30.6 0.0 copy-start.6
  30.6 1.0 %around.1 = (f32[128,512]{1,0:T(8,128)S(1)}, bf16[128,512]{1,0:T(8,128)(2,1)S(1)}) custom-call(s32[1,12]{1,0:T(1,128)S(1)} %get-tuple-element.48.refs_0_, s32[1,12]{1,0:T(1,128)S(1)} %collective-permute-done.13.refs_1_, bf16[16,128,128]{2,1,0:T(8,128)(2,1)S(1)} %copy-done.7, bf16[256,512]{1,0:T(8,128)(2,1)S(1)} %lineup.6.both_ref.refs_3_, ...), custom_call_target="tpu_custom_call" | custom-call | flops 14680064 | bytes 65536 | tf_op jit(solution)/shard_map/around/pallas_call | solution.py:465
  31.6 0.0 copy-start.10
  31.6 0.3 collective-permute-start.15
  31.9 1.1 %collective-permute-done.15.got_ref = bf16[128,512]{1,0:T(8,128)(2,1)S(1)} collective-permute-done((bf16[128,512]{1,0:T(8,128)(2,1)S(1)}, bf16[128,512]{1,0:T(8,128)(2,1)S(1)}, u32[]{:S(2)}, u32[]{:S(2)}) %collective-permute-start.15) | collective-permute-done | bytes 131104 | tf_op jit(solution)/shard_map/ppermute | solution.py:35
  33.0 0.6 %message.1 = (f32[128,512]{1,0:T(8,128)S(1)}, f32[1,512]{1,0:T(1,128)S(1)}) custom-call(f32[128,512]{1,0:T(8,128)S(1)} %get-tuple-element.49.mine_ref, bf16[128,512]{1,0:T(8,128)(2,1)S(1)} %collective-permute-done.15.got_ref, bf16[512,1024]{1,0:T(8,128)(2,1)S(1)} %copy-done.5, bf16[1024,512]{1,0:T(8,128)(2,1)S(1)} %copy-done.6, f32[1,512]{1,0:T(1,128)S(1)} %bitcast.2), custom_call_target="tpu_custom_call" | custom-call | flops 16777216 | bytes 262144 | tf_op jit(solution)/shard_map/message/pallas_call | solution.py:493
  33.6 0.0 collective-permute-done.11.crossed_ref
  33.6 1.2 %finish.1 = bf16[128,512]{1,0:T(8,128)(2,1)} custom-call(f32[128,512]{1,0:T(8,128)S(1)} %get-tuple-element.45.refs_8_.numer_ref, f32[128,512]{1,0:T(8,128)S(1)} %get-tuple-element.46.denom_ref, bf16[144,512]{1,0:T(8,128)(2,1)S(1)} %collective-permute-done.11.crossed_ref, bf16[128,640]{1,0:T(8,128)(2,1)S(1)} %collective-permute-done.12.packed_ref, ...), custom_call_target="tpu_custom_call" | custom-call | flops 4194304 | bytes 131072 | tf_op jit(solution)/shard_map/finish/pallas_call | solution.py:536
  (26 shorter events, 0.1 us)
Async XLA Ops:
  0.0 1.6 %collective-permute-start.1 = (bf16[128,512]{1,0:T(8,128)(2,1)}, bf16[128,512]{1,0:T(8,128)(2,1)S(1)}, u32[]{:S(2)}, u32[]{:S(2)}) collective-permute-start(bf16[128,512]{1,0:T(8,128)(2,1)} %refs_0_.1), channel_id=1, source_target_pairs={{0,1},{1,0},{2,3},{3,2},{4,5},{5,4},{6,7},{7,6},{8,9},{9,8},{10,11... | collective-permute-start | bytes 393224 | tf_op jit(solution)/shard_map/ppermute | solution.py:35
  0.5 0.9 %copy-start.8 = (bf16[128,512]{1,0:T(8,128)(2,1)S(1)}, bf16[128,512]{1,0:T(8,128)(2,1)}, u32[]{:S(2)}) copy-start(bf16[128,512]{1,0:T(8,128)(2,1)} %refs_0_.1) | copy-start | bytes 393220
  1.4 3.2 %copy-start.9 = (bf16[128,512]{1,0:T(8,128)(2,1)S(1)}, bf16[128,512]{1,0:T(8,128)(2,1)}, u32[]{:S(2)}) copy-start(bf16[128,512]{1,0:T(8,128)(2,1)} %refs_0_.1) | copy-start | bytes 393220
  1.4 9.7 %copy-start.1 = (bf16[512,512]{1,0:T(8,128)(2,1)S(1)}, bf16[512,512]{1,0:T(8,128)(2,1)}, u32[]{:S(2)}) copy-start(bf16[512,512]{1,0:T(8,128)(2,1)} %refs_3_.3) | copy-start | bytes 1572868
  1.4 9.7 %copy-start = (bf16[512,512]{1,0:T(8,128)(2,1)S(1)}, bf16[512,512]{1,0:T(8,128)(2,1)}, u32[]{:S(2)}) copy-start(bf16[512,512]{1,0:T(8,128)(2,1)} %refs_2_.2) | copy-start | bytes 1572868
  1.7 7.3 %collective-permute-start.2 = (bf16[256,512]{1,0:T(8,128)(2,1)S(1)}, bf16[256,512]{1,0:T(8,128)(2,1)S(1)}, u32[]{:S(2)}, u32[]{:S(2)}) collective-permute-start(bf16[256,512]{1,0:T(8,128)(2,1)S(1)} %lineup.6.both_ref.refs_3_), channel_id=1, source_target_pairs={{0,4},{1,3},{2,6},{3,1},{4,0},{5,7},{6,2},{7,5},{8,12},{9,11},{10,... | collective-permute-start | bytes 786440 | tf_op jit(solution)/shard_map/ppermute | solution.py:55
  4.6 9.1 %collective-permute-start = (bf16[128,512]{1,0:T(8,128)(2,1)S(1)}, bf16[128,512]{1,0:T(8,128)(2,1)S(1)}, u32[]{:S(2)}, u32[]{:S(2)}) collective-permute-start(bf16[128,512]{1,0:T(8,128)(2,1)S(1)} %copy-done.9), channel_id=1, source_target_pairs={{0,16},{4,20},{8,24},{12,28},{16,0},{20,4},{24,8},{28,12},{1,17},{... | collective-permute-start | bytes 393224 | tf_op jit(solution)/shard_map/ppermute | solution.py:35
  7.2 10.1 %collective-permute-start.5 = (bf16[128,512]{1,0:T(8,128)(2,1)S(1)}, bf16[128,512]{1,0:T(8,128)(2,1)S(1)}, u32[]{:S(2)}, u32[]{:S(2)}) collective-permute-start(bf16[128,512]{1,0:T(8,128)(2,1)S(1)} %copy-done.9), channel_id=1, source_target_pairs={{0,8},{4,12},{8,0},{12,4},{16,24},{20,28},{24,16},{28,20},{1,9},{5... | collective-permute-start | bytes 393224 | tf_op jit(solution)/shard_map/ppermute | solution.py:35
  9.0 2.1 %copy-start.11 = (f32[8]{0:T(128)S(1)}, f32[8]{0:T(128)}, u32[]{:S(2)}) copy-start(f32[8]{0:T(128)} %softness_ref.1) | copy-start | bytes 100
  9.0 2.1 %copy-start.12 = (s32[1,1,12]{2,1,0:T(1,128)S(1)}, s32[1,1,12]{2,1,0:T(1,128)}, u32[]{:S(2)}) copy-start(s32[1,1,12]{2,1,0:T(1,128)} %param.12) | copy-start | bytes 148
  9.0 8.4 %collective-permute-start.8 = (bf16[128,512]{1,0:T(8,128)(2,1)S(1)}, bf16[128,512]{1,0:T(8,128)(2,1)S(1)}, u32[]{:S(2)}, u32[]{:S(2)}) collective-permute-start(bf16[128,512]{1,0:T(8,128)(2,1)S(1)} %lineup.8), channel_id=1, source_target_pairs={{0,2},{1,5},{2,0},{3,7},{4,6},{5,1},{6,4},{7,3},{8,10},{9,13},{10,... | collective-permute-start | bytes 393224 | tf_op jit(solution)/shard_map/ppermute | solution.py:55
  11.1 1.0 %copy-start.2 = (bf16[512,512]{1,0:T(8,128)(2,1)S(1)}, bf16[512,512]{1,0:T(8,128)(2,1)}, u32[]{:S(2)}) copy-start(bf16[512,512]{1,0:T(8,128)(2,1)} %refs_3_.2) | copy-start | bytes 1572868
  13.7 6.1 %collective-permute-start.9 = (bf16[128,512]{1,0:T(8,128)(2,1)S(1)}, bf16[128,512]{1,0:T(8,128)(2,1)S(1)}, u32[]{:S(2)}, u32[]{:S(2)}) collective-permute-start(bf16[128,512]{1,0:T(8,128)(2,1)S(1)} %lineup.7.refs_1_), channel_id=1, source_target_pairs={{0,4},{4,0},{8,12},{12,8},{16,20},{20,16},{24,28},{28,24},{1,5},{5... | collective-permute-start | bytes 393224 | tf_op jit(solution)/shard_map/ppermute | solution.py:35
  14.8 8.0 %collective-permute-start.3 = (bf16[128,512]{1,0:T(8,128)(2,1)S(1)}, bf16[128,512]{1,0:T(8,128)(2,1)S(1)}, u32[]{:S(2)}, u32[]{:S(2)}) collective-permute-start(bf16[128,512]{1,0:T(8,128)(2,1)S(1)} %lineup.7.refs_1_), channel_id=1, source_target_pairs={{0,2},{1,3},{2,0},{3,1},{4,6},{5,7},{6,4},{7,5},{8,10},{9,11},{10,... | collective-permute-start | bytes 393224 | tf_op jit(solution)/shard_map/ppermute | solution.py:35
  16.1 6.8 %collective-permute-start.4 = (bf16[128,512]{1,0:T(8,128)(2,1)S(1)}, bf16[128,512]{1,0:T(8,128)(2,1)S(1)}, u32[]{:S(2)}, u32[]{:S(2)}) collective-permute-start(bf16[128,512]{1,0:T(8,128)(2,1)S(1)} %lineup.7.refs_1_), channel_id=1, source_target_pairs={{0,6},{1,7},{2,4},{3,5},{4,2},{5,3},{6,0},{7,1},{8,14},{9,15},{10,... | collective-permute-start | bytes 393224 | tf_op jit(solution)/shard_map/ppermute | solution.py:45
  17.3 2.5 %copy-start.3 = (bf16[512,512]{1,0:T(8,128)(2,1)S(1)}, bf16[512,512]{1,0:T(8,128)(2,1)}, u32[]{:S(2)}) copy-start(bf16[512,512]{1,0:T(8,128)(2,1)} %refs_3_.2) | copy-start | bytes 1572868
  17.3 1.3 %collective-permute-start.6 = (bf16[64,512]{1,0:T(8,128)(2,1)S(1)}, bf16[64,512]{1,0:T(8,128)(2,1)S(1)}, u32[]{:S(2)}, u32[]{:S(2)}) collective-permute-start(bf16[64,512]{1,0:T(8,128)(2,1)S(1)} %rows.2), channel_id=1, source_target_pairs={{0,1},{1,0},{2,3},{3,2},{4,5},{5,4},{6,7},{7,6},{8,9},{9,8},{10,11... | collective-permute-start | bytes 196616 | tf_op jit(solution)/shard_map/ppermute | solution.py:35
  17.4 2.4 %collective-permute-start.7 = (bf16[64,512]{1,0:T(8,128)(2,1)S(1)}, bf16[64,512]{1,0:T(8,128)(2,1)S(1)}, u32[]{:S(2)}, u32[]{:S(2)}) collective-permute-start(bf16[64,512]{1,0:T(8,128)(2,1)S(1)} %rows.3), channel_id=1, source_target_pairs={{0,1},{1,0},{2,3},{3,2},{4,5},{5,4},{6,7},{7,6},{8,9},{9,8},{10,11... | collective-permute-start | bytes 196616 | tf_op jit(solution)/shard_map/ppermute | solution.py:35
  18.6 11.9 %collective-permute-start.14 = (bf16[384,512]{1,0:T(8,128)(2,1)S(1)}, bf16[384,512]{1,0:T(8,128)(2,1)S(1)}, u32[]{:S(2)}, u32[]{:S(2)}) collective-permute-start(bf16[384,512]{1,0:T(8,128)(2,1)S(1)} %lineup.9), channel_id=1, source_target_pairs={{0,8},{8,16},{16,24},{24,28},{12,4},{20,12},{28,20},{4,0},{1,9},{9... | collective-permute-start | bytes 1179656 | tf_op jit(solution)/shard_map/ppermute | solution.py:619
  24.1 1.7 %collective-permute-start.10 = (bf16[256,640]{1,0:T(8,128)(2,1)S(1)}, bf16[256,640]{1,0:T(8,128)(2,1)S(1)}, u32[]{:S(2)}, u32[]{:S(2)}) collective-permute-start(bf16[256,640]{1,0:T(8,128)(2,1)S(1)} %get-tuple-element.40.refs_0_), channel_id=1, source_target_pairs={{0,1},{1,0},{2,3},{3,2},{4,5},{5,4},{6,7},{7,6},{8,9},{9,8},{10,11... | collective-permute-start | bytes 983048 | tf_op jit(solution)/shard_map/ppermute | solution.py:35
  26.1 7.5 %collective-permute-start.12 = (bf16[128,640]{1,0:T(8,128)(2,1)S(1)}, bf16[128,640]{1,0:T(8,128)(2,1)S(1)}, u32[]{:S(2)}, u32[]{:S(2)}) collective-permute-start(bf16[128,640]{1,0:T(8,128)(2,1)S(1)} %combine.1.refs_7_), channel_id=1, source_target_pairs={{0,8},{4,12},{8,0},{12,4},{16,24},{20,28},{24,16},{28,20},{1,9},{5... | collective-permute-start | bytes 491528 | tf_op jit(solution)/shard_map/ppermute | solution.py:35
  27.6 3.0 %copy-start.4 = (bf16[512,512]{1,0:T(8,128)(2,1)S(1)}, bf16[512,512]{1,0:T(8,128)(2,1)}, u32[]{:S(2)}) copy-start(bf16[512,512]{1,0:T(8,128)(2,1)} %final_ref.1) | copy-start | bytes 1572868
  27.6 3.0 %copy-start.7 = (bf16[16,128,128]{2,1,0:T(8,128)(2,1)S(1)}, bf16[16,128,128]{2,1,0:T(8,128)(2,1)}, u32[]{:S(2)}) copy-start(bf16[16,128,128]{2,1,0:T(8,128)(2,1)} %refs_2_.3) | copy-start | bytes 1572868
  29.2 4.5 %collective-permute-start.11 = (bf16[144,512]{1,0:T(8,128)(2,1)S(1)}, bf16[144,512]{1,0:T(8,128)(2,1)S(1)}, u32[]{:S(2)}, u32[]{:S(2)}) collective-permute-start(bf16[144,512]{1,0:T(8,128)(2,1)S(1)} %get-tuple-element.47), channel_id=1, source_target_pairs={{0,1},{1,0},{2,3},{3,2},{4,5},{5,4},{6,7},{7,6},{8,9},{9,8},{10,11... | collective-permute-start | bytes 442376 | tf_op jit(solution)/shard_map/ppermute | solution.py:35
  29.2 1.4 %collective-permute-start.13 = (s32[1,12]{1,0:T(1,128)S(1)}, s32[1,12]{1,0:T(1,128)S(1)}, u32[]{:S(2)}, u32[]{:S(2)}) collective-permute-start(s32[1,12]{1,0:T(1,128)S(1)} %bitcast.4), channel_id=1, source_target_pairs={{0,1},{1,0},{2,3},{3,2},{4,5},{5,4},{6,7},{7,6},{8,9},{9,8},{10,11... | collective-permute-start | bytes 152 | tf_op jit(solution)/shard_map/ppermute | solution.py:35
  30.6 2.5 %copy-start.5 = (bf16[512,1024]{1,0:T(8,128)(2,1)S(1)}, bf16[512,1024]{1,0:T(8,128)(2,1)}, u32[]{:S(2)}) copy-start(bf16[512,1024]{1,0:T(8,128)(2,1)} %inner_ref.1) | copy-start | bytes 3145732
  30.6 2.5 %copy-start.6 = (bf16[1024,512]{1,0:T(8,128)(2,1)S(1)}, bf16[1024,512]{1,0:T(8,128)(2,1)}, u32[]{:S(2)}) copy-start(bf16[1024,512]{1,0:T(8,128)(2,1)} %outer_ref.1) | copy-start | bytes 3145732
  31.6 1.4 %copy-start.10 = (f32[512]{0:T(512)S(1)}, f32[512]{0:T(512)}, u32[]{:S(2)}) copy-start(f32[512]{0:T(512)} %param.21) | copy-start | bytes 6148
  31.6 1.4 %collective-permute-start.15 = (bf16[128,512]{1,0:T(8,128)(2,1)S(1)}, bf16[128,512]{1,0:T(8,128)(2,1)S(1)}, u32[]{:S(2)}, u32[]{:S(2)}) collective-permute-start(bf16[128,512]{1,0:T(8,128)(2,1)S(1)} %get-tuple-element.50), channel_id=1, source_target_pairs={{0,1},{1,0},{2,3},{3,2},{4,5},{5,4},{6,7},{7,6},{8,9},{9,8},{10,11... | collective-permute-start | bytes 393224 | tf_op jit(solution)/shard_map/ppermute | solution.py:35
